TPU v7x, 512 devices: a whole 4x8x8 slice. The times are simulated.
512 devices in a mesh: row: 16 (over x_hi, y), col: 32 (over x_lo, z, core).
Axes of the slice: x: 4 (x_hi: 2, x_lo: 2; x = x_hi * 2 + x_lo), y: 8, z: 8, core: 2. Of those that a mesh axis runs over, the one named last changes fastest.
Arguments:
- orbitals: bfloat16 [64, 96, 64, 128], P('col', None, 'row'), may hold values from -6 to 6
- potential: float32 [96, 64, 128], P('row'), may hold values from -1 to 1
- proj_points: int32 [128, 128], P('row'), may hold values from 0 to 49151
- projector: float32 [128, 128], P('row'), may hold values from -4 to 4
- strength: float32 [128], P('row'), may hold values from 0.5 to 2
- ritz_panel: bfloat16 [64, 64], P('row', 'col'), may hold values from -0.75 to 0.75
- panel_rows: int32 [64], replicated, may hold values from 0 to 63, each once
Outputs:
- rotated: float32 [64, 96, 64, 128], P('col', 'row')
Inputs may be any that keep to these rules, and one draw needn't show every extreme that they name: `proj_points`: flat indices into the 6 x 64 x 128 cells of the slab of that atom, first dimension slowest. `panel_rows`: each state appears once.
All inputs are finite; a program needn't handle non-finite values.
Results may differ from a plain program's by a relative error of at most 0.0029.
Values may be sent and summed in bfloat16 or wider, within the bound.
No kernel may reach another device: no remote copies, remote signals or barrier semaphores. Data moves between devices by JAX's collectives and lax.ppermute only.
A program may use at most 128 MiB of HBM per device.

v0:
```python
import jax
import jax.numpy as jnp
from jax import lax
from jax.sharding import PartitionSpec as P

DEG = 3


STENCIL = (
    -5369.0 / 1800.0,
    12.0 / 7.0,
    -15.0 / 56.0,
    10.0 / 189.0,
    -1.0 / 112.0,
    2.0 / 1925.0,
    -1.0 / 16632.0,
)
CENTER = 7.0
HALF_WIDTH = 5.0


def extended(cells, sides, width):
    for axis, dim in sides:
        count = lax.axis_size(axis)
        head = lax.slice_in_dim(cells, 0, width, axis=dim)
        tail = lax.slice_in_dim(cells, cells.shape[dim] - width, cells.shape[dim], axis=dim)
        cells = jnp.concatenate(
            [
                lax.ppermute(tail, axis, [(i, (i + 1) % count) for i in range(count)]),
                cells,
                lax.ppermute(head, axis, [((i + 1) % count, i) for i in range(count)]),
            ],
            axis=dim,
        )
    return cells


def laplace(states, across):
    summed = 3.0 * STENCIL[0] * states
    for offset in range(1, 7):
        forward, backward = across(offset)
        summed = summed + STENCIL[offset] * (forward + backward)
    for offset in range(1, 7):
        summed = summed + STENCIL[offset] * (
            jnp.roll(states, -offset, axis=2) + jnp.roll(states, offset, axis=2)
        )
    for offset in range(1, 7):
        summed = summed + STENCIL[offset] * (
            jnp.roll(states, -offset, axis=3) + jnp.roll(states, offset, axis=3)
        )
    return summed


def nonlocal_term(states, points, projector, strength):
    state_count = states.shape[0]
    flattened = states.reshape(state_count, -1)
    sampled = flattened[:, points]
    weights = jnp.sum(sampled * projector, axis=2) * strength
    spread = weights[:, :, None] * projector
    placed = (
        jnp.zeros_like(flattened).at[:, points.reshape(-1)].add(spread.reshape(state_count, -1))
    )
    return placed.reshape(states.shape)


def chebyshev(states, make_across, potential, points, projector, strength):

    def apply_ham(states_now):
        return (
            -0.5 * laplace(states_now, make_across(states_now))
            + potential * states_now
            + nonlocal_term(states_now, points, projector, strength)
        )

    previous = states
    current = (apply_ham(states) - CENTER * states) / HALF_WIDTH
    for degree_step in range(DEG - 1):
        following = 2.0 * (apply_ham(current) - CENTER * current) / HALF_WIDTH - previous
        previous, current = (current, following)
    return current


def bordered(states_now):
    padded = extended(states_now, (("row", 1),), 6)
    thickness = states_now.shape[1]
    return lambda offset: (
        padded[:, 6 + offset : 6 + offset + thickness],
        padded[:, 6 - offset : 6 - offset + thickness],
    )


def rotate(coeffs, columns):
    return jnp.einsum("ij,irk->jrk", coeffs, columns, preferred_element_type=jnp.float32)


def per_device(orbitals, potential, proj_points, projector, strength, ritz_panel, panel_rows):
    regrouped = lax.all_to_all(orbitals, "row", split_axis=1, concat_axis=2, tiled=True)
    slabs = chebyshev(
        regrouped.astype(jnp.float32), bordered, potential, proj_points, projector, strength
    ).astype(jnp.bfloat16)
    stored = lax.all_gather(ritz_panel, "row", axis=0, tiled=True)
    everything = lax.all_gather(stored, "col", axis=1, tiled=True)
    total_states = everything.shape[0]
    selector = (jnp.arange(total_states, dtype=jnp.int32)[:, None] == panel_rows[None, :]).astype(
        jnp.bfloat16
    )
    coeffs = jnp.dot(selector, everything, preferred_element_type=jnp.float32).astype(jnp.bfloat16)
    layered = slabs.reshape(slabs.shape[0], slabs.shape[1] * slabs.shape[2], slabs.shape[3])
    columns = lax.all_to_all(layered, "col", split_axis=1, concat_axis=0, tiled=True)
    turned = rotate(coeffs, columns)
    result = lax.all_to_all(turned, "col", split_axis=0, concat_axis=1, tiled=True)
    return result.reshape(slabs.shape)


def solution(mesh):
    placed = (
        P("col", None, "row", None),
        P("row", None, None),
        P("row", None),
        P("row", None),
        P("row"),
        P("row", "col"),
        P(),
    )
    return jax.shard_map(
        per_device,
        mesh=mesh,
        in_specs=placed,
        out_specs=P("col", "row", None, None),
        check_vma=False,
    )
```

profile of v0, /device:TPU:1, one launch (start us, length us, event | category | flops | bytes accessed | tf_op | source)
XLA Modules:
  0.0 413.1 jit_solution(11960352908996134665)
XLA Ops:
  0.0 1.7 copy.18
  1.7 10.2 %all-to-all-start = ((bf16[2,96,4,128]{3,2,0,1:T(4,128)(2,1)}), bf16[2,96,4,128]{3,2,0,1:T(4,128)(2,1)S(1)}, u32[]{:S(2)}, u32[]{:S(2)}) async-start(bf16[2,96,4,128]{3,2,0,1:T(4,128)(2,1)} %copy.18), calls=%async_computation | async-start | bytes 393216 | tf_op jit(solution)/shard_map/all_to_all | solution.py:97
  13.3 1.6 broadcast_multiply_fusion.1
  14.9 6.0 %all-to-all-done = bf16[2,96,4,128]{3,2,0,1:T(4,128)(2,1)S(1)} async-done(((bf16[2,96,4,128]{3,2,0,1:T(4,128)(2,1)}), bf16[2,96,4,128]{3,2,0,1:T(4,128)(2,1)S(1)}, u32[]{:S(2)}, u32[]{:S(2)}) %all-to-all-start) | async-done | bytes 196640 | tf_op jit(solution)/shard_map/all_to_all | solution.py:97
  20.9 11.4 %copy.19 = f32[2,16,6,4,128]{0,4,3,1,2:T(8,128)} copy(bf16[2,16,6,4,128]{4,3,0,2,1:T(4,128)(2,1)S(1)} %bitcast.105) | data formatting | bytes 589824 | tf_op jit(solution)/shard_map/convert_element_type | solution.py:99
  32.3 14.7 %copy.20 = f32[2,6,16,4,128]{4,3,2,1,0:T(4,128)S(1)} copy(f32[2,6,16,4,128]{0,4,3,2,1:T(8,128)} %bitcast.95) | data formatting | bytes 786432 | tf_op jit(solution)/shard_map/convert_element_type | solution.py:99
  47.5 1.0 fusion.227
  51.5 1.0 fusion.223
  52.5 1.0 fusion.224
  53.5 1.0 fusion.221
  54.5 1.0 fusion.222
  55.5 1.0 fusion.219
  64.2 3.9 collective-permute-start
  68.1 1.9 collective-permute-start.1
  70.0 11.0 %gather_fusion = f32[1024,2]{1,0:T(8,128)S(1)} fusion(f32[2,49152]{0,1:T(8,128)} %bitcast.96, s32[1024]{0:T(1024)S(1)} %fusion.158), kind=kCustom, calls=%fused_computation | custom fusion | bytes 20480 | tf_op jit(solution)/shard_map/gather | solution.py:57
  81.5 16.0 %scatter_custom_fusion = f32[2,49152]{0,1:T(8,128)} fusion(s32[1024]{0:T(1024)S(1)} %bitcast.113, f32[]{:T(128)} %constant.14.clone.1, f32[2,1024]{0,1:T(8,128)S(1)} %bitcast_multiply_fusion.2), kind=kCustom, calls=%fused_computation.10 | custom fusion | flops 2048 | bytes 917508 | tf_op jit(solution)/shard_map/scatter-add | solution.py:61
  97.5 15.4 %copy.21 = f32[2,6,64,128]{3,2,1,0:T(8,128)} copy(f32[2,6,64,128]{0,3,2,1:T(8,128)} %bitcast.98) | data formatting | bytes 786432 | tf_op jit(solution)/shard_map/reshape | solution.py:63
  113.8 7.7 %broadcast_multiply_fusion = (f32[2,6,64,128]{3,2,1,0:T(8,128)S(1)}, f32[2,6,64,128]{3,2,1,0:T(8,128)S(1)}) fusion(f32[2,6,64,128]{3,2,1,0:T(8,128)S(1)} %bitcast.93, f32[2,6,64,128]{3,2,1,0:T(8,128)} %copy.21, f32[6,64,128]{2,1,0:T(8,128)S(1)} %copy-done, f32[2,6,64,122]{3,2,1,0:T(8,128)S(1)} %get-tuple-element.148, ...), kind=kLoop, calls=%fused_computation.261 | loop fusion | flops 9437184 | bytes 11993088 | tf_op jit(solution)/shard_map/div | solution.py:76
  121.4 12.8 %copy.22 = f32[2,6,64,128]{0,3,2,1:T(8,128)} copy(f32[2,6,64,128]{3,2,1,0:T(8,128)S(1)} %get-tuple-element.5) | data formatting | bytes 786432 | tf_op jit(solution)/shard_map/div | solution.py:76
  135.3 1.0 fusion.203
  139.3 1.0 fusion.199
  140.3 1.0 fusion.200
  141.4 1.0 fusion.197
  142.4 1.0 fusion.198
  143.4 1.0 fusion.195
  153.3 7.0 %collective-permute-start.2 = (f32[2,6,64,128]{3,2,1,0:T(8,128)S(1)}, f32[2,6,64,128]{3,2,1,0:T(8,128)S(1)}, u32[]{:S(2)}, u32[]{:S(2)}) collective-permute-start(f32[2,6,64,128]{3,2,1,0:T(8,128)S(1)} %get-tuple-element.5), channel_id=1, source_target_pairs={{32,0},{64,32},{96,64},{128,96},{160,128},{192,160},{224,192},{256... | collective-permute-start | bytes 1179656 | tf_op jit(solution)/shard_map/ppermute | solution.py:31
  160.3 1.9 collective-permute-start.3
  162.2 11.0 %gather_fusion.1 = f32[1024,2]{1,0:T(8,128)S(1)} fusion(f32[2,49152]{0,1:T(8,128)} %bitcast.101, s32[1024]{0:T(1024)S(1)} %fusion.158), kind=kCustom, calls=%fused_computation.1 | custom fusion | bytes 20480 | tf_op jit(solution)/shard_map/gather | solution.py:57
  174.3 16.1 %scatter_custom_fusion.1 = f32[2,49152]{0,1:T(8,128)} fusion(s32[1024]{0:T(1024)} %bitcast.114, f32[]{:T(128)} %constant.14.clone.1, f32[2,1024]{0,1:T(8,128)S(1)} %bitcast_multiply_fusion.1), kind=kCustom, calls=%fused_computation.8 | custom fusion | flops 2048 | bytes 401920 | tf_op jit(solution)/shard_map/scatter-add | solution.py:61
  190.4 15.4 %copy.23 = f32[2,6,64,128]{3,2,1,0:T(8,128)} copy(f32[2,6,64,128]{0,3,2,1:T(8,128)} %bitcast.99) | data formatting | bytes 786432 | tf_op jit(solution)/shard_map/reshape | solution.py:63
  206.7 7.8 %multiply_subtract_fusion = f32[2,6,64,128]{3,2,1,0:T(8,128)S(1)} fusion(f32[2,6,64,128]{3,2,1,0:T(8,128)S(1)} %bitcast.94, f32[2,6,64,128]{3,2,1,0:T(8,128)S(1)} %get-tuple-element.6, f32[2,6,64,128]{3,2,1,0:T(8,128)} %copy.23, f32[2,6,64,122]{3,2,1,0:T(8,128)S(1)} %get-tuple-element.100, f32[2,6,64,6]{3,2,1,0:T(8,128)S(1)} %copy-done.1, ...), kind=kLoop, calls=%fused_computation.259 | loop fusion | flops 9535488 | bytes 12386304 | tf_op jit(solution)/shard_map/sub | solution.py:78
  214.5 12.8 %copy.24 = f32[2,6,64,128]{0,3,2,1:T(8,128)} copy(f32[2,6,64,128]{3,2,1,0:T(8,128)S(1)} %multiply_subtract_fusion) | data formatting | bytes 786432 | tf_op jit(solution)/shard_map/sub | solution.py:78
  227.6 1.0 fusion.179
  231.7 1.0 fusion.175
  232.7 1.0 fusion.176
  233.7 1.0 fusion.173
  234.7 1.0 fusion.174
  235.7 1.0 fusion.171
  244.4 1.9 collective-permute-start.5
  246.3 7.0 %collective-permute-start.4 = (f32[2,6,64,128]{3,2,1,0:T(8,128)S(1)}, f32[2,6,64,128]{3,2,1,0:T(8,128)}, u32[]{:S(2)}, u32[]{:S(2)}) collective-permute-start(f32[2,6,64,128]{3,2,1,0:T(8,128)S(1)} %multiply_subtract_fusion), channel_id=1, source_target_pairs={{32,0},{64,32},{96,64},{128,96},{160,128},{192,160},{224,192},{256... | collective-permute-start | bytes 1179656 | tf_op jit(solution)/shard_map/ppermute | solution.py:31
  253.3 11.0 %gather_fusion.2 = f32[1024,2]{1,0:T(8,128)S(1)} fusion(f32[2,49152]{0,1:T(8,128)} %bitcast.100, s32[1024]{0:T(1024)S(1)} %fusion.158), kind=kCustom, calls=%fused_computation.2 | custom fusion | bytes 20480 | tf_op jit(solution)/shard_map/gather | solution.py:57
  264.8 16.1 %scatter_custom_fusion.2 = f32[2,49152]{0,1:T(8,128)} fusion(s32[1024]{0:T(1024)} %bitcast.115, f32[]{:T(128)} %constant.14.clone.1, f32[2,1024]{0,1:T(8,128)S(1)} %bitcast_multiply_fusion), kind=kCustom, calls=%fused_computation.6 | custom fusion | flops 2048 | bytes 401920 | tf_op jit(solution)/shard_map/scatter-add | solution.py:61
  280.9 15.5 %copy.25 = f32[2,6,64,128]{3,2,1,0:T(8,128)} copy(f32[2,6,64,128]{0,3,2,1:T(8,128)} %bitcast.97) | data formatting | bytes 786432 | tf_op jit(solution)/shard_map/reshape | solution.py:63
  296.5 7.9 %subtract_convert_fusion = bf16[2,6,64,128]{3,2,1,0:T(8,128)(2,1)S(1)} fusion(f32[2,6,64,128]{3,2,1,0:T(8,128)S(1)} %multiply_subtract_fusion, f32[2,6,64,128]{3,2,1,0:T(8,128)} %copy.25, f32[2,6,64,122]{3,2,1,0:T(8,128)S(1)} %get-tuple-element.52, f32[2,6,64,6]{3,2,1,0:T(8,128)S(1)} %get-tuple-element.54, f32[2,6,64,6]{3,2,1,0:T(8,128)S(1)} %get-tuple-element.53, ...), kind=kLoop, calls=%fused_computation.258 | loop fusion | flops 9732096 | bytes 11796480 | tf_op jit(solution)/shard_map/convert_element_type | solution.py:100
  305.3 14.8 %all-to-all-start.1 = ((bf16[2,384,128]{2,0,1:T(2,128)(2,1)}), bf16[2,384,128]{2,0,1:T(2,128)(2,1)S(1)}, u32[]{:S(2)}, u32[]{:S(2)}) async-start(bf16[2,384,128]{2,0,1:T(2,128)(2,1)} %copy.26), calls=%async_computation.1 | async-start | bytes 393216 | tf_op jit(solution)/shard_map/all_to_all | solution.py:109
  320.1 31.0 %all-gather = bf16[16,4,2]{1,2,0:T(2,128)(2,1)S(1)} all-gather(bf16[1,4,2]{1,2,0:T(2,128)(2,1)S(1)} %bitcast.117), channel_id=1, replica_groups=mesh['row'=16,'col'=32] {'row'}, dimensions={0}, use_global_device_ids=true | all-gather | bytes 272 | tf_op jit(solution)/shard_map/all_gather | solution.py:101
  351.2 40.5 %all-gather.1 = bf16[32,2,64]{2,1,0:T(2,128)(2,1)S(1)} all-gather(bf16[1,2,64]{2,1,0:T(2,128)(2,1)S(1)} %bitcast.116), channel_id=1, replica_groups=mesh['row'=16,'col'=32] {'col'}, dimensions={0}, use_global_device_ids=true | all-gather | bytes 8448 | tf_op jit(solution)/shard_map/all_gather | solution.py:102
  392.5 19.6 %all_to_all.42 = f32[64,12,128]{2,1,0:T(8,128)S(1)} all-to-all(f32[64,12,128]{2,1,0:T(8,128)S(1)} %copy.29), channel_id=1, replica_groups=mesh['row'=16,'col'=32] {'col'}, dimensions={0} | all-to-all | bytes 786432 | tf_op jit(solution)/shard_map/all_to_all | solution.py:111
  (112 shorter events, 42.9 us)
Async XLA Ops:
  1.7 19.3 %all-to-all-start = ((bf16[2,96,4,128]{3,2,0,1:T(4,128)(2,1)}), bf16[2,96,4,128]{3,2,0,1:T(4,128)(2,1)S(1)}, u32[]{:S(2)}, u32[]{:S(2)}) async-start(bf16[2,96,4,128]{3,2,0,1:T(4,128)(2,1)} %copy.18), calls=%async_computation | async-start | bytes 393216 | tf_op jit(solution)/shard_map/all_to_all | solution.py:97
  13.3 68.2 %copy-start.13 = (s32[1024,1]{0,1:T(1,128)}, s32[1024,1]{0,1:T(1,128)S(1)}, u32[]{:S(2)}) copy-start(s32[1024,1]{0,1:T(1,128)S(1)} %compare_select_fusion) | copy-start | bytes 12292
  32.3 48.7 %copy-start.9 = (f32[8,128]{1,0:T(8,128)S(1)}, f32[8,128]{1,0:T(8,128)}, u32[]{:S(2)}) copy-start(f32[8,128]{1,0:T(8,128)} %param.10) | copy-start | bytes 12292
  32.3 48.9 %copy-start.11 = (f32[8]{0:T(128)S(1)}, f32[8]{0:T(128)}, u32[]{:S(2)}) copy-start(f32[8]{0:T(128)} %param.11) | copy-start | bytes 100
  64.2 48.8 %collective-permute-start = (f32[2,6,64,128]{3,2,1,0:T(8,128)S(1)}, f32[2,6,64,128]{3,2,1,0:T(8,128)S(1)}, u32[]{:S(2)}, u32[]{:S(2)}) collective-permute-start(f32[2,6,64,128]{3,2,1,0:T(8,128)S(1)} %bitcast.89), channel_id=1, source_target_pairs={{32,0},{64,32},{96,64},{128,96},{160,128},{192,160},{224,192},{256... | collective-permute-start | bytes 1179656 | tf_op jit(solution)/shard_map/ppermute | solution.py:31
  68.1 44.9 %collective-permute-start.1 = (f32[2,6,64,128]{3,2,1,0:T(8,128)S(1)}, f32[2,6,64,128]{3,2,1,0:T(8,128)}, u32[]{:S(2)}, u32[]{:S(2)}) collective-permute-start(f32[2,6,64,128]{3,2,1,0:T(8,128)S(1)} %bitcast.90), channel_id=1, source_target_pairs={{0,32},{32,64},{64,96},{96,128},{128,160},{160,192},{192,224},{224... | collective-permute-start | bytes 1179656 | tf_op jit(solution)/shard_map/ppermute | solution.py:29
  81.5 32.3 %copy-start = (f32[6,64,128]{2,1,0:T(8,128)S(1)}, f32[6,64,128]{2,1,0:T(8,128)}, u32[]{:S(2)}) copy-start(f32[6,64,128]{2,1,0:T(8,128)} %param.8) | copy-start | bytes 589828
  97.5 16.3 %copy-start.4 = (f32[2,6,64,123]{3,2,1,0:T(8,128)S(1)}, f32[2,6,64,123]{3,2,1,0:T(8,128)}, u32[]{:S(2)}) copy-start(f32[2,6,64,123]{3,2,1,0:T(8,128)} %get-tuple-element.143) | copy-start | bytes 1133572
  113.0 0.8 copy-start.6
  153.3 52.6 %collective-permute-start.2 = (f32[2,6,64,128]{3,2,1,0:T(8,128)S(1)}, f32[2,6,64,128]{3,2,1,0:T(8,128)S(1)}, u32[]{:S(2)}, u32[]{:S(2)}) collective-permute-start(f32[2,6,64,128]{3,2,1,0:T(8,128)S(1)} %get-tuple-element.5), channel_id=1, source_target_pairs={{32,0},{64,32},{96,64},{128,96},{160,128},{192,160},{224,192},{256... | collective-permute-start | bytes 1179656 | tf_op jit(solution)/shard_map/ppermute | solution.py:31
  160.3 45.7 %collective-permute-start.3 = (f32[2,6,64,128]{3,2,1,0:T(8,128)S(1)}, f32[2,6,64,128]{3,2,1,0:T(8,128)}, u32[]{:S(2)}, u32[]{:S(2)}) collective-permute-start(f32[2,6,64,128]{3,2,1,0:T(8,128)S(1)} %get-tuple-element.5), channel_id=1, source_target_pairs={{0,32},{32,64},{64,96},{96,128},{128,160},{160,192},{192,224},{224... | collective-permute-start | bytes 1179656 | tf_op jit(solution)/shard_map/ppermute | solution.py:29
  190.4 16.3 %copy-start.1 = (f32[2,6,64,6]{3,2,1,0:T(8,128)S(1)}, f32[2,6,64,6]{3,2,1,0:T(8,128)}, u32[]{:S(2)}) copy-start(f32[2,6,64,6]{3,2,1,0:T(8,128)} %get-tuple-element.102) | copy-start | bytes 55300
  190.4 16.3 %copy-start.7 = (f32[2,6,6,128]{3,2,1,0:T(8,128)S(1)}, f32[2,6,6,128]{3,2,1,0:T(8,128)}, u32[]{:S(2)}) copy-start(f32[2,6,6,128]{3,2,1,0:T(8,128)} %get-tuple-element.78) | copy-start | bytes 110596
  190.4 16.3 %copy-start.8 = (f32[2,6,5,128]{3,2,1,0:T(8,128)S(1)}, f32[2,6,5,128]{3,2,1,0:T(8,128)}, u32[]{:S(2)}) copy-start(f32[2,6,5,128]{3,2,1,0:T(8,128)} %get-tuple-element.73) | copy-start | bytes 92164
  190.4 16.3 %copy-start.10 = (f32[2,6,4,128]{3,2,1,0:T(4,128)S(1)}, f32[2,6,4,128]{3,2,1,0:T(4,128)}, u32[]{:S(2)}) copy-start(f32[2,6,4,128]{3,2,1,0:T(4,128)} %get-tuple-element.70) | copy-start | bytes 73732
  206.0 0.8 copy-start.5
  214.5 50.0 %copy-start.12 = (f32[8]{0:T(128)S(1)}, f32[8]{0:T(128)}, u32[]{:S(2)}) copy-start(f32[8]{0:T(128)} %param.11) | copy-start | bytes 100
  244.4 52.0 %collective-permute-start.5 = (f32[2,6,64,128]{3,2,1,0:T(8,128)S(1)}, f32[2,6,64,128]{3,2,1,0:T(8,128)}, u32[]{:S(2)}, u32[]{:S(2)}) collective-permute-start(f32[2,6,64,128]{3,2,1,0:T(8,128)S(1)} %multiply_subtract_fusion), channel_id=1, source_target_pairs={{0,32},{32,64},{64,96},{96,128},{128,160},{160,192},{192,224},{224... | collective-permute-start | bytes 1179656 | tf_op jit(solution)/shard_map/ppermute | solution.py:29
  246.3 50.1 %collective-permute-start.4 = (f32[2,6,64,128]{3,2,1,0:T(8,128)S(1)}, f32[2,6,64,128]{3,2,1,0:T(8,128)}, u32[]{:S(2)}, u32[]{:S(2)}) collective-permute-start(f32[2,6,64,128]{3,2,1,0:T(8,128)S(1)} %multiply_subtract_fusion), channel_id=1, source_target_pairs={{32,0},{64,32},{96,64},{128,96},{160,128},{192,160},{224,192},{256... | collective-permute-start | bytes 1179656 | tf_op jit(solution)/shard_map/ppermute | solution.py:31
  280.9 15.6 %copy-start.2 = (f32[2,6,64,123]{3,2,1,0:T(8,128)S(1)}, f32[2,6,64,123]{3,2,1,0:T(8,128)}, u32[]{:S(2)}) copy-start(f32[2,6,64,123]{3,2,1,0:T(8,128)} %get-tuple-element.47) | copy-start | bytes 1133572
  280.9 15.6 %copy-start.3 = (f32[2,6,64,123]{3,2,1,0:T(8,128)S(1)}, f32[2,6,64,123]{3,2,1,0:T(8,128)}, u32[]{:S(2)}) copy-start(f32[2,6,64,123]{3,2,1,0:T(8,128)} %get-tuple-element.48) | copy-start | bytes 1133572
  280.9 39.2 %copy-start.14 = (bf16[4,2]{0,1:T(2,128)(2,1)S(1)}, bf16[4,2]{0,1:T(2,128)(2,1)}, u32[]{:S(2)}) copy-start(bf16[4,2]{0,1:T(2,128)(2,1)} %param.12) | copy-start | bytes 52
  280.9 111.0 %copy-start.15 = (s32[64]{0:T(128)S(1)}, s32[64]{0:T(128)}, u32[]{:S(2)}) copy-start(s32[64]{0:T(128)} %param.13) | copy-start | bytes 772
  305.3 86.5 %all-to-all-start.1 = ((bf16[2,384,128]{2,0,1:T(2,128)(2,1)}), bf16[2,384,128]{2,0,1:T(2,128)(2,1)S(1)}, u32[]{:S(2)}, u32[]{:S(2)}) async-start(bf16[2,384,128]{2,0,1:T(2,128)(2,1)} %copy.26), calls=%async_computation.1 | async-start | bytes 393216 | tf_op jit(solution)/shard_map/all_to_all | solution.py:109
where the time goes:
time: 415 us; the launch traced here: 413 us
  local copies, waits for them, and re-layouts  190 us (46%)
  blocking collectives  91.1 us (22%)
  other arithmetic  76.6 us (18%)
  starting transfers between devices  48.5 us (12%)
  waiting for transfers between devices  6.05 us (1%)
    scatter-add x3, other arithmetic, nonlocal_term(): jnp.zeros_like(flattened).at[:, points.reshape(-1)]  48.1 us
    reshape x3, local copies, waits for them, and re-layouts, nonlocal_term(): return placed.reshape(states.shape)  46.3 us
    all_gather x1, blocking collectives, per_device(): everything = lax.all_gather(stored, 'col', axis=1, tiled=True)  40.5 us
    gather x3, local copies, waits for them, and re-layouts, nonlocal_term(): sampled = flattened[:, points]  32.9 us
    slice x36, local copies, waits for them, and re-layouts, laplace(): jnp.roll(states, -offset, axis=3) + jnp.roll(states, offset, axis=3)  32.2 us
    all_gather x1, blocking collectives, per_device(): stored = lax.all_gather(ritz_panel, 'row', axis=0, tiled=True)  31 us
    convert_element_type x2, local copies, waits for them, and re-layouts, per_device(): regrouped.astype(jnp.float32)  26.1 us
    slice x36, local copies, waits for them, and re-layouts, laplace(): jnp.roll(states, -offset, axis=2) + jnp.roll(states, offset, axis=2)  21.4 us
  transfers between devices with their start and end apart: 8, of which 1 were waited for; matrix products, arithmetic and copies ran while one was open for 32% of the time, Pallas kernels for 0%

commit v1 on v0

v1 whole, which is shorter than its diff:
```python
import functools

import jax
import jax.numpy as jnp
import numpy as np
from jax import lax
from jax.experimental import pallas as pl
from jax.experimental.pallas import tpu as pltpu
from jax.sharding import PartitionSpec as P

F32 = jnp.float32
BF16 = jnp.bfloat16

STENCIL = (
    -5369.0 / 1800.0,
    12.0 / 7.0,
    -15.0 / 56.0,
    10.0 / 189.0,
    -1.0 / 112.0,
    2.0 / 1925.0,
    -1.0 / 16632.0,
)
CENTER = 7.0
HALF_WIDTH = 5.0

ROWS, COLS = 16, 32
SLAB, GY, GZ = 6, 64, 128
GX = ROWS * SLAB
YPART = GY // ROWS
WIDE = 3 * SLAB
ATOM_DEV = 8
SLAB_ROWS = SLAB * GY
SENT = 2 * WIDE + 1

SIDE = tuple(-0.5 * c for c in STENCIL)
DIAGONAL = -0.5 * 3.0 * STENCIL[0] - CENTER

VMEM = pl.BlockSpec(memory_space=pltpu.VMEM)
PARAMS = pltpu.CompilerParams(vmem_limit_bytes=40 * 1024 * 1024)


def circulant(size):
    whole = np.zeros((size, size), np.float32)
    for offset in range(1, 7):
        for i in range(size):
            whole[i, (i + offset) % size] += SIDE[offset]
            whole[i, (i - offset) % size] += SIDE[offset]
    high = whole.astype(jnp.bfloat16)
    low = (whole - high.astype(np.float32)).astype(jnp.bfloat16)
    return high, low


def stencil_matrices():
    high, low = circulant(GZ)
    along_z = np.block([[high, low], [high, low]])
    high, low = circulant(GY)
    along_y = np.block([[high, high], [low, low]])
    return jnp.asarray(along_z), jnp.asarray(along_y)


def call(kernel, outs, scratch=(), flops=0, bytes_accessed=0, specs=None):
    return pl.pallas_call(
        kernel,
        out_shape=outs,
        in_specs=specs,
        out_specs=jax.tree.map(lambda _: VMEM, outs),
        scratch_shapes=list(scratch),
        compiler_params=PARAMS,
        cost_estimate=pl.CostEstimate(
            flops=flops, bytes_accessed=bytes_accessed, transcendentals=0
        ),
    )


def pack_kernel(orbitals, panel, out):
    row = lax.axis_index("row")
    place = lax.broadcasted_iota(jnp.int32, (YPART, GZ), 1)
    stored = lax.broadcasted_iota(jnp.int32, (YPART, GZ), 0)
    here = jnp.where(place == stored + YPART * row, 1.0, 0.0)
    values = panel[...].astype(F32)
    first = jnp.sum(here * values[:, 0:1], axis=0, keepdims=True)
    second = jnp.sum(here * values[:, 1:2], axis=0, keepdims=True)
    line = lax.broadcasted_iota(jnp.int32, (YPART, GZ), 0)
    tile = jnp.where(line == 0, first, jnp.where(line == 1, second, 0.0)).astype(BF16)
    for target in range(ROWS):
        begin = (SLAB * target - SLAB) % GX
        for state in range(2):
            base = state * WIDE
            head = min(WIDE, GX - begin)
            out[target, base : base + head] = orbitals[state, begin : begin + head]
            if head < WIDE:
                out[target, base + head : base + WIDE] = orbitals[state, : WIDE - head]
        out[target, 2 * WIDE] = tile


def project_kernel(points, projector, strength, dense, gains):
    for atom in range(ATOM_DEV):
        at = points[atom : atom + 1, :]
        value = projector[atom : atom + 1, :]
        grid_row = lax.shift_right_logical(at, 7)
        lane = at & (GZ - 1)
        rows = jnp.where(
            lax.broadcasted_iota(jnp.int32, (SLAB_ROWS, GZ), 0) == grid_row, 1.0, 0.0
        ).astype(BF16)
        at_lane = lax.broadcasted_iota(jnp.int32, (GZ, GZ), 0) == lane
        high = value.astype(BF16).astype(F32)
        rest = value - high
        middle = rest.astype(BF16).astype(F32)
        low = rest - middle
        lanes = [jnp.where(at_lane, part, 0.0).astype(BF16) for part in (high, middle, low)]
        dense[atom] = lax.dot_general(
            jnp.concatenate([rows] * 3, axis=1),
            jnp.concatenate(lanes, axis=1),
            (((1,), (1,)), ((), ())),
            preferred_element_type=F32,
        )
        gains[atom : atom + 1, :] = jnp.full((1, GZ), strength[atom], F32)


def inside(planes, scale, potential, dense, gains, along_z, along_y, wide_z, summed_z, emit):
    partial = [[None] * ATOM_DEV for _ in range(2)]
    for p in range(SLAB):
        for state in range(2):
            value = planes(state, p)
            high = value.astype(BF16)
            low = (value - high.astype(F32)).astype(BF16)
            start = (state * SLAB + p) * GY
            wide_z[start : start + GY, 0:GZ] = high
            wide_z[start : start + GY, GZ : 2 * GZ] = low
        own = [planes(state, p) for state in range(2)]
        for atom in range(ATOM_DEV):
            weight = dense[atom, p * GY : (p + 1) * GY, :]
            for state in range(2):
                term = jnp.sum((weight * own[state]).reshape(GY // 8, 8, GZ), axis=0)
                before = partial[state][atom]
                partial[state][atom] = term if before is None else before + term
    summed_z[...] = jnp.dot(wide_z[...], along_z[...], preferred_element_type=F32)
    weights = []
    for state in range(2):
        lines = [jnp.sum(term, axis=0, keepdims=True) for term in partial[state]]
        total = jnp.sum(jnp.concatenate(lines, axis=0), axis=1, keepdims=True)
        weights.append(total * gains[...])
    for p in range(SLAB):
        both = jnp.concatenate(
            [
                jnp.concatenate(
                    [
                        wide_z[start : start + GY, 0:GZ],
                        wide_z[start : start + GY, GZ : 2 * GZ],
                    ],
                    axis=0,
                )
                for start in (p * GY, (SLAB + p) * GY)
            ],
            axis=1,
        )
        turned = jnp.dot(along_y[...], both, preferred_element_type=F32)
        turned = turned[:GY] + turned[GY:]
        level = DIAGONAL + potential[p]
        for state in range(2):
            start = (state * SLAB + p) * GY
            total = level * planes(state, p) + turned[:, state * GZ : (state + 1) * GZ]
            total = total + (
                summed_z[start : start + GY, 0:GZ] + summed_z[start : start + GY, GZ : 2 * GZ]
            )
            for atom in range(ATOM_DEV):
                total = (
                    total
                    + weights[state][atom : atom + 1, :] * dense[atom, p * GY : (p + 1) * GY, :]
                )
            for offset in range(1, 7):
                terms = [planes(state, q) for q in (p - offset, p + offset) if 0 <= q < SLAB]
                if terms:
                    total = total + SIDE[offset] * functools.reduce(jnp.add, terms)
            emit(state, p, scale * total)


def beside(below, above, state, p):
    total = None
    for offset in range(1, 7):
        if p - offset < 0:
            plane = below(state, SLAB + p - offset)
        else:
            plane = None
        if p + offset >= SLAB:
            other = above(state, p + offset - SLAB)
            plane = other if plane is None else plane + other
        if plane is not None:
            total = SIDE[offset] * plane if total is None else total + SIDE[offset] * plane
    return total


def first_kernel(
    received, potential, dense, gains, along_z, along_y,
    start_out, next_out, sent_out, panel_out, slabs, wide_z, summed_z,
):
    panel = jnp.zeros((YPART, GZ), F32)
    for source in range(ROWS):
        for state in range(2):
            slabs[state, :, source * YPART : (source + 1) * YPART, :] = received[
                source, state * WIDE : (state + 1) * WIDE
            ].astype(F32)
        panel = panel + received[source, 2 * WIDE].astype(F32)
    panel_out[0:YPART, :] = panel
    panel_out[YPART:8, :] = jnp.zeros((8 - YPART, GZ), F32)
    for state in range(2):
        start_out[state] = slabs[state, SLAB : 2 * SLAB]
    scale = 1.0 / HALF_WIDTH

    def emit(state, p, value):
        value = value + scale * beside(
            lambda s, q: slabs[s, q], lambda s, q: slabs[s, 2 * SLAB + q], state, p
        )
        next_out[state, p] = value
        sent_out[state, p] = value.astype(BF16)

    inside(
        lambda state, p: slabs[state, SLAB + p],
        scale, potential, dense, gains, along_z, along_y, wide_z, summed_z, emit,
    )


def inside_kernel(
    current, previous, potential, dense, gains, along_z, along_y, out, wide_z, summed_z
):
    def emit(state, p, value):
        out[state, p] = value - previous[state, p]

    inside(
        lambda state, p: current[state, p],
        2.0 / HALF_WIDTH, potential, dense, gains, along_z, along_y, wide_z, summed_z, emit,
    )


def joined(partial, below, above, state, p):
    return partial[state, p] + (2.0 / HALF_WIDTH) * beside(
        lambda s, q: below[s, q].astype(F32), lambda s, q: above[s, q].astype(F32), state, p
    )


def join_kernel(partial, below, above, next_out, sent_out):
    for p in range(SLAB):
        for state in range(2):
            value = joined(partial, below, above, state, p)
            next_out[state, p] = value
            sent_out[state, p] = value.astype(BF16)


def lane_below(half):
    return lax.broadcasted_iota(jnp.int32, (8, GZ), 1) < half


def last_kernel(partial, below, above, panel, out, slab):
    for p in range(SLAB):
        for state in range(2):
            slab[state, p * GY : (p + 1) * GY, :] = joined(partial, below, above, state, p)
    left = lane_below(GZ // 2)
    for target in range(COLS):
        tiles = [slab[state, 8 * target : 8 * target + 8, :] for state in range(2)]
        shared = 8 * (COLS + target // 2)
        first, second = (slab[state, shared : shared + 8, :] for state in range(2))
        if target % 2 == 0:
            tiles.append(jnp.where(left, first, pltpu.roll(second, GZ // 2, 1)))
        else:
            tiles.append(jnp.where(left, pltpu.roll(first, GZ // 2, 1), second))
        tiles.append(panel[...])
        out[target] = jnp.concatenate(tiles, axis=0).astype(BF16)


def rotate_kernel(received, panel_rows, out):
    left = lane_below(GZ // 2)
    columns = [[], []]
    turned = [[], []]
    for source in range(COLS):
        chunk = received[source].astype(F32)
        for state in range(2):
            shared = chunk[16:24]
            if state == 1:
                shared = pltpu.roll(shared, GZ // 2, 1)
            columns[state].append(
                jnp.concatenate([chunk[8 * state : 8 * state + 8], shared], axis=1)
            )
            turned[state].append(
                jnp.broadcast_to(chunk[24 + state : 25 + state, :64], (8, 64))
            )
    states = jnp.concatenate(columns[0] + columns[1], axis=0).astype(BF16)
    wanted = jnp.concatenate(turned[0] + turned[1], axis=0).astype(BF16)
    size = 16 * COLS
    order = lax.broadcasted_iota(jnp.int32, (size, 64), 0)
    half = 8 * COLS
    state_of = jnp.where(order < half, (order >> 3) * 2, ((order - half) >> 3) * 2 + 1)
    stored = jnp.where(panel_rows[...] == state_of, 1.0, 0.0).astype(BF16)
    spread = lax.dot_general(
        wanted, stored, (((1,), (1,)), ((), ())), preferred_element_type=F32
    )
    same = (
        lax.broadcasted_iota(jnp.int32, (size, size), 0) & 7
    ) == (lax.broadcasted_iota(jnp.int32, (size, size), 1) & 7)
    spread = jnp.where(same, spread, 0.0).astype(BF16)
    rotated = jnp.dot(spread, states, preferred_element_type=F32)
    for target in range(COLS):
        pair = [rotated[start : start + 8] for start in (8 * target, half + 8 * target)]
        shared = jnp.where(left, pair[0][:, GZ:], pltpu.roll(pair[1][:, GZ:], GZ // 2, 1))
        out[target] = jnp.concatenate([pair[0][:, :GZ], pair[1][:, :GZ], shared], axis=0).astype(
            BF16
        )


def place_kernel(received, out):
    left = lane_below(GZ // 2)
    for pair in range(COLS // 2):
        chunks = [received[2 * pair + k].astype(F32) for k in range(2)]
        for k in range(2):
            at = 8 * (2 * pair + k)
            for state in range(2):
                out[state, at : at + 8, :] = chunks[k][8 * state : 8 * state + 8]
        even, odd = (chunk[16:24] for chunk in chunks)
        at = 8 * (COLS + pair)
        out[0, at : at + 8, :] = jnp.where(left, even, pltpu.roll(odd, GZ // 2, 1))
        out[1, at : at + 8, :] = jnp.where(left, pltpu.roll(even, GZ // 2, 1), odd)


def per_device(orbitals, potential, proj_points, projector, strength, ritz_panel, panel_rows):
    shape = jax.ShapeDtypeStruct
    slab_f32 = shape((2, SLAB, GY, GZ), F32)
    slab_bf16 = shape((2, SLAB, GY, GZ), BF16)
    along_z, along_y = stencil_matrices()
    work = [
        pltpu.VMEM((2 * SLAB_ROWS, 2 * GZ), BF16),
        pltpu.VMEM((2 * SLAB_ROWS, 2 * GZ), F32),
    ]

    packed = call(pack_kernel, shape((ROWS, SENT, YPART, GZ), BF16), specs=[VMEM] * 2)(
        orbitals, ritz_panel
    )
    regrouped = lax.all_to_all(packed, "row", split_axis=0, concat_axis=0, tiled=True)
    dense, gains = call(
        project_kernel,
        (shape((ATOM_DEV, SLAB_ROWS, GZ), F32), shape((8, GZ), F32)),
        specs=[VMEM, VMEM, pl.BlockSpec(memory_space=pltpu.SMEM)],
        flops=1_000_000_000,
        bytes_accessed=1_600_000,
    )(proj_points, projector, strength)

    fixed = (potential, dense, gains, along_z, along_y)
    start, current, sent, panel = call(
        first_kernel,
        (slab_f32, slab_f32, slab_bf16, shape((8, GZ), F32)),
        scratch=[pltpu.VMEM((2, WIDE, GY, GZ), F32)] + work,
        specs=[VMEM] * 6,
    )(regrouped, *fixed)

    up = [(i, (i + 1) % ROWS) for i in range(ROWS)]
    down = [((i + 1) % ROWS, i) for i in range(ROWS)]
    previous = start
    for step in range(2):
        below = lax.ppermute(sent, "row", up)
        above = lax.ppermute(sent, "row", down)
        partial = call(
            inside_kernel,
            slab_f32,
            scratch=work,
            specs=[VMEM] * 7,
            flops=2_000_000_000,
            bytes_accessed=3_000_000,
        )(current, previous, *fixed)
        if step == 0:
            previous = current
            current, sent = call(join_kernel, (slab_f32, slab_bf16), specs=[VMEM] * 3)(
                partial, below, above
            )
    layered = call(
        last_kernel,
        shape((COLS, 32, GZ), BF16),
        scratch=[pltpu.VMEM((2, SLAB_ROWS, GZ), F32)],
        specs=[VMEM] * 4,
    )(partial, below, above, panel)
    columns = lax.all_to_all(layered, "col", split_axis=0, concat_axis=0, tiled=True)
    turned = call(rotate_kernel, shape((COLS, 24, GZ), BF16), specs=[VMEM] * 2)(
        columns, panel_rows.reshape(1, -1)
    )
    result = lax.all_to_all(turned, "col", split_axis=0, concat_axis=0, tiled=True)
    whole = call(place_kernel, shape((2, SLAB_ROWS, GZ), F32), specs=[VMEM])(result)
    return whole.reshape(2, SLAB, GY, GZ)


def solution(mesh):
    placed = (
        P("col", None, "row", None),
        P("row", None, None),
        P("row", None),
        P("row", None),
        P("row"),
        P("row", "col"),
        P(),
    )
    return jax.shard_map(
        per_device,
        mesh=mesh,
        in_specs=placed,
        out_specs=P("col", "row", None, None),
        check_vma=False,
    )
```

time: 415 us -> 102 us (0.25)
  local copies, waits for them, and re-layouts: 190 us -> 1.73 us
  other arithmetic: 76.6 us -> 0 us
  blocking collectives: 91.1 us -> 42 us
  starting transfers between devices: 48.5 us -> 21.3 us
  waiting for transfers between devices: 6.05 us -> 29 us
  Pallas kernels: 0 us -> 7.59 us
    all_gather x2 -> x0, blocking collectives: 71.5 us -> none  [the longest x1 40.5 us: per_device(): everything = lax.all_gather(stored, 'col', axis=1, tiled=True)]
    slice x72 -> x0, local copies, waits for them, and re-layouts: 53.5 us -> none  [the longest x36 32.2 us: laplace(): jnp.roll(states, -offset, axis=3) + jnp.roll(states, offset, axis=3)]
    scatter-add x3 -> x0, other arithmetic: 48.1 us -> none  [nonlocal_term(): jnp.zeros_like(flattened).at[:, points.reshape(-1)]]
    reshape x5 -> x0, local copies, waits for them, and re-layouts: 48 us -> none  [the longest x3 46.3 us: nonlocal_term(): return placed.reshape(states.shape)]
    gather x3 -> x0, local copies, waits for them, and re-layouts: 32.9 us -> none  [nonlocal_term(): sampled = flattened[:, points]]
    convert_element_type x2 -> x0, local copies, waits for them, and re-layouts: 26.1 us -> none  [per_device(): regrouped.astype(jnp.float32)]
    all_to_all x1 -> x2, blocking collectives: 19.6 us -> 42 us  [the longest x1 27.6 us: per_device(): lax.all_to_all(layered, 'col', split_axis=0, concat_axis=0, tiled=True)]
    all_to_all x2 -> x1, starting transfers between devices: 25 us -> 10.2 us  [per_device(): lax.all_to_all(packed, 'row', split_axis=0, concat_axis=0, tiled=True)]
  transfers between devices with their start and end apart: 8 -> 5, of which waited for: 1 -> 4; matrix products, arithmetic and copies ran while one was open for 32% -> 0% of each run, Pallas kernels for 0% -> 3%
where the time goes in v1:
time: 102 us
  blocking collectives  42 us (41%)
  waiting for transfers between devices  29 us (28%)
  starting transfers between devices  21.3 us (21%)
  Pallas kernels  7.59 us (7%)
  local copies, waits for them, and re-layouts  1.73 us (2%)
    all_to_all x1, blocking collectives, per_device(): lax.all_to_all(layered, 'col', split_axis=0, concat_axis=0, tiled=True)  27.6 us
    all_to_all x1, waiting for transfers between devices, per_device(): lax.all_to_all(packed, 'row', split_axis=0, concat_axis=0, tiled=True)  16.2 us
    all_to_all x1, blocking collectives, per_device(): lax.all_to_all(turned, 'col', split_axis=0, concat_axis=0, tiled=True)  14.4 us
    ppermute x2, waiting for transfers between devices, per_device(): below = lax.ppermute(sent, 'row', up)  12.7 us
    all_to_all x1, starting transfers between devices, per_device(): lax.all_to_all(packed, 'row', split_axis=0, concat_axis=0, tiled=True)  10.2 us
    ppermute x2, starting transfers between devices, per_device(): above = lax.ppermute(sent, 'row', down)  5.85 us
    ppermute x2, starting transfers between devices, per_device(): below = lax.ppermute(sent, 'row', up)  5.28 us
  transfers between devices with their start and end apart: 5, of which 4 were waited for; matrix products, arithmetic and copies ran while one was open for 0% of the time, Pallas kernels for 3%

profile of v1, /device:TPU:1, one launch (start us, length us, event | category | flops | bytes accessed | tf_op | source)
XLA Modules:
  0.0 101.8 jit_solution(10748184149888309238)
XLA Ops:
  0.0 0.0 copy-start.7
  0.0 0.8 copy.10.panel
  0.8 0.0 copy-start.1
  0.8 0.9 copy-done.1
  1.7 0.0 copy-start.5
  1.7 0.0 copy-start.6
  1.7 1.0 shard_map.91
  2.7 10.2 %all-to-all-start = ((bf16[16,37,4,128]{3,2,1,0:T(4,128)(2,1)}), bf16[16,37,4,128]{3,2,1,0:T(4,128)(2,1)S(1)}, u32[]{:S(2)}, u32[]{:S(2)}) async-start(bf16[16,37,4,128]{3,2,1,0:T(4,128)(2,1)} %shard_map.91), calls=%async_computation | async-start | bytes 1212416 | tf_op jit(solution)/shard_map/all_to_all | solution.py:336
  12.9 0.0 copy-done.7
  12.9 0.0 copy-done.5
  12.9 0.0 copy-done.6
  12.9 0.0 copy-start
  13.0 0.0 copy-start.2
  13.0 0.0 copy-start.3
  13.0 1.3 %shard_map.92 = (f32[8,384,128]{2,1,0:T(8,128)S(1)}, f32[8,128]{1,0:T(8,128)S(1)}) custom-call(s32[8,128]{1,0:T(8,128)S(1)} %copy-done.5, f32[8,128]{1,0:T(8,128)S(1)} %copy-done.6, f32[8]{0:T(128)S(1)} %copy-done.7), custom_call_target="tpu_custom_call" | custom-call | flops 1000000000 | bytes 1600000 | tf_op jit(solution)/shard_map/pallas_call | solution.py:337
  14.3 16.2 %all-to-all-done.received = bf16[16,37,4,128]{3,2,1,0:T(4,128)(2,1)S(1)} async-done(((bf16[16,37,4,128]{3,2,1,0:T(4,128)(2,1)}), bf16[16,37,4,128]{3,2,1,0:T(4,128)(2,1)S(1)}, u32[]{:S(2)}, u32[]{:S(2)}) %all-to-all-start) | async-done | bytes 606240 | tf_op jit(solution)/shard_map/all_to_all | solution.py:336
  30.5 0.0 copy-done
  30.5 0.0 copy-done.2
  30.5 0.0 copy-done.3
  30.5 1.4 %shard_map.93 = (f32[2,6,64,128]{3,2,1,0:T(8,128)S(1)}, f32[2,6,64,128]{3,2,1,0:T(8,128)S(1)}, bf16[2,6,64,128]{3,2,1,0:T(8,128)(2,1)S(1)}, f32[8,128]{1,0:T(8,128)S(1)}) custom-call(bf16[16,37,4,128]{3,2,1,0:T(4,128)(2,1)S(1)} %all-to-all-done.received, f32[6,64,128]{2,1,0:T(8,128)S(1)} %copy-done, f32[8,384,128]{2,1,0:T(8,128)S(1)} %get-tuple-element.13.dense, ...), custom_call_target="tpu_custom_call" | custom-call | tf_op jit(solution)/shard_map/pallas_call | solution.py:346
  31.9 3.9 %collective-permute-start.1 = (bf16[2,6,64,128]{3,2,1,0:T(8,128)(2,1)S(1)}, bf16[2,6,64,128]{3,2,1,0:T(8,128)(2,1)S(1)}, u32[]{:S(2)}, u32[]{:S(2)}) collective-permute-start(bf16[2,6,64,128]{3,2,1,0:T(8,128)(2,1)S(1)} %get-tuple-element.17), channel_id=1, source_target_pairs={{32,0},{64,32},{96,64},{128,96},{160,128},{192,160},{224,192},{256... | collective-permute-start | bytes 589832 | tf_op jit(solution)/shard_map/ppermute | solution.py:358
  35.8 1.9 %collective-permute-start = (bf16[2,6,64,128]{3,2,1,0:T(8,128)(2,1)S(1)}, bf16[2,6,64,128]{3,2,1,0:T(8,128)(2,1)S(1)}, u32[]{:S(2)}, u32[]{:S(2)}) collective-permute-start(bf16[2,6,64,128]{3,2,1,0:T(8,128)(2,1)S(1)} %get-tuple-element.17), channel_id=1, source_target_pairs={{0,32},{32,64},{64,96},{96,128},{128,160},{160,192},{192,224},{224... | collective-permute-start | bytes 589832 | tf_op jit(solution)/shard_map/ppermute | solution.py:357
  37.7 1.0 shard_map.94.partial
  38.7 0.0 collective-permute-done.1.above
  38.7 7.1 %collective-permute-done.below = bf16[2,6,64,128]{3,2,1,0:T(8,128)(2,1)S(1)} collective-permute-done((bf16[2,6,64,128]{3,2,1,0:T(8,128)(2,1)S(1)}, bf16[2,6,64,128]{3,2,1,0:T(8,128)(2,1)S(1)}, u32[]{:S(2)}, u32[]{:S(2)}) %collective-permute-start) | collective-permute-done | bytes 196640 | tf_op jit(solution)/shard_map/ppermute | solution.py:357
  45.8 0.3 shard_map.95
  46.1 1.9 %collective-permute-start.3 = (bf16[2,6,64,128]{3,2,1,0:T(8,128)(2,1)S(1)}, bf16[2,6,64,128]{3,2,1,0:T(8,128)(2,1)S(1)}, u32[]{:S(2)}, u32[]{:S(2)}) collective-permute-start(bf16[2,6,64,128]{3,2,1,0:T(8,128)(2,1)S(1)} %get-tuple-element.19), channel_id=1, source_target_pairs={{32,0},{64,32},{96,64},{128,96},{160,128},{192,160},{224,192},{256... | collective-permute-start | bytes 589832 | tf_op jit(solution)/shard_map/ppermute | solution.py:358
  48.0 3.4 %collective-permute-start.2 = (bf16[2,6,64,128]{3,2,1,0:T(8,128)(2,1)S(1)}, bf16[2,6,64,128]{3,2,1,0:T(8,128)(2,1)S(1)}, u32[]{:S(2)}, u32[]{:S(2)}) collective-permute-start(bf16[2,6,64,128]{3,2,1,0:T(8,128)(2,1)S(1)} %get-tuple-element.19), channel_id=1, source_target_pairs={{0,32},{32,64},{64,96},{96,128},{128,160},{160,192},{192,224},{224... | collective-permute-start | bytes 589832 | tf_op jit(solution)/shard_map/ppermute | solution.py:357
  51.4 1.0 shard_map.96.partial
  52.4 0.0 copy-start.4
  52.4 0.1 collective-permute-done.3.above
  52.5 5.5 %collective-permute-done.2.below = bf16[2,6,64,128]{3,2,1,0:T(8,128)(2,1)S(1)} collective-permute-done((bf16[2,6,64,128]{3,2,1,0:T(8,128)(2,1)S(1)}, bf16[2,6,64,128]{3,2,1,0:T(8,128)(2,1)S(1)}, u32[]{:S(2)}, u32[]{:S(2)}) %collective-permute-start.2) | collective-permute-done | bytes 196640 | tf_op jit(solution)/shard_map/ppermute | solution.py:357
  58.1 0.3 shard_map.97
  58.4 27.6 %all_to_all.15.received = bf16[32,32,128]{2,1,0:T(8,128)(2,1)S(1)} all-to-all(bf16[32,32,128]{2,1,0:T(8,128)(2,1)S(1)} %shard_map.97), channel_id=1, replica_groups=mesh['row'=16,'col'=32] {'col'}, dimensions={0} | all-to-all | bytes 524288 | tf_op jit(solution)/shard_map/all_to_all | solution.py:378
  85.9 0.0 copy-done.4
  85.9 0.6 shard_map.98
  86.6 14.4 %all_to_all.16.received = bf16[32,24,128]{2,1,0:T(8,128)(2,1)S(1)} all-to-all(bf16[32,24,128]{2,1,0:T(8,128)(2,1)S(1)} %shard_map.98), channel_id=1, replica_groups=mesh['row'=16,'col'=32] {'col'}, dimensions={0} | all-to-all | bytes 393216 | tf_op jit(solution)/shard_map/all_to_all | solution.py:382
  101.0 0.8 shard_map.99
Async XLA Ops:
  0.0 12.9 %copy-start.7 = (f32[8]{0:T(128)S(1)}, f32[8]{0:T(128)}, u32[]{:S(2)}) copy-start(f32[8]{0:T(128)} %strength.1) | copy-start | bytes 100
  0.8 0.9 copy-start.1
  1.7 11.2 %copy-start.5 = (s32[8,128]{1,0:T(8,128)S(1)}, s32[8,128]{1,0:T(8,128)}, u32[]{:S(2)}) copy-start(s32[8,128]{1,0:T(8,128)} %points.1) | copy-start | bytes 12292
  1.7 11.2 %copy-start.6 = (f32[8,128]{1,0:T(8,128)S(1)}, f32[8,128]{1,0:T(8,128)}, u32[]{:S(2)}) copy-start(f32[8,128]{1,0:T(8,128)} %projector.1) | copy-start | bytes 12292
  2.7 27.8 %all-to-all-start = ((bf16[16,37,4,128]{3,2,1,0:T(4,128)(2,1)}), bf16[16,37,4,128]{3,2,1,0:T(4,128)(2,1)S(1)}, u32[]{:S(2)}, u32[]{:S(2)}) async-start(bf16[16,37,4,128]{3,2,1,0:T(4,128)(2,1)} %shard_map.91), calls=%async_computation | async-start | bytes 1212416 | tf_op jit(solution)/shard_map/all_to_all | solution.py:336
  12.9 17.6 %copy-start = (f32[6,64,128]{2,1,0:T(8,128)S(1)}, f32[6,64,128]{2,1,0:T(8,128)}, u32[]{:S(2)}) copy-start(f32[6,64,128]{2,1,0:T(8,128)} %potential.5) | copy-start | bytes 589828
  13.0 17.5 %copy-start.2 = (bf16[256,256]{1,0:T(8,128)(2,1)S(1)}, bf16[256,256]{1,0:T(8,128)(2,1)}, u32[]{:S(2)}) copy-start(bf16[256,256]{1,0:T(8,128)(2,1)} %constant.4.clone.along_z) | copy-start | bytes 393220
  13.0 17.5 %copy-start.3 = (bf16[128,128]{1,0:T(8,128)(2,1)S(1)}, bf16[128,128]{1,0:T(8,128)(2,1)}, u32[]{:S(2)}) copy-start(bf16[128,128]{1,0:T(8,128)(2,1)} %constant.5.clone.along_y) | copy-start | bytes 98308
  31.9 6.8 %collective-permute-start.1 = (bf16[2,6,64,128]{3,2,1,0:T(8,128)(2,1)S(1)}, bf16[2,6,64,128]{3,2,1,0:T(8,128)(2,1)S(1)}, u32[]{:S(2)}, u32[]{:S(2)}) collective-permute-start(bf16[2,6,64,128]{3,2,1,0:T(8,128)(2,1)S(1)} %get-tuple-element.17), channel_id=1, source_target_pairs={{32,0},{64,32},{96,64},{128,96},{160,128},{192,160},{224,192},{256... | collective-permute-start | bytes 589832 | tf_op jit(solution)/shard_map/ppermute | solution.py:358
  35.8 10.0 %collective-permute-start = (bf16[2,6,64,128]{3,2,1,0:T(8,128)(2,1)S(1)}, bf16[2,6,64,128]{3,2,1,0:T(8,128)(2,1)S(1)}, u32[]{:S(2)}, u32[]{:S(2)}) collective-permute-start(bf16[2,6,64,128]{3,2,1,0:T(8,128)(2,1)S(1)} %get-tuple-element.17), channel_id=1, source_target_pairs={{0,32},{32,64},{64,96},{96,128},{128,160},{160,192},{192,224},{224... | collective-permute-start | bytes 589832 | tf_op jit(solution)/shard_map/ppermute | solution.py:357
  46.1 6.4 %collective-permute-start.3 = (bf16[2,6,64,128]{3,2,1,0:T(8,128)(2,1)S(1)}, bf16[2,6,64,128]{3,2,1,0:T(8,128)(2,1)S(1)}, u32[]{:S(2)}, u32[]{:S(2)}) collective-permute-start(bf16[2,6,64,128]{3,2,1,0:T(8,128)(2,1)S(1)} %get-tuple-element.19), channel_id=1, source_target_pairs={{32,0},{64,32},{96,64},{128,96},{160,128},{192,160},{224,192},{256... | collective-permute-start | bytes 589832 | tf_op jit(solution)/shard_map/ppermute | solution.py:358
  48.0 10.0 %collective-permute-start.2 = (bf16[2,6,64,128]{3,2,1,0:T(8,128)(2,1)S(1)}, bf16[2,6,64,128]{3,2,1,0:T(8,128)(2,1)S(1)}, u32[]{:S(2)}, u32[]{:S(2)}) collective-permute-start(bf16[2,6,64,128]{3,2,1,0:T(8,128)(2,1)S(1)} %get-tuple-element.19), channel_id=1, source_target_pairs={{0,32},{32,64},{64,96},{96,128},{128,160},{160,192},{192,224},{224... | collective-permute-start | bytes 589832 | tf_op jit(solution)/shard_map/ppermute | solution.py:357
  52.4 33.6 %copy-start.4 = (s32[64]{0:T(128)S(1)}, s32[64]{0:T(128)}, u32[]{:S(2)}) copy-start(s32[64]{0:T(128)} %param.15) | copy-start | bytes 772

commit v2 on v1

v2 whole, which is shorter than its diff:
```python
import functools

import jax
import jax.numpy as jnp
import numpy as np
from jax import lax
from jax.experimental import pallas as pl
from jax.experimental.pallas import tpu as pltpu
from jax.sharding import PartitionSpec as P

F32 = jnp.float32
BF16 = jnp.bfloat16

STENCIL = (
    -5369.0 / 1800.0,
    12.0 / 7.0,
    -15.0 / 56.0,
    10.0 / 189.0,
    -1.0 / 112.0,
    2.0 / 1925.0,
    -1.0 / 16632.0,
)
CENTER = 7.0
HALF_WIDTH = 5.0

ROWS, COLS = 16, 32
SLAB, GY, GZ = 6, 64, 128
GX = ROWS * SLAB
YPART = GY // ROWS
WIDE = 5 * SLAB
REACH = (WIDE - SLAB) // 2
ATOM_DEV = 8
SLAB_ROWS = SLAB * GY
SENT = 2 * WIDE + 1
NEXT_ROWS = SLAB_ROWS + 6 * ATOM_DEV

SIDE = tuple(-0.5 * c for c in STENCIL)
DIAGONAL = -0.5 * 3.0 * STENCIL[0] - CENTER

VMEM = pl.BlockSpec(memory_space=pltpu.VMEM)
PARAMS = pltpu.CompilerParams(vmem_limit_bytes=40 * 1024 * 1024)


def circulant(size):
    whole = np.zeros((size, size), np.float32)
    for offset in range(1, 7):
        for i in range(size):
            whole[i, (i + offset) % size] += SIDE[offset]
            whole[i, (i - offset) % size] += SIDE[offset]
    high = whole.astype(jnp.bfloat16)
    low = (whole - high.astype(np.float32)).astype(jnp.bfloat16)
    return high, low


def stencil_matrices():
    high, low = circulant(GZ)
    along_z = np.block([[high, low], [high, low]])
    high, low = circulant(GY)
    along_y = np.block([[high, high], [low, low]])
    return jnp.asarray(along_z), jnp.asarray(along_y)


def call(kernel, outs, scratch=(), flops=0, bytes_accessed=0, specs=None):
    return pl.pallas_call(
        kernel,
        out_shape=outs,
        in_specs=specs,
        out_specs=jax.tree.map(lambda _: VMEM, outs),
        scratch_shapes=list(scratch),
        compiler_params=PARAMS,
        cost_estimate=pl.CostEstimate(
            flops=flops, bytes_accessed=bytes_accessed, transcendentals=0
        ),
    )


def pack_pieces():
    pieces = []
    for target in range(ROWS):
        begin = (SLAB * target - REACH) % GX
        head = min(WIDE, GX - begin)
        for state in range(2):
            pieces.append((target, state, begin, state * WIDE, head))
            if head < WIDE:
                pieces.append((target, state, 0, state * WIDE + head, WIDE - head))
    return pieces


def pack_kernel(orbitals, panel, out, sems):
    copies = []
    for i, (target, state, begin, at, count) in enumerate(pack_pieces()):
        copies.append(
            pltpu.make_async_copy(
                orbitals.at[state, pl.ds(begin, count)],
                out.at[target, pl.ds(at, count)],
                sems.at[i],
            )
        )
        copies[-1].start()
    row = lax.axis_index("row")
    place = lax.broadcasted_iota(jnp.int32, (2, GZ), 1)
    values = panel[...].astype(F32)
    tile = jnp.zeros((2, GZ), F32)
    for k in range(YPART):
        tile = jnp.where(place == YPART * row + k, values[:, k : k + 1], tile)
    tile = jnp.concatenate([tile, jnp.zeros((YPART - 2, GZ), F32)], axis=0).astype(BF16)
    for target in range(ROWS):
        out[target, 2 * WIDE] = tile
    for copy in copies:
        copy.wait()


def three_parts(value):
    high = value.astype(BF16).astype(F32)
    rest = value - high
    middle = rest.astype(BF16).astype(F32)
    return high, middle, rest - middle


def next_kernel(potential, points, projector, strength, out):
    for p in range(SLAB):
        out[p * GY : (p + 1) * GY, :] = potential[p].astype(BF16)
    gains = jnp.concatenate(
        [jnp.full((1, GZ), strength[atom], F32) for atom in range(ATOM_DEV)], axis=0
    )
    lane = lax.broadcasted_iota(jnp.int32, (ATOM_DEV, GZ), 1)
    high, middle, low = three_parts(gains)
    gains = jnp.where(lane == 0, high, jnp.where(lane == 1, middle, low))
    at = points[...]
    tail = [
        lax.shift_right_logical(at, 8).astype(F32),
        (at & 255).astype(F32),
        *three_parts(projector[...]),
        gains,
    ]
    out[SLAB_ROWS:NEXT_ROWS, :] = jnp.concatenate(tail, axis=0).astype(BF16)


def densify(grid_row, lane, parts, store):
    for atom in range(ATOM_DEV):
        rows = jnp.where(
            lax.broadcasted_iota(jnp.int32, (SLAB_ROWS, GZ), 0) == grid_row[atom : atom + 1, :],
            1.0,
            0.0,
        ).astype(BF16)
        at_lane = lax.broadcasted_iota(jnp.int32, (GZ, GZ), 0) == lane[atom : atom + 1, :]
        lanes = [
            jnp.where(at_lane, part[atom : atom + 1, :], 0.0).astype(BF16) for part in parts
        ]
        store(
            atom,
            lax.dot_general(
                jnp.concatenate([rows] * 3, axis=1),
                jnp.concatenate(lanes, axis=1),
                (((1,), (1,)), ((), ())),
                preferred_element_type=F32,
            ),
        )


def project_kernel(points, projector, strength, dense, gains):
    at = points[...]

    def store(atom, value):
        dense[atom] = value

    densify(lax.shift_right_logical(at, 7), at & (GZ - 1), three_parts(projector[...]), store)
    for atom in range(ATOM_DEV):
        gains[atom : atom + 1, :] = jnp.full((1, GZ), strength[atom], F32)


def project_next_kernel(below, above, dense, gains):
    for side, received in enumerate((below, above)):
        tail = received[SLAB_ROWS:NEXT_ROWS, :].astype(F32)
        pieces = [tail[ATOM_DEV * i : ATOM_DEV * (i + 1)] for i in range(6)]
        top, bottom = (piece.astype(jnp.int32) for piece in pieces[:2])

        def store(atom, value):
            dense[side, atom] = value

        densify(
            top * 2 + lax.shift_right_logical(bottom, 7), bottom & (GZ - 1), pieces[2:5], store
        )
        gain = pieces[5]
        gain = gain[:, 0:1] + (gain[:, 1:2] + gain[:, 2:3])
        gains[side] = jnp.broadcast_to(gain, (ATOM_DEV, GZ))


def apply(planes, slabs, reach, scale, along_z, along_y, wide_z, summed_z, emit):
    count = SLAB * len(slabs)
    weights = []
    for s, (_, dense, gains) in enumerate(slabs):
        partial = [[None] * ATOM_DEV for _ in range(2)]
        for p in range(SLAB):
            own = [planes(state, SLAB * s + p) for state in range(2)]
            for state in range(2):
                high = own[state].astype(BF16)
                low = (own[state] - high.astype(F32)).astype(BF16)
                start = (state * count + SLAB * s + p) * GY
                wide_z[start : start + GY, 0:GZ] = high
                wide_z[start : start + GY, GZ : 2 * GZ] = low
            for atom in range(ATOM_DEV):
                weight = dense[atom, p * GY : (p + 1) * GY, :]
                for state in range(2):
                    term = jnp.sum((weight * own[state]).reshape(GY // 8, 8, GZ), axis=0)
                    before = partial[state][atom]
                    partial[state][atom] = term if before is None else before + term
        lines = []
        for state in range(2):
            sums = [jnp.sum(term, axis=0, keepdims=True) for term in partial[state]]
            total = jnp.sum(jnp.concatenate(sums, axis=0), axis=1, keepdims=True)
            lines.append(total * gains)
        weights.append(lines)
    height = 2 * count * GY
    summed_z[0:height, :] = jnp.dot(
        wide_z[0:height, :], along_z[...], preferred_element_type=F32
    )
    for s, (potential, dense, _) in enumerate(slabs):
        for q in range(SLAB):
            p = SLAB * s + q
            both = jnp.concatenate(
                [
                    jnp.concatenate(
                        [
                            wide_z[start : start + GY, 0:GZ],
                            wide_z[start : start + GY, GZ : 2 * GZ],
                        ],
                        axis=0,
                    )
                    for start in (p * GY, (count + p) * GY)
                ],
                axis=1,
            )
            turned = jnp.dot(along_y[...], both, preferred_element_type=F32)
            turned = turned[:GY] + turned[GY:]
            level = DIAGONAL + potential(q)
            for state in range(2):
                start = (state * count + p) * GY
                total = level * planes(state, p) + turned[:, state * GZ : (state + 1) * GZ]
                total = total + (
                    summed_z[start : start + GY, 0:GZ]
                    + summed_z[start : start + GY, GZ : 2 * GZ]
                )
                for atom in range(ATOM_DEV):
                    total = (
                        total
                        + weights[s][state][atom : atom + 1, :]
                        * dense[atom, q * GY : (q + 1) * GY, :]
                    )
                for offset in range(1, 7):
                    terms = [
                        planes(state, k)
                        for k in (p - offset, p + offset)
                        if -reach <= k < count + reach
                    ]
                    if terms:
                        total = total + SIDE[offset] * functools.reduce(jnp.add, terms)
                emit(state, p, scale * total)


def beside(below, above, state, p):
    total = None
    for offset in range(1, 7):
        if p - offset < 0:
            plane = below(state, SLAB + p - offset)
        else:
            plane = None
        if p + offset >= SLAB:
            other = above(state, p + offset - SLAB)
            plane = other if plane is None else plane + other
        if plane is not None:
            total = SIDE[offset] * plane if total is None else total + SIDE[offset] * plane
    return total


def first_kernel(
    received, below, above, next_dense, next_gains, potential, dense, gains, along_z, along_y,
    previous_out, current_out, sent_out, panel_out, start, first, wide_z, summed_z,
):
    panel = jnp.zeros((YPART, GZ), F32)
    for source in range(ROWS):
        for state in range(2):
            start[state, :, source * YPART : (source + 1) * YPART, :] = received[
                source, state * WIDE : (state + 1) * WIDE
            ].astype(F32)
        panel = panel + received[source, 2 * WIDE].astype(F32)
    panel_out[0:YPART, :] = panel
    panel_out[YPART:8, :] = jnp.zeros((8 - YPART, GZ), F32)

    own = (lambda q: potential[q], dense, gains[...])
    slabs = [
        (lambda q: below[q * GY : (q + 1) * GY, :].astype(F32), next_dense.at[0], next_gains[0]),
        own,
        (lambda q: above[q * GY : (q + 1) * GY, :].astype(F32), next_dense.at[1], next_gains[1]),
    ]

    def emit_first(state, p, value):
        first[state, p] = value
        if SLAB <= p < 2 * SLAB:
            previous_out[state, p - SLAB] = value

    apply(
        lambda state, p: start[state, SLAB + p],
        slabs, SLAB, 1.0 / HALF_WIDTH, along_z, along_y, wide_z, summed_z, emit_first,
    )

    def emit_second(state, p, value):
        value = value - start[state, REACH + p]
        current_out[state, p] = value
        sent_out[state, p] = value.astype(BF16)

    apply(
        lambda state, p: first[state, SLAB + p],
        [own], SLAB, 2.0 / HALF_WIDTH, along_z, along_y, wide_z, summed_z, emit_second,
    )


def inside_kernel(
    current, previous, potential, dense, gains, along_z, along_y, out, wide_z, summed_z
):
    def emit(state, p, value):
        out[state, p] = value - previous[state, p]

    apply(
        lambda state, p: current[state, p],
        [(lambda q: potential[q], dense, gains[...])],
        0, 2.0 / HALF_WIDTH, along_z, along_y, wide_z, summed_z, emit,
    )


def joined(partial, below, above, state, p):
    return partial[state, p] + (2.0 / HALF_WIDTH) * beside(
        lambda s, q: below[s, q].astype(F32), lambda s, q: above[s, q].astype(F32), state, p
    )


def lane_below(half):
    return lax.broadcasted_iota(jnp.int32, (8, GZ), 1) < half


def last_kernel(partial, below, above, panel, out, slab):
    for p in range(SLAB):
        for state in range(2):
            slab[state, p * GY : (p + 1) * GY, :] = joined(partial, below, above, state, p)
    left = lane_below(GZ // 2)
    for target in range(COLS):
        tiles = [slab[state, 8 * target : 8 * target + 8, :] for state in range(2)]
        shared = 8 * (COLS + target // 2)
        first, second = (slab[state, shared : shared + 8, :] for state in range(2))
        if target % 2 == 0:
            tiles.append(jnp.where(left, first, pltpu.roll(second, GZ // 2, 1)))
        else:
            tiles.append(jnp.where(left, pltpu.roll(first, GZ // 2, 1), second))
        tiles.append(panel[...])
        out[target] = jnp.concatenate(tiles, axis=0).astype(BF16)


def rotate_kernel(received, panel_rows, out):
    left = lane_below(GZ // 2)
    columns = [[], []]
    turned = [[], []]
    for source in range(COLS):
        chunk = received[source].astype(F32)
        for state in range(2):
            shared = chunk[16:24]
            if state == 1:
                shared = pltpu.roll(shared, GZ // 2, 1)
            columns[state].append(
                jnp.concatenate([chunk[8 * state : 8 * state + 8], shared], axis=1)
            )
            turned[state].append(
                jnp.broadcast_to(chunk[24 + state : 25 + state, :64], (8, 64))
            )
    states = jnp.concatenate(columns[0] + columns[1], axis=0).astype(BF16)
    wanted = jnp.concatenate(turned[0] + turned[1], axis=0).astype(BF16)
    size = 16 * COLS
    order = lax.broadcasted_iota(jnp.int32, (size, 64), 0)
    half = 8 * COLS
    state_of = jnp.where(order < half, (order >> 3) * 2, ((order - half) >> 3) * 2 + 1)
    stored = jnp.where(panel_rows[...] == state_of, 1.0, 0.0).astype(BF16)
    spread = lax.dot_general(
        wanted, stored, (((1,), (1,)), ((), ())), preferred_element_type=F32
    )
    same = (
        lax.broadcasted_iota(jnp.int32, (size, size), 0) & 7
    ) == (lax.broadcasted_iota(jnp.int32, (size, size), 1) & 7)
    spread = jnp.where(same, spread, 0.0).astype(BF16)
    rotated = jnp.dot(spread, states, preferred_element_type=F32)
    for target in range(COLS):
        pair = [rotated[start : start + 8] for start in (8 * target, half + 8 * target)]
        shared = jnp.where(left, pair[0][:, GZ:], pltpu.roll(pair[1][:, GZ:], GZ // 2, 1))
        out[target] = jnp.concatenate([pair[0][:, :GZ], pair[1][:, :GZ], shared], axis=0).astype(
            BF16
        )


def place_kernel(received, out):
    left = lane_below(GZ // 2)
    for pair in range(COLS // 2):
        chunks = [received[2 * pair + k].astype(F32) for k in range(2)]
        for k in range(2):
            at = 8 * (2 * pair + k)
            for state in range(2):
                out[state, at : at + 8, :] = chunks[k][8 * state : 8 * state + 8]
        even, odd = (chunk[16:24] for chunk in chunks)
        at = 8 * (COLS + pair)
        out[0, at : at + 8, :] = jnp.where(left, even, pltpu.roll(odd, GZ // 2, 1))
        out[1, at : at + 8, :] = jnp.where(left, pltpu.roll(even, GZ // 2, 1), odd)


def per_device(orbitals, potential, proj_points, projector, strength, ritz_panel, panel_rows):
    shape = jax.ShapeDtypeStruct
    slab_f32 = shape((2, SLAB, GY, GZ), F32)
    slab_bf16 = shape((2, SLAB, GY, GZ), BF16)
    along_z, along_y = stencil_matrices()
    smem = pl.BlockSpec(memory_space=pltpu.SMEM)
    up = [(i, (i + 1) % ROWS) for i in range(ROWS)]
    down = [((i + 1) % ROWS, i) for i in range(ROWS)]

    def work(slabs):
        height = 2 * slabs * SLAB_ROWS
        return [pltpu.VMEM((height, 2 * GZ), BF16), pltpu.VMEM((height, 2 * GZ), F32)]

    def beside_of(array):
        return lax.ppermute(array, "row", up), lax.ppermute(array, "row", down)

    packed = call(
        pack_kernel,
        shape((ROWS, SENT, YPART, GZ), BF16),
        scratch=[pltpu.SemaphoreType.DMA((len(pack_pieces()),))],
        specs=[pl.BlockSpec(memory_space=pl.ANY), VMEM],
    )(orbitals, ritz_panel.T)
    regrouped = lax.all_to_all(packed, "row", split_axis=0, concat_axis=0, tiled=True)
    given = call(
        next_kernel,
        shape((NEXT_ROWS, GZ), BF16),
        specs=[VMEM] * 3 + [smem],
        flops=1_000_000,
        bytes_accessed=300_000,
    )(potential, proj_points, projector, strength)
    next_below, next_above = beside_of(given)
    dense, gains = call(
        project_kernel,
        (shape((ATOM_DEV, SLAB_ROWS, GZ), F32), shape((ATOM_DEV, GZ), F32)),
        specs=[VMEM, VMEM, smem],
        flops=1_000_000_000,
        bytes_accessed=1_600_000,
    )(proj_points, projector, strength)
    next_dense, next_gains = call(
        project_next_kernel,
        (shape((2, ATOM_DEV, SLAB_ROWS, GZ), F32), shape((2, ATOM_DEV, GZ), F32)),
        specs=[VMEM] * 2,
        flops=2_000_000_000,
        bytes_accessed=3_200_000,
    )(next_below, next_above)

    fixed = (potential, dense, gains, along_z, along_y)
    previous, current, sent, panel = call(
        first_kernel,
        (slab_f32, slab_f32, slab_bf16, shape((8, GZ), F32)),
        scratch=[pltpu.VMEM((2, WIDE, GY, GZ), F32), pltpu.VMEM((2, 3 * SLAB, GY, GZ), F32)]
        + work(3),
        specs=[VMEM] * 10,
    )(regrouped, next_below, next_above, next_dense, next_gains, *fixed)
    below, above = beside_of(sent)
    partial = call(
        inside_kernel,
        slab_f32,
        scratch=work(1),
        specs=[VMEM] * 7,
        flops=2_000_000_000,
        bytes_accessed=3_000_000,
    )(current, previous, *fixed)
    layered = call(
        last_kernel,
        shape((COLS, 32, GZ), BF16),
        scratch=[pltpu.VMEM((2, SLAB_ROWS, GZ), F32)],
        specs=[VMEM] * 4,
    )(partial, below, above, panel)
    columns = lax.all_to_all(layered, "col", split_axis=0, concat_axis=0, tiled=True)
    turned = call(rotate_kernel, shape((COLS, 24, GZ), BF16), specs=[VMEM] * 2)(
        columns, panel_rows.reshape(1, -1)
    )
    result = lax.all_to_all(turned, "col", split_axis=0, concat_axis=0, tiled=True)
    whole = call(place_kernel, shape((2, SLAB_ROWS, GZ), F32), specs=[VMEM])(result)
    return whole.reshape(2, SLAB, GY, GZ)


def solution(mesh):
    placed = (
        P("col", None, "row", None),
        P("row", None, None),
        P("row", None),
        P("row", None),
        P("row"),
        P("row", "col"),
        P(),
    )
    return jax.shard_map(
        per_device,
        mesh=mesh,
        in_specs=placed,
        out_specs=P("col", "row", None, None),
        check_vma=False,
    )
```

time: 102 us -> 109 us (1.069)
  Pallas kernels: 7.59 us -> 13.5 us
  waiting for transfers between devices: 29 us -> 25.2 us
  local copies, waits for them, and re-layouts: 1.73 us -> 5.17 us
  starting transfers between devices: 21.3 us -> 24.3 us
  blocking collectives: 42 us -> 39.6 us
    all_to_all x1, waiting for transfers between devices: 16.2 us -> 0.01 us  [per_device(): lax.all_to_all(packed, 'row', split_axis=0, concat_axis=0, tiled=True)]
    ppermute x4, waiting for transfers between devices: 12.8 us -> 25.2 us  [beside_of(): return (lax.ppermute(array, 'row', up), lax.ppermute(array, 'row', down))]
    pallas_call x1, Pallas kernels: 1.36 us -> 4.89 us  [per_device(): call(first_kernel, (slab_f32, slab_f32, slab_bf16, shape((8, GZ), F32)),...]
    unnamed x17 -> x22, local copies, waits for them, and re-layouts: 1.73 us -> 5.17 us
    ppermute x4, starting transfers between devices: 11.1 us -> 14.1 us  [beside_of(): return (lax.ppermute(array, 'row', up), lax.ppermute(array, 'row', down))]
    all_to_all x1, blocking collectives: 27.6 us -> 25.1 us  [per_device(): lax.all_to_all(layered, 'col', split_axis=0, concat_axis=0, tiled=True)]
    pallas_call x5, Pallas kernels: 4.48 us -> 6.91 us  [the longest x1 2.68 us: per_device(): call(pack_kernel, shape((ROWS, SENT, YPART, GZ), BF16), scratch=[pltpu.Se...]
  transfers between devices with their start and end apart: 5 -> 5, of which waited for: 4 -> 4; matrix products, arithmetic and copies ran while one was open for 0% -> 0% of each run, Pallas kernels for 3% -> 4%
where the time goes in v2:
time: 109 us; the launch traced here: 108 us
  blocking collectives  39.6 us (36%)
  waiting for transfers between devices  25.2 us (23%)
  starting transfers between devices  24.3 us (22%)
  Pallas kernels  13.5 us (12%)
  local copies, waits for them, and re-layouts  5.17 us (5%)
    ppermute x4, waiting for transfers between devices, beside_of(): return (lax.ppermute(array, 'row', up), lax.ppermute(array, 'row', down))  25.2 us
    all_to_all x1, blocking collectives, per_device(): lax.all_to_all(layered, 'col', split_axis=0, concat_axis=0, tiled=True)  25.1 us
    all_to_all x1, blocking collectives, per_device(): lax.all_to_all(turned, 'col', split_axis=0, concat_axis=0, tiled=True)  14.4 us
    ppermute x4, starting transfers between devices, beside_of(): return (lax.ppermute(array, 'row', up), lax.ppermute(array, 'row', down))  14.1 us
    all_to_all x1, starting transfers between devices, per_device(): lax.all_to_all(packed, 'row', split_axis=0, concat_axis=0, tiled=True)  10.2 us
    unnamed x22, local copies, waits for them, and re-layouts  5.17 us
    pallas_call x1, Pallas kernels, per_device(): call(first_kernel, (slab_f32, slab_f32, slab_bf16, shape((8, GZ), F32)),...  4.89 us
    pallas_call x1, Pallas kernels, per_device(): call(pack_kernel, shape((ROWS, SENT, YPART, GZ), BF16), scratch=[pltpu.Se...  2.68 us
  transfers between devices with their start and end apart: 5, of which 4 were waited for; matrix products, arithmetic and copies ran while one was open for 0% of the time, Pallas kernels for 4%

profile of v2, /device:TPU:1, one launch (start us, length us, event | category | flops | bytes accessed | tf_op | source)
XLA Modules:
  0.0 108.0 jit_solution(12683177154924045729)
XLA Ops:
  0.0 0.0 copy-start.2
  0.0 0.0 copy-start.3
  0.0 1.0 copy-done.3
  1.0 0.0 copy-start.8
  1.0 0.7 copy-done.8
  1.6 0.0 copy-start.6
  1.6 0.0 copy-start.7
  1.6 0.0 copy-start.9
  1.6 2.7 %shard_map.91 = bf16[16,61,4,128]{3,2,1,0:T(4,128)(2,1)} custom-call(bf16[2,96,4,128]{3,2,1,0:T(4,128)(2,1)S(1)} %copy-done.3, bf16[2,4]{1,0:T(2,128)(2,1)S(1)} %bitcast.3), custom_call_target="tpu_custom_call" | custom-call | tf_op jit(solution)/shard_map/pallas_call | solution.py:427
  4.3 10.2 %all-to-all-start = ((bf16[16,61,4,128]{3,2,1,0:T(4,128)(2,1)}), bf16[16,61,4,128]{3,2,1,0:T(4,128)(2,1)S(1)}, u32[]{:S(2)}, u32[]{:S(2)}) async-start(bf16[16,61,4,128]{3,2,1,0:T(4,128)(2,1)} %shard_map.91), calls=%async_computation | async-start | bytes 1998848 | tf_op jit(solution)/shard_map/all_to_all | solution.py:433
  14.6 0.0 copy-done.2
  14.6 0.0 copy-done.6
  14.6 0.0 copy-done.7
  14.6 0.0 copy-done.9
  14.6 0.6 shard_map.92
  15.2 6.9 %collective-permute-start.1 = (bf16[432,128]{1,0:T(8,128)(2,1)S(1)}, bf16[432,128]{1,0:T(8,128)(2,1)S(1)}, u32[]{:S(2)}, u32[]{:S(2)}) collective-permute-start(bf16[432,128]{1,0:T(8,128)(2,1)S(1)} %shard_map.92), channel_id=1, source_target_pairs={{32,0},{64,32},{96,64},{128,96},{160,128},{192,160},{224,192},{256... | collective-permute-start | bytes 331784 | tf_op jit(solution)/shard_map/ppermute | solution.py:425
  22.1 1.9 %collective-permute-start = (bf16[432,128]{1,0:T(8,128)(2,1)S(1)}, bf16[432,128]{1,0:T(8,128)(2,1)S(1)}, u32[]{:S(2)}, u32[]{:S(2)}) collective-permute-start(bf16[432,128]{1,0:T(8,128)(2,1)S(1)} %shard_map.92), channel_id=1, source_target_pairs={{0,32},{32,64},{64,96},{96,128},{128,160},{160,192},{192,224},{224... | collective-permute-start | bytes 331784 | tf_op jit(solution)/shard_map/ppermute | solution.py:425
  24.0 1.3 %shard_map.94 = (f32[8,384,128]{2,1,0:T(8,128)S(1)}, f32[8,128]{1,0:T(8,128)S(1)}) custom-call(s32[8,128]{1,0:T(8,128)S(1)} %copy-done.6, f32[8,128]{1,0:T(8,128)S(1)} %copy-done.7, f32[8]{0:T(128)S(1)} %copy-done.9), custom_call_target="tpu_custom_call" | custom-call | flops 1000000000 | bytes 1600000 | tf_op jit(solution)/shard_map/pallas_call | solution.py:442
  25.3 0.0 copy-start.4
  25.3 0.0 copy-start.5
  25.3 14.7 %collective-permute-done.1.above = bf16[432,128]{1,0:T(8,128)(2,1)S(1)} collective-permute-done((bf16[432,128]{1,0:T(8,128)(2,1)S(1)}, bf16[432,128]{1,0:T(8,128)(2,1)S(1)}, u32[]{:S(2)}, u32[]{:S(2)}) %collective-permute-start.1) | collective-permute-done | bytes 110624 | tf_op jit(solution)/shard_map/ppermute | solution.py:425
  40.1 3.5 %collective-permute-done.below = bf16[432,128]{1,0:T(8,128)(2,1)S(1)} collective-permute-done((bf16[432,128]{1,0:T(8,128)(2,1)S(1)}, bf16[432,128]{1,0:T(8,128)(2,1)S(1)}, u32[]{:S(2)}, u32[]{:S(2)}) %collective-permute-start) | collective-permute-done | bytes 110624 | tf_op jit(solution)/shard_map/ppermute | solution.py:425
  43.6 1.4 %shard_map.93 = (f32[2,8,384,128]{3,2,1,0:T(8,128)S(1)}, f32[2,8,128]{2,1,0:T(8,128)S(1)}) custom-call(bf16[432,128]{1,0:T(8,128)(2,1)S(1)} %collective-permute-done.below, bf16[432,128]{1,0:T(8,128)(2,1)S(1)} %collective-permute-done.1.above), custom_call_target="tpu_custom_call" | custom-call | flops 2000000000 | bytes 3200000 | tf_op jit(solution)/shard_map/pallas_call | solution.py:449
  45.0 0.0 copy-start
  45.0 1.6 %copy-done = f32[2,8,384,128]{3,2,1,0:T(8,128)} copy-done((f32[2,8,384,128]{3,2,1,0:T(8,128)}, f32[2,8,384,128]{3,2,1,0:T(8,128)S(1)}, u32[]{:S(2)}) %copy-start) | copy-done | bytes 3145752
  46.6 0.0 all-to-all-done.received
  46.7 0.0 copy-done.4
  46.7 0.0 copy-done.5
  46.7 0.0 copy-start.1
  46.7 1.9 %copy-done.1 = f32[2,8,384,128]{3,2,1,0:T(8,128)S(1)} copy-done((f32[2,8,384,128]{3,2,1,0:T(8,128)S(1)}, f32[2,8,384,128]{3,2,1,0:T(8,128)}, u32[]{:S(2)}) %copy-start.1) | copy-done | bytes 3145752
  48.6 4.9 %shard_map.95 = (f32[2,6,64,128]{3,2,1,0:T(8,128)S(1)}, f32[2,6,64,128]{3,2,1,0:T(8,128)S(1)}, bf16[2,6,64,128]{3,2,1,0:T(8,128)(2,1)S(1)}, f32[8,128]{1,0:T(8,128)S(1)}) custom-call(bf16[16,61,4,128]{3,2,1,0:T(4,128)(2,1)S(1)} %all-to-all-done.received, bf16[432,128]{1,0:T(8,128)(2,1)S(1)} %collective-permute-done.below, ...), custom_call_target="tpu_custom_call" | custom-call | tf_op jit(solution)/shard_map/pallas_call | solution.py:458
  53.4 3.2 %collective-permute-start.3 = (bf16[2,6,64,128]{3,2,1,0:T(8,128)(2,1)S(1)}, bf16[2,6,64,128]{3,2,1,0:T(8,128)(2,1)S(1)}, u32[]{:S(2)}, u32[]{:S(2)}) collective-permute-start(bf16[2,6,64,128]{3,2,1,0:T(8,128)(2,1)S(1)} %get-tuple-element.19), channel_id=1, source_target_pairs={{32,0},{64,32},{96,64},{128,96},{160,128},{192,160},{224,192},{256... | collective-permute-start | bytes 589832 | tf_op jit(solution)/shard_map/ppermute | solution.py:425
  56.6 2.1 %collective-permute-start.2 = (bf16[2,6,64,128]{3,2,1,0:T(8,128)(2,1)S(1)}, bf16[2,6,64,128]{3,2,1,0:T(8,128)(2,1)S(1)}, u32[]{:S(2)}, u32[]{:S(2)}) collective-permute-start(bf16[2,6,64,128]{3,2,1,0:T(8,128)(2,1)S(1)} %get-tuple-element.19), channel_id=1, source_target_pairs={{0,32},{32,64},{64,96},{96,128},{128,160},{160,192},{192,224},{224... | collective-permute-start | bytes 589832 | tf_op jit(solution)/shard_map/ppermute | solution.py:425
  58.7 0.0 copy-start.10
  58.8 0.9 shard_map.96.partial
  59.7 0.5 collective-permute-done.3.above
  60.2 6.5 %collective-permute-done.2.below = bf16[2,6,64,128]{3,2,1,0:T(8,128)(2,1)S(1)} collective-permute-done((bf16[2,6,64,128]{3,2,1,0:T(8,128)(2,1)S(1)}, bf16[2,6,64,128]{3,2,1,0:T(8,128)(2,1)S(1)}, u32[]{:S(2)}, u32[]{:S(2)}) %collective-permute-start.2) | collective-permute-done | bytes 196640 | tf_op jit(solution)/shard_map/ppermute | solution.py:425
  66.7 0.3 shard_map.97
  67.0 25.1 %all_to_all.15.received = bf16[32,32,128]{2,1,0:T(8,128)(2,1)S(1)} all-to-all(bf16[32,32,128]{2,1,0:T(8,128)(2,1)S(1)} %shard_map.97), channel_id=1, replica_groups=mesh['row'=16,'col'=32] {'col'}, dimensions={0} | all-to-all | bytes 524288 | tf_op jit(solution)/shard_map/all_to_all | solution.py:480
  92.1 0.0 copy-done.10
  92.1 0.6 shard_map.98
  92.7 14.4 %all_to_all.16.received = bf16[32,24,128]{2,1,0:T(8,128)(2,1)S(1)} all-to-all(bf16[32,24,128]{2,1,0:T(8,128)(2,1)S(1)} %shard_map.98), channel_id=1, replica_groups=mesh['row'=16,'col'=32] {'col'}, dimensions={0} | all-to-all | bytes 393216 | tf_op jit(solution)/shard_map/all_to_all | solution.py:484
  107.2 0.8 shard_map.99
Async XLA Ops:
  0.0 14.6 %copy-start.2 = (f32[6,64,128]{2,1,0:T(8,128)S(1)}, f32[6,64,128]{2,1,0:T(8,128)}, u32[]{:S(2)}) copy-start(f32[6,64,128]{2,1,0:T(8,128)} %potential.5) | copy-start | bytes 589828
  0.0 1.0 copy-start.3
  1.0 0.7 copy-start.8
  1.6 12.9 %copy-start.6 = (s32[8,128]{1,0:T(8,128)S(1)}, s32[8,128]{1,0:T(8,128)}, u32[]{:S(2)}) copy-start(s32[8,128]{1,0:T(8,128)} %points.3) | copy-start | bytes 12292
  1.6 13.0 %copy-start.7 = (f32[8,128]{1,0:T(8,128)S(1)}, f32[8,128]{1,0:T(8,128)}, u32[]{:S(2)}) copy-start(f32[8,128]{1,0:T(8,128)} %projector.3) | copy-start | bytes 12292
  1.6 13.0 %copy-start.9 = (f32[8]{0:T(128)S(1)}, f32[8]{0:T(128)}, u32[]{:S(2)}) copy-start(f32[8]{0:T(128)} %strength.3) | copy-start | bytes 100
  4.3 42.3 %all-to-all-start = ((bf16[16,61,4,128]{3,2,1,0:T(4,128)(2,1)}), bf16[16,61,4,128]{3,2,1,0:T(4,128)(2,1)S(1)}, u32[]{:S(2)}, u32[]{:S(2)}) async-start(bf16[16,61,4,128]{3,2,1,0:T(4,128)(2,1)} %shard_map.91), calls=%async_computation | async-start | bytes 1998848 | tf_op jit(solution)/shard_map/all_to_all | solution.py:433
  15.2 24.9 %collective-permute-start.1 = (bf16[432,128]{1,0:T(8,128)(2,1)S(1)}, bf16[432,128]{1,0:T(8,128)(2,1)S(1)}, u32[]{:S(2)}, u32[]{:S(2)}) collective-permute-start(bf16[432,128]{1,0:T(8,128)(2,1)S(1)} %shard_map.92), channel_id=1, source_target_pairs={{32,0},{64,32},{96,64},{128,96},{160,128},{192,160},{224,192},{256... | collective-permute-start | bytes 331784 | tf_op jit(solution)/shard_map/ppermute | solution.py:425
  22.1 21.5 %collective-permute-start = (bf16[432,128]{1,0:T(8,128)(2,1)S(1)}, bf16[432,128]{1,0:T(8,128)(2,1)S(1)}, u32[]{:S(2)}, u32[]{:S(2)}) collective-permute-start(bf16[432,128]{1,0:T(8,128)(2,1)S(1)} %shard_map.92), channel_id=1, source_target_pairs={{0,32},{32,64},{64,96},{96,128},{128,160},{160,192},{192,224},{224... | collective-permute-start | bytes 331784 | tf_op jit(solution)/shard_map/ppermute | solution.py:425
  25.3 21.3 %copy-start.4 = (bf16[256,256]{1,0:T(8,128)(2,1)S(1)}, bf16[256,256]{1,0:T(8,128)(2,1)}, u32[]{:S(2)}) copy-start(bf16[256,256]{1,0:T(8,128)(2,1)} %constant.4.clone.along_z) | copy-start | bytes 393220
  25.3 21.3 %copy-start.5 = (bf16[128,128]{1,0:T(8,128)(2,1)S(1)}, bf16[128,128]{1,0:T(8,128)(2,1)}, u32[]{:S(2)}) copy-start(bf16[128,128]{1,0:T(8,128)(2,1)} %constant.5.clone.along_y) | copy-start | bytes 98308
  45.0 1.6 %copy-start = (f32[2,8,384,128]{3,2,1,0:T(8,128)}, f32[2,8,384,128]{3,2,1,0:T(8,128)S(1)}, u32[]{:S(2)}) copy-start(f32[2,8,384,128]{3,2,1,0:T(8,128)S(1)} %get-tuple-element.13.next_dense) | copy-start | bytes 9437188
  46.7 1.9 %copy-start.1 = (f32[2,8,384,128]{3,2,1,0:T(8,128)S(1)}, f32[2,8,384,128]{3,2,1,0:T(8,128)}, u32[]{:S(2)}) copy-start(f32[2,8,384,128]{3,2,1,0:T(8,128)} %copy-done) | copy-start | bytes 9437188
  53.4 6.7 %collective-permute-start.3 = (bf16[2,6,64,128]{3,2,1,0:T(8,128)(2,1)S(1)}, bf16[2,6,64,128]{3,2,1,0:T(8,128)(2,1)S(1)}, u32[]{:S(2)}, u32[]{:S(2)}) collective-permute-start(bf16[2,6,64,128]{3,2,1,0:T(8,128)(2,1)S(1)} %get-tuple-element.19), channel_id=1, source_target_pairs={{32,0},{64,32},{96,64},{128,96},{160,128},{192,160},{224,192},{256... | collective-permute-start | bytes 589832 | tf_op jit(solution)/shard_map/ppermute | solution.py:425
  56.6 10.0 %collective-permute-start.2 = (bf16[2,6,64,128]{3,2,1,0:T(8,128)(2,1)S(1)}, bf16[2,6,64,128]{3,2,1,0:T(8,128)(2,1)S(1)}, u32[]{:S(2)}, u32[]{:S(2)}) collective-permute-start(bf16[2,6,64,128]{3,2,1,0:T(8,128)(2,1)S(1)} %get-tuple-element.19), channel_id=1, source_target_pairs={{0,32},{32,64},{64,96},{96,128},{128,160},{160,192},{192,224},{224... | collective-permute-start | bytes 589832 | tf_op jit(solution)/shard_map/ppermute | solution.py:425
  58.7 33.3 %copy-start.10 = (s32[64]{0:T(128)S(1)}, s32[64]{0:T(128)}, u32[]{:S(2)}) copy-start(s32[64]{0:T(128)} %param.15) | copy-start | bytes 772

commit v3 on v1

v3 whole, which is shorter than its diff:
```python
import functools

import jax
import jax.numpy as jnp
import numpy as np
from jax import lax
from jax.experimental import pallas as pl
from jax.experimental.pallas import tpu as pltpu
from jax.sharding import PartitionSpec as P

F32 = jnp.float32
BF16 = jnp.bfloat16

STENCIL = (
    -5369.0 / 1800.0,
    12.0 / 7.0,
    -15.0 / 56.0,
    10.0 / 189.0,
    -1.0 / 112.0,
    2.0 / 1925.0,
    -1.0 / 16632.0,
)
CENTER = 7.0
HALF_WIDTH = 5.0

ROWS, COLS = 16, 32
SLAB, GY, GZ = 6, 64, 128
GX = ROWS * SLAB
YPART = GY // ROWS
WIDE = 3 * SLAB
ATOM_DEV = 8
SLAB_ROWS = SLAB * GY
SENT = 2 * WIDE + 1
HALF = ROWS // 2
PIECE = SLAB_ROWS // COLS // 4
OTHER_ROWS = SLAB_ROWS + 3 * ATOM_DEV

SIDE = tuple(-0.5 * c for c in STENCIL)
DIAGONAL = -0.5 * 3.0 * STENCIL[0] - CENTER

VMEM = pl.BlockSpec(memory_space=pltpu.VMEM)
PARAMS = pltpu.CompilerParams(vmem_limit_bytes=40 * 1024 * 1024)


def circulant(size):
    whole = np.zeros((size, size), np.float32)
    for offset in range(1, 7):
        for i in range(size):
            whole[i, (i + offset) % size] += SIDE[offset]
            whole[i, (i - offset) % size] += SIDE[offset]
    high = whole.astype(jnp.bfloat16)
    low = (whole - high.astype(np.float32)).astype(jnp.bfloat16)
    return high, low


def stencil_matrices():
    high, low = circulant(GZ)
    along_z = np.block([[high, low], [high, low]])
    high, low = circulant(GY)
    along_y = np.block([[high, high], [low, low]])
    return jnp.asarray(along_z), jnp.asarray(along_y)


def call(kernel, outs, scratch=(), flops=0, bytes_accessed=0, specs=None):
    return pl.pallas_call(
        kernel,
        out_shape=outs,
        in_specs=specs,
        out_specs=jax.tree.map(lambda _: VMEM, outs),
        scratch_shapes=list(scratch),
        compiler_params=PARAMS,
        cost_estimate=pl.CostEstimate(
            flops=flops, bytes_accessed=bytes_accessed, transcendentals=0
        ),
    )


def pack_kernel(orbitals, panel, out):
    row = lax.axis_index("row")
    place = lax.broadcasted_iota(jnp.int32, (2, GZ), 1)
    values = panel[...].astype(F32)
    tile = jnp.zeros((2, GZ), F32)
    for k in range(YPART):
        tile = jnp.where(place == YPART * row + k, values[:, k : k + 1], tile)
    tile = jnp.concatenate([tile, jnp.zeros((YPART - 2, GZ), F32)], axis=0).astype(BF16)
    for target in range(ROWS):
        state = target // HALF
        for index, slab in enumerate((target, target ^ HALF)):
            begin = (SLAB * slab - SLAB) % GX
            base = index * WIDE
            head = min(WIDE, GX - begin)
            out[target, base : base + head] = orbitals[state, begin : begin + head]
            if head < WIDE:
                out[target, base + head : base + WIDE] = orbitals[state, : WIDE - head]
        out[target, 2 * WIDE] = tile


def other_kernel(potential, points, projector, strength, out):
    for p in range(SLAB):
        out[p * GY : (p + 1) * GY, :] = potential[p]
    out[SLAB_ROWS : SLAB_ROWS + 8, :] = points[...].astype(F32)
    out[SLAB_ROWS + 8 : SLAB_ROWS + 16, :] = projector[...]
    for atom in range(ATOM_DEV):
        at = SLAB_ROWS + 16 + atom
        out[at : at + 1, :] = jnp.full((1, GZ), strength[atom], F32)


def densify(points, projector, dense):
    grid_row, lane = lax.shift_right_logical(points, 7), points & (GZ - 1)
    high = projector.astype(BF16).astype(F32)
    parts = (high, projector - high)
    for atom in range(ATOM_DEV):
        rows = jnp.where(
            lax.broadcasted_iota(jnp.int32, (SLAB_ROWS, GZ), 0) == grid_row[atom : atom + 1, :],
            1.0,
            0.0,
        ).astype(BF16)
        at_lane = lax.broadcasted_iota(jnp.int32, (GZ, GZ), 0) == lane[atom : atom + 1, :]
        lanes = [
            jnp.where(at_lane, part[atom : atom + 1, :], 0.0).astype(BF16) for part in parts
        ]
        dense[atom] = lax.dot_general(
            jnp.concatenate([rows] * 2, axis=1),
            jnp.concatenate(lanes, axis=1),
            (((1,), (1,)), ((), ())),
            preferred_element_type=F32,
        )


def project_kernel(points, projector, strength, dense, gains):
    densify(points[...], projector[...], dense)
    for atom in range(ATOM_DEV):
        gains[atom : atom + 1, :] = jnp.full((1, GZ), strength[atom], F32)


def project_other_kernel(given, dense, gains):
    points = given[SLAB_ROWS : SLAB_ROWS + 8, :].astype(jnp.int32)
    densify(points, given[SLAB_ROWS + 8 : SLAB_ROWS + 16, :], dense)
    gains[...] = given[SLAB_ROWS + 16 : SLAB_ROWS + 24, :]


def apply(planes, reach, scale, potentials, denses, gains, along_z, along_y, wide_z, summed_z, emit):
    weights = []
    for slab in range(2):
        partial = [None] * ATOM_DEV
        for p in range(SLAB):
            value = planes(slab, p)
            high = value.astype(BF16)
            low = (value - high.astype(F32)).astype(BF16)
            start = (slab * SLAB + p) * GY
            wide_z[start : start + GY, 0:GZ] = high
            wide_z[start : start + GY, GZ : 2 * GZ] = low
            for atom in range(ATOM_DEV):
                weight = denses[slab][atom, p * GY : (p + 1) * GY, :]
                term = jnp.sum((weight * value).reshape(GY // 8, 8, GZ), axis=0)
                partial[atom] = term if p == 0 else partial[atom] + term
        lines = [jnp.sum(term, axis=0, keepdims=True) for term in partial]
        total = jnp.sum(jnp.concatenate(lines, axis=0), axis=1, keepdims=True)
        weights.append(total * gains[slab][...])
    summed_z[...] = jnp.dot(wide_z[...], along_z[...], preferred_element_type=F32)
    for p in range(SLAB):
        both = jnp.concatenate(
            [
                jnp.concatenate(
                    [
                        wide_z[start : start + GY, 0:GZ],
                        wide_z[start : start + GY, GZ : 2 * GZ],
                    ],
                    axis=0,
                )
                for start in (p * GY, (SLAB + p) * GY)
            ],
            axis=1,
        )
        turned = jnp.dot(along_y[...], both, preferred_element_type=F32)
        turned = turned[:GY] + turned[GY:]
        for slab in range(2):
            start = (slab * SLAB + p) * GY
            level = DIAGONAL + potentials[slab](p)
            total = level * planes(slab, p) + turned[:, slab * GZ : (slab + 1) * GZ]
            total = total + (
                summed_z[start : start + GY, 0:GZ] + summed_z[start : start + GY, GZ : 2 * GZ]
            )
            for atom in range(ATOM_DEV):
                total = (
                    total
                    + weights[slab][atom : atom + 1, :]
                    * denses[slab][atom, p * GY : (p + 1) * GY, :]
                )
            for offset in range(1, 7):
                terms = [
                    planes(slab, k)
                    for k in (p - offset, p + offset)
                    if -reach <= k < SLAB + reach
                ]
                if terms:
                    total = total + SIDE[offset] * functools.reduce(jnp.add, terms)
            emit(slab, p, scale * total)


def potentials_of(own, other):
    return (lambda p: own[p]), (lambda p: other[p * GY : (p + 1) * GY, :])


def first_kernel(
    received, potential, other, dense, gains, other_dense, other_gains, along_z, along_y,
    start_out, next_out, sent_out, panel_out, slabs, wide_z, summed_z,
):
    panel = jnp.zeros((YPART, GZ), F32)
    for source in range(ROWS):
        for slab in range(2):
            slabs[slab, :, source * YPART : (source + 1) * YPART, :] = received[
                source, slab * WIDE : (slab + 1) * WIDE
            ].astype(F32)
        panel = panel + received[source, 2 * WIDE].astype(F32)
    mine = jnp.where(lax.axis_index("row") < HALF, panel[0:1], panel[1:2])
    panel_out[...] = jnp.broadcast_to(mine, (8, GZ))
    for slab in range(2):
        start_out[slab] = slabs[slab, SLAB : 2 * SLAB]

    def emit(slab, p, value):
        next_out[slab, p] = value
        sent_out[slab, p] = value.astype(BF16)

    apply(
        lambda slab, p: slabs[slab, SLAB + p], SLAB, 1.0 / HALF_WIDTH,
        potentials_of(potential, other), (dense, other_dense), (gains, other_gains),
        along_z, along_y, wide_z, summed_z, emit,
    )


def inside_kernel(
    current, previous, potential, other, dense, gains, other_dense, other_gains, along_z, along_y,
    out, wide_z, summed_z,
):
    def emit(slab, p, value):
        out[slab, p] = value - previous[slab, p]

    apply(
        lambda slab, p: current[slab, p], 0, 2.0 / HALF_WIDTH,
        potentials_of(potential, other), (dense, other_dense), (gains, other_gains),
        along_z, along_y, wide_z, summed_z, emit,
    )


def joining(partial, below, above):
    column = lax.axis_index("row") & (HALF - 1)
    lower = jnp.where(column == 0, 1, 0)
    upper = jnp.where(column == HALF - 1, 1, 0)

    def joined(slab, p):
        total = partial[slab, p]
        lower_slab = lower ^ slab
        upper_slab = upper ^ slab
        for offset in range(1, 7):
            terms = []
            if p - offset < 0:
                terms.append(below[lower_slab, SLAB + p - offset].astype(F32))
            if p + offset >= SLAB:
                terms.append(above[upper_slab, p + offset - SLAB].astype(F32))
            if terms:
                side = (2.0 / HALF_WIDTH) * SIDE[offset]
                total = total + side * functools.reduce(jnp.add, terms)
        return total

    return joined


def join_kernel(partial, below, above, next_out, sent_out):
    joined = joining(partial, below, above)
    for p in range(SLAB):
        for slab in range(2):
            value = joined(slab, p)
            next_out[slab, p] = value
            sent_out[slab, p] = value.astype(BF16)


def last_kernel(partial, below, above, panel, out, slabs):
    joined = joining(partial, below, above)
    for p in range(SLAB):
        for slab in range(2):
            slabs[slab, p * GY : (p + 1) * GY, :] = joined(slab, p)
    upper = lax.axis_index("row") // HALF
    line = lax.broadcasted_iota(jnp.int32, (4, GZ), 0)
    tile = jnp.where(line == 0, panel[0:4], 0.0).astype(BF16)
    for half in range(2):
        slab = upper ^ half
        for col in range(COLS):
            member = half * COLS + col
            for k in range(PIECE):
                at = 4 * (PIECE * col + k)
                out[member, k] = slabs[slab, at : at + 4, :].astype(BF16)
            out[member, PIECE] = tile


def rotate_kernel(received, panel_rows, out, states, wanted, rotated):
    members = 2 * COLS
    size = 4 * members
    for member in range(members):
        at = slice(4 * member, 4 * member + 4)
        for k in range(PIECE):
            states[at, k * GZ : (k + 1) * GZ] = received[member, k].astype(F32)
        tile = received[member, PIECE].astype(F32)
        wanted[at, :] = jnp.broadcast_to(tile[0:1], (4, GZ))
    order = lax.broadcasted_iota(jnp.int32, (size, 64), 0) >> 2
    state_of = 2 * (order & (COLS - 1)) + lax.shift_right_logical(order, 5)
    stored = jnp.where(panel_rows[...] == state_of, 1.0, 0.0).astype(BF16)
    spread = lax.dot_general(
        wanted[:, 0:64].astype(BF16), stored, (((1,), (1,)), ((), ())),
        preferred_element_type=F32,
    )
    same = (
        lax.broadcasted_iota(jnp.int32, (size, size), 0) & 3
    ) == (lax.broadcasted_iota(jnp.int32, (size, size), 1) & 3)
    spread = jnp.where(same, spread, 0.0).astype(BF16)
    rotated[...] = jnp.dot(spread, states[...].astype(BF16), preferred_element_type=F32)
    for col in range(COLS):
        for state in range(2):
            at = 4 * (state * COLS + col)
            for k in range(PIECE):
                out[col, state * PIECE + k] = rotated[
                    at : at + 4, k * GZ : (k + 1) * GZ
                ].astype(BF16)


def place_kernel(received, out):
    for col in range(COLS):
        for state in range(2):
            for k in range(PIECE):
                at = 4 * (PIECE * col + k)
                out[state, at : at + 4, :] = received[col, state * PIECE + k].astype(F32)


def per_device(orbitals, potential, proj_points, projector, strength, ritz_panel, panel_rows):
    shape = jax.ShapeDtypeStruct
    slabs_f32 = shape((2, SLAB, GY, GZ), F32)
    slabs_bf16 = shape((2, SLAB, GY, GZ), BF16)
    dense_gains = (shape((ATOM_DEV, SLAB_ROWS, GZ), F32), shape((ATOM_DEV, GZ), F32))
    along_z, along_y = stencil_matrices()
    smem = pl.BlockSpec(memory_space=pltpu.SMEM)
    work = [
        pltpu.VMEM((2 * SLAB_ROWS, 2 * GZ), BF16),
        pltpu.VMEM((2 * SLAB_ROWS, 2 * GZ), F32),
    ]
    around = [(i, i // HALF * HALF + (i + 1) % HALF) for i in range(ROWS)]

    packed = call(pack_kernel, shape((ROWS, SENT, YPART, GZ), BF16), specs=[VMEM] * 2)(
        orbitals, ritz_panel.T
    )
    regrouped = lax.all_to_all(packed, "row", split_axis=0, concat_axis=0, tiled=True)
    given = call(
        other_kernel,
        shape((OTHER_ROWS, GZ), F32),
        specs=[VMEM] * 3 + [smem],
        flops=1_000_000,
        bytes_accessed=400_000,
    )(potential, proj_points, projector, strength)
    other = lax.ppermute(given, "row", [(i, i ^ HALF) for i in range(ROWS)])
    dense, gains = call(
        project_kernel,
        dense_gains,
        specs=[VMEM, VMEM, smem],
        flops=1_000_000_000,
        bytes_accessed=1_600_000,
    )(proj_points, projector, strength)
    other_dense, other_gains = call(
        project_other_kernel,
        dense_gains,
        specs=[VMEM],
        flops=1_000_000_000,
        bytes_accessed=1_600_000,
    )(other)

    fixed = (potential, other, dense, gains, other_dense, other_gains, along_z, along_y)
    previous, current, sent, panel = call(
        first_kernel,
        (slabs_f32, slabs_f32, slabs_bf16, shape((8, GZ), F32)),
        scratch=[pltpu.VMEM((2, WIDE, GY, GZ), F32)] + work,
        specs=[VMEM] * 9,
    )(regrouped, *fixed)
    for step in range(2):
        below = lax.ppermute(sent, "row", around)
        above = lax.ppermute(sent, "row", [(d, s) for s, d in around])
        partial = call(
            inside_kernel,
            slabs_f32,
            scratch=work,
            specs=[VMEM] * 10,
            flops=2_000_000_000,
            bytes_accessed=3_000_000,
        )(current, previous, *fixed)
        if step == 0:
            previous = current
            current, sent = call(join_kernel, (slabs_f32, slabs_bf16), specs=[VMEM] * 3)(
                partial, below, above
            )
    layered = call(
        last_kernel,
        shape((2 * COLS, PIECE + 1, 4, GZ), BF16),
        scratch=[pltpu.VMEM((2, SLAB_ROWS, GZ), F32)],
        specs=[VMEM] * 4,
    )(partial, below, above, panel)
    both = [
        [(i + HALF * half) * COLS + col for half in range(2) for col in range(COLS)]
        for i in range(HALF)
    ]
    columns = lax.all_to_all(
        layered, ("row", "col"), split_axis=0, concat_axis=0, tiled=True, axis_index_groups=both
    )
    turned = call(
        rotate_kernel,
        shape((COLS, 2 * PIECE, 4, GZ), BF16),
        scratch=[
            pltpu.VMEM((8 * COLS, PIECE * GZ), F32),
            pltpu.VMEM((8 * COLS, GZ), F32),
            pltpu.VMEM((8 * COLS, PIECE * GZ), F32),
        ],
        specs=[VMEM] * 2,
    )(columns, panel_rows.reshape(1, -1))
    result = lax.all_to_all(turned, "col", split_axis=0, concat_axis=0, tiled=True)
    whole = call(place_kernel, shape((2, SLAB_ROWS, GZ), F32), specs=[VMEM])(result)
    return whole.reshape(2, SLAB, GY, GZ)


def solution(mesh):
    placed = (
        P("col", None, "row", None),
        P("row", None, None),
        P("row", None),
        P("row", None),
        P("row"),
        P("row", "col"),
        P(),
    )
    return jax.shard_map(
        per_device,
        mesh=mesh,
        in_specs=placed,
        out_specs=P("col", "row", None, None),
        check_vma=False,
    )
```

time: 102 us -> 101 us (level)
  waiting for transfers between devices: 29 us -> 17.4 us
  starting transfers between devices: 21.3 us -> 25.6 us
  blocking collectives: 42 us -> 45 us
  local copies, waits for them, and re-layouts: 1.73 us -> 4.23 us
    all_to_all x1, waiting for transfers between devices: 16.2 us -> 1.97 us  [per_device(): lax.all_to_all(packed, 'row', split_axis=0, concat_axis=0, tiled=True)]
    ppermute x4 -> x5, starting transfers between devices: 11.1 us -> 15.3 us  [the longest x2 5.29 us: per_device(): below = lax.ppermute(sent, 'row', around)]
    all_to_all x1, blocking collectives: 27.6 us -> 30.2 us  [per_device(): lax.all_to_all(layered, ('row', 'col'), split_axis=0, concat_axis=0, tile...]
    ppermute x4 -> x5, waiting for transfers between devices: 12.8 us -> 15.4 us  [the longest x2 7.71 us: per_device(): below = lax.ppermute(sent, 'row', around)]
    unnamed x17 -> x24, local copies, waits for them, and re-layouts: 1.73 us -> 4.23 us
    pallas_call x7 -> x9, Pallas kernels: 5.77 us -> 6.3 us  [the longest x2 1.83 us: per_device(): call(inside_kernel, slabs_f32, scratch=work, specs=[VMEM] * 10, flops=200...]
  transfers between devices with their start and end apart: 5 -> 6, of which waited for: 4 -> 6; matrix products, arithmetic and copies ran while one was open for 0% -> 0% of each run, Pallas kernels for 3% -> 4%
where the time goes in v3:
time: 101 us; the launch traced here: 100 us
  blocking collectives  45 us (45%)
  starting transfers between devices  25.6 us (25%)
  waiting for transfers between devices  17.4 us (17%)
  Pallas kernels  8.05 us (8%)
  local copies, waits for them, and re-layouts  4.23 us (4%)
    all_to_all x1, blocking collectives, per_device(): lax.all_to_all(layered, ('row', 'col'), split_axis=0, concat_axis=0, tile...  30.2 us
    all_to_all x1, blocking collectives, per_device(): lax.all_to_all(turned, 'col', split_axis=0, concat_axis=0, tiled=True)  14.8 us
    all_to_all x1, starting transfers between devices, per_device(): lax.all_to_all(packed, 'row', split_axis=0, concat_axis=0, tiled=True)  10.2 us
    ppermute x2, waiting for transfers between devices, per_device(): below = lax.ppermute(sent, 'row', around)  7.71 us
    ppermute x1, waiting for transfers between devices, per_device(): other = lax.ppermute(given, 'row', [(i, i ^ HALF) for i in range(ROWS)])  7.33 us
    ppermute x2, starting transfers between devices, per_device(): below = lax.ppermute(sent, 'row', around)  5.29 us
    ppermute x2, starting transfers between devices, per_device(): above = lax.ppermute(sent, 'row', [(d, s) for s, d in around])  5.28 us
    ppermute x1, starting transfers between devices, per_device(): other = lax.ppermute(given, 'row', [(i, i ^ HALF) for i in range(ROWS)])  4.78 us
  transfers between devices with their start and end apart: 6, of which 6 were waited for; matrix products, arithmetic and copies ran while one was open for 0% of the time, Pallas kernels for 4%

profile of v3, /device:TPU:1, one launch (start us, length us, event | category | flops | bytes accessed | tf_op | source)
XLA Modules:
  0.0 100.4 jit_solution(13362210798351396388)
XLA Ops:
  0.0 0.0 copy-start.3
  0.0 0.0 copy-start.4
  0.0 1.0 copy-done.4
  1.0 0.0 copy-start.10
  1.0 0.7 copy-done.10
  1.6 0.0 copy-start.7
  1.6 0.0 copy-start.8
  1.6 0.0 copy-start.9
  1.6 1.0 shard_map.91
  2.6 10.2 %all-to-all-start = ((bf16[16,37,4,128]{3,2,1,0:T(4,128)(2,1)}), bf16[16,37,4,128]{3,2,1,0:T(4,128)(2,1)S(1)}, u32[]{:S(2)}, u32[]{:S(2)}) async-start(bf16[16,37,4,128]{3,2,1,0:T(4,128)(2,1)} %shard_map.91), calls=%async_computation | async-start | bytes 1212416 | tf_op jit(solution)/shard_map/all_to_all | solution.py:350
  12.8 0.0 copy-done.3
  12.8 0.0 copy-done.7
  12.8 0.0 copy-done.8
  12.9 0.0 copy-done.9
  12.9 0.6 shard_map.92
  13.4 4.8 %collective-permute-start = (f32[408,128]{1,0:T(8,128)S(1)}, f32[408,128]{1,0:T(8,128)S(1)}, u32[]{:S(2)}, u32[]{:S(2)}) collective-permute-start(f32[408,128]{1,0:T(8,128)S(1)} %shard_map.92), channel_id=1, source_target_pairs={{0,256},{32,288},{64,320},{96,352},{128,384},{160,416},{192,448},{... | collective-permute-start | bytes 626696 | tf_op jit(solution)/shard_map/ppermute | solution.py:358
  18.2 1.1 %shard_map.93 = (f32[8,384,128]{2,1,0:T(8,128)S(1)}, f32[8,128]{1,0:T(8,128)S(1)}) custom-call(s32[8,128]{1,0:T(8,128)S(1)} %copy-done.7, f32[8,128]{1,0:T(8,128)S(1)} %copy-done.8, f32[8]{0:T(128)S(1)} %copy-done.9), custom_call_target="tpu_custom_call" | custom-call | flops 1000000000 | bytes 1600000 | tf_op jit(solution)/shard_map/pallas_call | solution.py:359
  19.3 0.0 copy-start.5
  19.3 0.0 copy-start.6
  19.4 7.3 %collective-permute-done.given.other = f32[408,128]{1,0:T(8,128)S(1)} collective-permute-done((f32[408,128]{1,0:T(8,128)S(1)}, f32[408,128]{1,0:T(8,128)S(1)}, u32[]{:S(2)}, u32[]{:S(2)}) %collective-permute-start) | collective-permute-done | bytes 208928 | tf_op jit(solution)/shard_map/ppermute | solution.py:358
  26.7 0.6 shard_map.94
  27.3 0.0 copy-start
  27.3 1.2 %copy-done = f32[8,384,128]{2,1,0:T(8,128)} copy-done((f32[8,384,128]{2,1,0:T(8,128)}, f32[8,384,128]{2,1,0:T(8,128)S(1)}, u32[]{:S(2)}) %copy-start) | copy-done | bytes 1572888
  28.4 2.0 %all-to-all-done.received = bf16[16,37,4,128]{3,2,1,0:T(4,128)(2,1)S(1)} async-done(((bf16[16,37,4,128]{3,2,1,0:T(4,128)(2,1)}), bf16[16,37,4,128]{3,2,1,0:T(4,128)(2,1)S(1)}, u32[]{:S(2)}, u32[]{:S(2)}) %all-to-all-start) | async-done | bytes 606240 | tf_op jit(solution)/shard_map/all_to_all | solution.py:350
  30.4 0.0 copy-done.5
  30.4 0.0 copy-done.6
  30.4 1.4 %copy-done.1 = f32[8,384,128]{2,1,0:T(8,128)S(1)} copy-done((f32[8,384,128]{2,1,0:T(8,128)S(1)}, f32[8,384,128]{2,1,0:T(8,128)}, u32[]{:S(2)}) %copy-start.1) | copy-done | bytes 1572888
  31.8 1.2 %shard_map.95 = (f32[2,6,64,128]{3,2,1,0:T(8,128)S(1)}, f32[2,6,64,128]{3,2,1,0:T(8,128)S(1)}, bf16[2,6,64,128]{3,2,1,0:T(8,128)(2,1)S(1)}, f32[8,128]{1,0:T(8,128)S(1)}) custom-call(bf16[16,37,4,128]{3,2,1,0:T(4,128)(2,1)S(1)} %all-to-all-done.received, f32[6,64,128]{2,1,0:T(8,128)S(1)} %copy-done.3, f32[408,128]{1,0:T(8,128)S(1)} %collective-permute-done.given.other, ...), custom_call_target="tpu_custom_call" | custom-call | tf_op jit(solution)/shard_map/pallas_call | solution.py:375
  33.1 2.6 %collective-permute-start.2 = (bf16[2,6,64,128]{3,2,1,0:T(8,128)(2,1)S(1)}, bf16[2,6,64,128]{3,2,1,0:T(8,128)(2,1)S(1)}, u32[]{:S(2)}, u32[]{:S(2)}) collective-permute-start(bf16[2,6,64,128]{3,2,1,0:T(8,128)(2,1)S(1)} %get-tuple-element.21), channel_id=1, source_target_pairs={{32,0},{64,32},{96,64},{128,96},{160,128},{192,160},{224,192},{0,2... | collective-permute-start | bytes 589832 | tf_op jit(solution)/shard_map/ppermute | solution.py:383
  35.7 2.7 %collective-permute-start.1 = (bf16[2,6,64,128]{3,2,1,0:T(8,128)(2,1)S(1)}, bf16[2,6,64,128]{3,2,1,0:T(8,128)(2,1)S(1)}, u32[]{:S(2)}, u32[]{:S(2)}) collective-permute-start(bf16[2,6,64,128]{3,2,1,0:T(8,128)(2,1)S(1)} %get-tuple-element.21), channel_id=1, source_target_pairs={{0,32},{32,64},{64,96},{96,128},{128,160},{160,192},{192,224},{224... | collective-permute-start | bytes 589832 | tf_op jit(solution)/shard_map/ppermute | solution.py:382
  38.4 0.0 copy-start.2
  38.4 1.0 shard_map.96.partial
  39.3 0.1 collective-permute-done.2.above
  39.5 3.8 %collective-permute-done.1.below = bf16[2,6,64,128]{3,2,1,0:T(8,128)(2,1)S(1)} collective-permute-done((bf16[2,6,64,128]{3,2,1,0:T(8,128)(2,1)S(1)}, bf16[2,6,64,128]{3,2,1,0:T(8,128)(2,1)S(1)}, u32[]{:S(2)}, u32[]{:S(2)}) %collective-permute-start.1) | collective-permute-done | bytes 196640 | tf_op jit(solution)/shard_map/ppermute | solution.py:382
  43.3 0.3 shard_map.97
  43.5 2.7 %collective-permute-start.4 = (bf16[2,6,64,128]{3,2,1,0:T(8,128)(2,1)S(1)}, bf16[2,6,64,128]{3,2,1,0:T(8,128)(2,1)S(1)}, u32[]{:S(2)}, u32[]{:S(2)}) collective-permute-start(bf16[2,6,64,128]{3,2,1,0:T(8,128)(2,1)S(1)} %get-tuple-element.23), channel_id=1, source_target_pairs={{32,0},{64,32},{96,64},{128,96},{160,128},{192,160},{224,192},{0,2... | collective-permute-start | bytes 589832 | tf_op jit(solution)/shard_map/ppermute | solution.py:383
  46.2 2.6 %collective-permute-start.3 = (bf16[2,6,64,128]{3,2,1,0:T(8,128)(2,1)S(1)}, bf16[2,6,64,128]{3,2,1,0:T(8,128)(2,1)S(1)}, u32[]{:S(2)}, u32[]{:S(2)}) collective-permute-start(bf16[2,6,64,128]{3,2,1,0:T(8,128)(2,1)S(1)} %get-tuple-element.23), channel_id=1, source_target_pairs={{0,32},{32,64},{64,96},{96,128},{128,160},{160,192},{192,224},{224... | collective-permute-start | bytes 589832 | tf_op jit(solution)/shard_map/ppermute | solution.py:382
  48.8 0.0 copy-done.2
  48.9 0.9 shard_map.98.partial
  49.7 0.0 copy-start.11
  49.7 0.2 collective-permute-done.4.above
  50.0 3.9 %collective-permute-done.3.below = bf16[2,6,64,128]{3,2,1,0:T(8,128)(2,1)S(1)} collective-permute-done((bf16[2,6,64,128]{3,2,1,0:T(8,128)(2,1)S(1)}, bf16[2,6,64,128]{3,2,1,0:T(8,128)(2,1)S(1)}, u32[]{:S(2)}, u32[]{:S(2)}) %collective-permute-start.3) | collective-permute-done | bytes 196640 | tf_op jit(solution)/shard_map/ppermute | solution.py:382
  53.9 0.3 shard_map.99
  54.2 30.2 %all_to_all.15.received = bf16[64,4,4,128]{3,2,1,0:T(4,128)(2,1)S(1)} all-to-all(bf16[64,4,4,128]{3,2,1,0:T(4,128)(2,1)S(1)} %shard_map.99), channel_id=1, replica_groups={{0,1,2,3,4,5,6,7,8,9,10,11,12,13,14,15,16,17,18,19,20,21,22,23,24,25,26..., dimensions={0} | all-to-all | bytes 524288 | tf_op jit(solution)/shard_map/all_to_all | solution.py:407
  84.4 0.0 copy-done.11
  84.4 0.4 shard_map.100
  84.8 14.8 %all_to_all.16.received = bf16[32,6,4,128]{3,2,1,0:T(4,128)(2,1)S(1)} all-to-all(bf16[32,6,4,128]{3,2,1,0:T(4,128)(2,1)S(1)} %shard_map.100), channel_id=1, replica_groups=mesh['row'=16,'col'=32] {'col'}, dimensions={0} | all-to-all | bytes 393216 | tf_op jit(solution)/shard_map/all_to_all | solution.py:420
  99.6 0.8 shard_map.101
  (1 shorter events, 0.0 us)
Async XLA Ops:
  0.0 12.8 %copy-start.3 = (f32[6,64,128]{2,1,0:T(8,128)S(1)}, f32[6,64,128]{2,1,0:T(8,128)}, u32[]{:S(2)}) copy-start(f32[6,64,128]{2,1,0:T(8,128)} %potential.7) | copy-start | bytes 589828
  0.0 1.0 copy-start.4
  1.0 0.7 copy-start.10
  1.6 11.2 %copy-start.7 = (s32[8,128]{1,0:T(8,128)S(1)}, s32[8,128]{1,0:T(8,128)}, u32[]{:S(2)}) copy-start(s32[8,128]{1,0:T(8,128)} %points.3) | copy-start | bytes 12292
  1.6 11.2 %copy-start.8 = (f32[8,128]{1,0:T(8,128)S(1)}, f32[8,128]{1,0:T(8,128)}, u32[]{:S(2)}) copy-start(f32[8,128]{1,0:T(8,128)} %projector.3) | copy-start | bytes 12292
  1.6 11.2 %copy-start.9 = (f32[8]{0:T(128)S(1)}, f32[8]{0:T(128)}, u32[]{:S(2)}) copy-start(f32[8]{0:T(128)} %strength.3) | copy-start | bytes 100
  2.6 27.8 %all-to-all-start = ((bf16[16,37,4,128]{3,2,1,0:T(4,128)(2,1)}), bf16[16,37,4,128]{3,2,1,0:T(4,128)(2,1)S(1)}, u32[]{:S(2)}, u32[]{:S(2)}) async-start(bf16[16,37,4,128]{3,2,1,0:T(4,128)(2,1)} %shard_map.91), calls=%async_computation | async-start | bytes 1212416 | tf_op jit(solution)/shard_map/all_to_all | solution.py:350
  13.4 13.3 %collective-permute-start = (f32[408,128]{1,0:T(8,128)S(1)}, f32[408,128]{1,0:T(8,128)S(1)}, u32[]{:S(2)}, u32[]{:S(2)}) collective-permute-start(f32[408,128]{1,0:T(8,128)S(1)} %shard_map.92), channel_id=1, source_target_pairs={{0,256},{32,288},{64,320},{96,352},{128,384},{160,416},{192,448},{... | collective-permute-start | bytes 626696 | tf_op jit(solution)/shard_map/ppermute | solution.py:358
  19.3 11.1 %copy-start.5 = (bf16[256,256]{1,0:T(8,128)(2,1)S(1)}, bf16[256,256]{1,0:T(8,128)(2,1)}, u32[]{:S(2)}) copy-start(bf16[256,256]{1,0:T(8,128)(2,1)} %constant.4.clone.along_z) | copy-start | bytes 393220
  19.3 11.1 %copy-start.6 = (bf16[128,128]{1,0:T(8,128)(2,1)S(1)}, bf16[128,128]{1,0:T(8,128)(2,1)}, u32[]{:S(2)}) copy-start(bf16[128,128]{1,0:T(8,128)(2,1)} %constant.5.clone.along_y) | copy-start | bytes 98308
  27.3 1.2 %copy-start = (f32[8,384,128]{2,1,0:T(8,128)}, f32[8,384,128]{2,1,0:T(8,128)S(1)}, u32[]{:S(2)}) copy-start(f32[8,384,128]{2,1,0:T(8,128)S(1)} %get-tuple-element.17.other_dense) | copy-start | bytes 4718596
  30.4 1.4 %copy-start.1 = (f32[8,384,128]{2,1,0:T(8,128)S(1)}, f32[8,384,128]{2,1,0:T(8,128)}, u32[]{:S(2)}) copy-start(f32[8,384,128]{2,1,0:T(8,128)} %copy-done) | copy-start | bytes 4718596
  33.1 6.4 %collective-permute-start.2 = (bf16[2,6,64,128]{3,2,1,0:T(8,128)(2,1)S(1)}, bf16[2,6,64,128]{3,2,1,0:T(8,128)(2,1)S(1)}, u32[]{:S(2)}, u32[]{:S(2)}) collective-permute-start(bf16[2,6,64,128]{3,2,1,0:T(8,128)(2,1)S(1)} %get-tuple-element.21), channel_id=1, source_target_pairs={{32,0},{64,32},{96,64},{128,96},{160,128},{192,160},{224,192},{0,2... | collective-permute-start | bytes 589832 | tf_op jit(solution)/shard_map/ppermute | solution.py:383
  35.7 7.6 %collective-permute-start.1 = (bf16[2,6,64,128]{3,2,1,0:T(8,128)(2,1)S(1)}, bf16[2,6,64,128]{3,2,1,0:T(8,128)(2,1)S(1)}, u32[]{:S(2)}, u32[]{:S(2)}) collective-permute-start(bf16[2,6,64,128]{3,2,1,0:T(8,128)(2,1)S(1)} %get-tuple-element.21), channel_id=1, source_target_pairs={{0,32},{32,64},{64,96},{96,128},{128,160},{160,192},{192,224},{224... | collective-permute-start | bytes 589832 | tf_op jit(solution)/shard_map/ppermute | solution.py:382
  38.4 10.5 %copy-start.2 = (f32[8,384,128]{2,1,0:T(8,128)S(1)}, f32[8,384,128]{2,1,0:T(8,128)}, u32[]{:S(2)}) copy-start(f32[8,384,128]{2,1,0:T(8,128)} %copy-done) | copy-start | bytes 4718596
  43.5 6.4 %collective-permute-start.4 = (bf16[2,6,64,128]{3,2,1,0:T(8,128)(2,1)S(1)}, bf16[2,6,64,128]{3,2,1,0:T(8,128)(2,1)S(1)}, u32[]{:S(2)}, u32[]{:S(2)}) collective-permute-start(bf16[2,6,64,128]{3,2,1,0:T(8,128)(2,1)S(1)} %get-tuple-element.23), channel_id=1, source_target_pairs={{32,0},{64,32},{96,64},{128,96},{160,128},{192,160},{224,192},{0,2... | collective-permute-start | bytes 589832 | tf_op jit(solution)/shard_map/ppermute | solution.py:383
  46.2 7.6 %collective-permute-start.3 = (bf16[2,6,64,128]{3,2,1,0:T(8,128)(2,1)S(1)}, bf16[2,6,64,128]{3,2,1,0:T(8,128)(2,1)S(1)}, u32[]{:S(2)}, u32[]{:S(2)}) collective-permute-start(bf16[2,6,64,128]{3,2,1,0:T(8,128)(2,1)S(1)} %get-tuple-element.23), channel_id=1, source_target_pairs={{0,32},{32,64},{64,96},{96,128},{128,160},{160,192},{192,224},{224... | collective-permute-start | bytes 589832 | tf_op jit(solution)/shard_map/ppermute | solution.py:382
  49.7 34.6 %copy-start.11 = (s32[64]{0:T(128)S(1)}, s32[64]{0:T(128)}, u32[]{:S(2)}) copy-start(s32[64]{0:T(128)} %param.15) | copy-start | bytes 772

commit v4 on v3

--- a/solution.py
+++ b/solution.py
@@ -39,7 +39,7 @@
 DIAGONAL = -0.5 * 3.0 * STENCIL[0] - CENTER
 
 VMEM = pl.BlockSpec(memory_space=pltpu.VMEM)
-PARAMS = pltpu.CompilerParams(vmem_limit_bytes=40 * 1024 * 1024)
+MIB = 1024 * 1024
 
 
 def circulant(size):
@@ -61,38 +61,52 @@
     return jnp.asarray(along_z), jnp.asarray(along_y)
 
 
-def call(kernel, outs, scratch=(), flops=0, bytes_accessed=0, specs=None):
+def call(kernel, outs, scratch=(), flops=0, bytes_accessed=0, specs=None, vmem=12 * MIB):
     return pl.pallas_call(
         kernel,
         out_shape=outs,
         in_specs=specs,
         out_specs=jax.tree.map(lambda _: VMEM, outs),
         scratch_shapes=list(scratch),
-        compiler_params=PARAMS,
+        compiler_params=pltpu.CompilerParams(vmem_limit_bytes=vmem),
         cost_estimate=pl.CostEstimate(
             flops=flops, bytes_accessed=bytes_accessed, transcendentals=0
         ),
     )
 
 
-def pack_kernel(orbitals, panel, out):
+def pack_kernel(orbitals, panel, out, states, columns, sems):
+    copies = [
+        pltpu.make_async_copy(source, target, sems.at[i])
+        for i, (source, target) in enumerate(
+            [
+                (panel, columns),
+                (orbitals.at[0], states.at[0]),
+                (orbitals.at[1], states.at[1]),
+            ]
+        )
+    ]
+    for copy in copies:
+        copy.start()
     row = lax.axis_index("row")
     place = lax.broadcasted_iota(jnp.int32, (2, GZ), 1)
-    values = panel[...].astype(F32)
+    copies[0].wait()
+    values = columns[...].astype(F32)
     tile = jnp.zeros((2, GZ), F32)
     for k in range(YPART):
         tile = jnp.where(place == YPART * row + k, values[:, k : k + 1], tile)
     tile = jnp.concatenate([tile, jnp.zeros((YPART - 2, GZ), F32)], axis=0).astype(BF16)
-    for target in range(ROWS):
-        state = target // HALF
-        for index, slab in enumerate((target, target ^ HALF)):
-            begin = (SLAB * slab - SLAB) % GX
-            base = index * WIDE
-            head = min(WIDE, GX - begin)
-            out[target, base : base + head] = orbitals[state, begin : begin + head]
-            if head < WIDE:
-                out[target, base + head : base + WIDE] = orbitals[state, : WIDE - head]
-        out[target, 2 * WIDE] = tile
+    for state in range(2):
+        copies[1 + state].wait()
+        for target in range(HALF * state, HALF * state + HALF):
+            for index, slab in enumerate((target, target ^ HALF)):
+                begin = (SLAB * slab - SLAB) % GX
+                base = index * WIDE
+                head = min(WIDE, GX - begin)
+                out[target, base : base + head] = states[state, begin : begin + head]
+                if head < WIDE:
+                    out[target, base + head : base + WIDE] = states[state, : WIDE - head]
+            out[target, 2 * WIDE] = tile
 
 
 def other_kernel(potential, points, projector, strength, out):
@@ -344,9 +358,17 @@
     ]
     around = [(i, i // HALF * HALF + (i + 1) % HALF) for i in range(ROWS)]
 
-    packed = call(pack_kernel, shape((ROWS, SENT, YPART, GZ), BF16), specs=[VMEM] * 2)(
-        orbitals, ritz_panel.T
-    )
+    packed = call(
+        pack_kernel,
+        shape((ROWS, SENT, YPART, GZ), BF16),
+        scratch=[
+            pltpu.VMEM((2, GX, YPART, GZ), BF16),
+            pltpu.VMEM((2, YPART), BF16),
+            pltpu.SemaphoreType.DMA((3,)),
+        ],
+        specs=[pl.BlockSpec(memory_space=pl.ANY)] * 2,
+        vmem=60 * MIB,
+    )(orbitals, ritz_panel.T)
     regrouped = lax.all_to_all(packed, "row", split_axis=0, concat_axis=0, tiled=True)
     given = call(
         other_kernel,

time: 101 us -> 100 us (0.990)
  local copies, waits for them, and re-layouts: 4.23 us -> 2.61 us
  Pallas kernels: 8.05 us -> 9.27 us
    unnamed x24 -> x20, local copies, waits for them, and re-layouts: 4.23 us -> 2.61 us
where the time goes in v4:
time: 100 us; the launch traced here: 99.8 us
  blocking collectives  45 us (45%)
  starting transfers between devices  25.6 us (26%)
  waiting for transfers between devices  17.2 us (17%)
  Pallas kernels  9.27 us (9%)
  local copies, waits for them, and re-layouts  2.61 us (3%)
    all_to_all x1, blocking collectives, per_device(): lax.all_to_all(layered, ('row', 'col'), split_axis=0, concat_axis=0, tile...  30.2 us
    all_to_all x1, blocking collectives, per_device(): lax.all_to_all(turned, 'col', split_axis=0, concat_axis=0, tiled=True)  14.8 us
    all_to_all x1, starting transfers between devices, per_device(): lax.all_to_all(packed, 'row', split_axis=0, concat_axis=0, tiled=True)  10.2 us
    ppermute x2, waiting for transfers between devices, per_device(): below = lax.ppermute(sent, 'row', around)  7.72 us
    ppermute x1, waiting for transfers between devices, per_device(): other = lax.ppermute(given, 'row', [(i, i ^ HALF) for i in range(ROWS)])  7.33 us
    ppermute x2, starting transfers between devices, per_device(): below = lax.ppermute(sent, 'row', around)  5.28 us
    ppermute x2, starting transfers between devices, per_device(): above = lax.ppermute(sent, 'row', [(d, s) for s, d in around])  5.28 us
    ppermute x1, starting transfers between devices, per_device(): other = lax.ppermute(given, 'row', [(i, i ^ HALF) for i in range(ROWS)])  4.78 us
  transfers between devices with their start and end apart: 6, of which 6 were waited for; matrix products, arithmetic and copies ran while one was open for 0% of the time, Pallas kernels for 4%

profile of v4, /device:TPU:1, one launch (start us, length us, event | category | flops | bytes accessed | tf_op | source)
XLA Modules:
  0.0 99.8 jit_solution(9949945476667892543)
XLA Ops:
  0.0 0.0 copy-start.3
  0.0 0.0 copy-start.8
  0.0 0.0 copy-start.7
  0.0 0.0 copy-start.6
  0.0 1.9 %shard_map.91 = bf16[16,37,4,128]{3,2,1,0:T(4,128)(2,1)} custom-call(bf16[2,96,4,128]{3,2,1,0:T(4,128)(2,1)} %orbitals.1, bf16[2,4]{1,0:T(2,128)(2,1)} %bitcast.4), custom_call_target="tpu_custom_call" | custom-call | tf_op jit(solution)/shard_map/pallas_call | solution.py:361
  2.0 10.2 %all-to-all-start = ((bf16[16,37,4,128]{3,2,1,0:T(4,128)(2,1)}), bf16[16,37,4,128]{3,2,1,0:T(4,128)(2,1)S(1)}, u32[]{:S(2)}, u32[]{:S(2)}) async-start(bf16[16,37,4,128]{3,2,1,0:T(4,128)(2,1)} %shard_map.91), calls=%async_computation | async-start | bytes 1212416 | tf_op jit(solution)/shard_map/all_to_all | solution.py:372
  12.2 0.0 copy-done.3
  12.2 0.0 copy-done.8
  12.2 0.0 copy-done.7
  12.2 0.0 copy-done.6
  12.3 0.6 shard_map.92
  12.8 4.8 %collective-permute-start = (f32[408,128]{1,0:T(8,128)S(1)}, f32[408,128]{1,0:T(8,128)S(1)}, u32[]{:S(2)}, u32[]{:S(2)}) collective-permute-start(f32[408,128]{1,0:T(8,128)S(1)} %shard_map.92), channel_id=1, source_target_pairs={{0,256},{32,288},{64,320},{96,352},{128,384},{160,416},{192,448},{... | collective-permute-start | bytes 626696 | tf_op jit(solution)/shard_map/ppermute | solution.py:380
  17.6 1.1 %shard_map.93 = (f32[8,384,128]{2,1,0:T(8,128)S(1)}, f32[8,128]{1,0:T(8,128)S(1)}) custom-call(s32[8,128]{1,0:T(8,128)S(1)} %copy-done.6, f32[8,128]{1,0:T(8,128)S(1)} %copy-done.7, f32[8]{0:T(128)S(1)} %copy-done.8), custom_call_target="tpu_custom_call" | custom-call | flops 1000000000 | bytes 1600000 | tf_op jit(solution)/shard_map/pallas_call | solution.py:381
  18.7 0.0 copy-start.4
  18.7 0.0 copy-start.5
  18.7 7.3 %collective-permute-done.given.other = f32[408,128]{1,0:T(8,128)S(1)} collective-permute-done((f32[408,128]{1,0:T(8,128)S(1)}, f32[408,128]{1,0:T(8,128)S(1)}, u32[]{:S(2)}, u32[]{:S(2)}) %collective-permute-start) | collective-permute-done | bytes 208928 | tf_op jit(solution)/shard_map/ppermute | solution.py:380
  26.1 0.6 shard_map.94
  26.7 0.0 copy-start
  26.7 1.2 %copy-done = f32[8,384,128]{2,1,0:T(8,128)} copy-done((f32[8,384,128]{2,1,0:T(8,128)}, f32[8,384,128]{2,1,0:T(8,128)S(1)}, u32[]{:S(2)}) %copy-start) | copy-done | bytes 1572888
  27.8 2.0 %all-to-all-done.received = bf16[16,37,4,128]{3,2,1,0:T(4,128)(2,1)S(1)} async-done(((bf16[16,37,4,128]{3,2,1,0:T(4,128)(2,1)}), bf16[16,37,4,128]{3,2,1,0:T(4,128)(2,1)S(1)}, u32[]{:S(2)}, u32[]{:S(2)}) %all-to-all-start) | async-done | bytes 606240 | tf_op jit(solution)/shard_map/all_to_all | solution.py:372
  29.8 0.0 copy-done.4
  29.8 0.0 copy-done.5
  29.8 0.0 copy-start.1
  29.8 1.4 %copy-done.1 = f32[8,384,128]{2,1,0:T(8,128)S(1)} copy-done((f32[8,384,128]{2,1,0:T(8,128)S(1)}, f32[8,384,128]{2,1,0:T(8,128)}, u32[]{:S(2)}) %copy-start.1) | copy-done | bytes 1572888
  31.2 1.3 %shard_map.95 = (f32[2,6,64,128]{3,2,1,0:T(8,128)S(1)}, f32[2,6,64,128]{3,2,1,0:T(8,128)S(1)}, bf16[2,6,64,128]{3,2,1,0:T(8,128)(2,1)S(1)}, f32[8,128]{1,0:T(8,128)S(1)}) custom-call(bf16[16,37,4,128]{3,2,1,0:T(4,128)(2,1)S(1)} %all-to-all-done.received, f32[6,64,128]{2,1,0:T(8,128)S(1)} %copy-done.3, f32[408,128]{1,0:T(8,128)S(1)} %collective-permute-done.given.other, ...), custom_call_target="tpu_custom_call" | custom-call | tf_op jit(solution)/shard_map/pallas_call | solution.py:397
  32.5 2.6 %collective-permute-start.2 = (bf16[2,6,64,128]{3,2,1,0:T(8,128)(2,1)S(1)}, bf16[2,6,64,128]{3,2,1,0:T(8,128)(2,1)S(1)}, u32[]{:S(2)}, u32[]{:S(2)}) collective-permute-start(bf16[2,6,64,128]{3,2,1,0:T(8,128)(2,1)S(1)} %get-tuple-element.21), channel_id=1, source_target_pairs={{32,0},{64,32},{96,64},{128,96},{160,128},{192,160},{224,192},{0,2... | collective-permute-start | bytes 589832 | tf_op jit(solution)/shard_map/ppermute | solution.py:405
  35.2 2.7 %collective-permute-start.1 = (bf16[2,6,64,128]{3,2,1,0:T(8,128)(2,1)S(1)}, bf16[2,6,64,128]{3,2,1,0:T(8,128)(2,1)S(1)}, u32[]{:S(2)}, u32[]{:S(2)}) collective-permute-start(bf16[2,6,64,128]{3,2,1,0:T(8,128)(2,1)S(1)} %get-tuple-element.21), channel_id=1, source_target_pairs={{0,32},{32,64},{64,96},{96,128},{128,160},{160,192},{192,224},{224... | collective-permute-start | bytes 589832 | tf_op jit(solution)/shard_map/ppermute | solution.py:404
  37.8 0.0 copy-start.2
  37.9 1.0 shard_map.96.partial
  38.8 0.1 collective-permute-done.2.above
  39.0 3.8 %collective-permute-done.1.below = bf16[2,6,64,128]{3,2,1,0:T(8,128)(2,1)S(1)} collective-permute-done((bf16[2,6,64,128]{3,2,1,0:T(8,128)(2,1)S(1)}, bf16[2,6,64,128]{3,2,1,0:T(8,128)(2,1)S(1)}, u32[]{:S(2)}, u32[]{:S(2)}) %collective-permute-start.1) | collective-permute-done | bytes 196640 | tf_op jit(solution)/shard_map/ppermute | solution.py:404
  42.8 0.2 shard_map.97
  43.0 2.7 %collective-permute-start.4 = (bf16[2,6,64,128]{3,2,1,0:T(8,128)(2,1)S(1)}, bf16[2,6,64,128]{3,2,1,0:T(8,128)(2,1)S(1)}, u32[]{:S(2)}, u32[]{:S(2)}) collective-permute-start(bf16[2,6,64,128]{3,2,1,0:T(8,128)(2,1)S(1)} %get-tuple-element.23), channel_id=1, source_target_pairs={{32,0},{64,32},{96,64},{128,96},{160,128},{192,160},{224,192},{0,2... | collective-permute-start | bytes 589832 | tf_op jit(solution)/shard_map/ppermute | solution.py:405
  45.7 2.6 %collective-permute-start.3 = (bf16[2,6,64,128]{3,2,1,0:T(8,128)(2,1)S(1)}, bf16[2,6,64,128]{3,2,1,0:T(8,128)(2,1)S(1)}, u32[]{:S(2)}, u32[]{:S(2)}) collective-permute-start(bf16[2,6,64,128]{3,2,1,0:T(8,128)(2,1)S(1)} %get-tuple-element.23), channel_id=1, source_target_pairs={{0,32},{32,64},{64,96},{96,128},{128,160},{160,192},{192,224},{224... | collective-permute-start | bytes 589832 | tf_op jit(solution)/shard_map/ppermute | solution.py:404
  48.3 0.0 copy-done.2
  48.3 1.0 shard_map.98.partial
  49.3 0.0 copy-start.9
  49.3 0.1 collective-permute-done.4.above
  49.4 3.9 %collective-permute-done.3.below = bf16[2,6,64,128]{3,2,1,0:T(8,128)(2,1)S(1)} collective-permute-done((bf16[2,6,64,128]{3,2,1,0:T(8,128)(2,1)S(1)}, bf16[2,6,64,128]{3,2,1,0:T(8,128)(2,1)S(1)}, u32[]{:S(2)}, u32[]{:S(2)}) %collective-permute-start.3) | collective-permute-done | bytes 196640 | tf_op jit(solution)/shard_map/ppermute | solution.py:404
  53.3 0.3 shard_map.99
  53.7 30.2 %all_to_all.15.received = bf16[64,4,4,128]{3,2,1,0:T(4,128)(2,1)S(1)} all-to-all(bf16[64,4,4,128]{3,2,1,0:T(4,128)(2,1)S(1)} %shard_map.99), channel_id=1, replica_groups={{0,1,2,3,4,5,6,7,8,9,10,11,12,13,14,15,16,17,18,19,20,21,22,23,24,25,26..., dimensions={0} | all-to-all | bytes 524288 | tf_op jit(solution)/shard_map/all_to_all | solution.py:429
  83.8 0.0 copy-done.9
  83.8 0.4 shard_map.100
  84.3 14.8 %all_to_all.16.received = bf16[32,6,4,128]{3,2,1,0:T(4,128)(2,1)S(1)} all-to-all(bf16[32,6,4,128]{3,2,1,0:T(4,128)(2,1)S(1)} %shard_map.100), channel_id=1, replica_groups=mesh['row'=16,'col'=32] {'col'}, dimensions={0} | all-to-all | bytes 393216 | tf_op jit(solution)/shard_map/all_to_all | solution.py:442
  99.1 0.8 shard_map.101
Async XLA Ops:
  0.0 12.2 %copy-start.3 = (f32[6,64,128]{2,1,0:T(8,128)S(1)}, f32[6,64,128]{2,1,0:T(8,128)}, u32[]{:S(2)}) copy-start(f32[6,64,128]{2,1,0:T(8,128)} %potential.7) | copy-start | bytes 589828
  0.0 12.2 %copy-start.8 = (f32[8]{0:T(128)S(1)}, f32[8]{0:T(128)}, u32[]{:S(2)}) copy-start(f32[8]{0:T(128)} %strength.3) | copy-start | bytes 100
  0.0 12.2 %copy-start.7 = (f32[8,128]{1,0:T(8,128)S(1)}, f32[8,128]{1,0:T(8,128)}, u32[]{:S(2)}) copy-start(f32[8,128]{1,0:T(8,128)} %projector.3) | copy-start | bytes 12292
  0.0 12.2 %copy-start.6 = (s32[8,128]{1,0:T(8,128)S(1)}, s32[8,128]{1,0:T(8,128)}, u32[]{:S(2)}) copy-start(s32[8,128]{1,0:T(8,128)} %points.3) | copy-start | bytes 12292
  2.0 27.8 %all-to-all-start = ((bf16[16,37,4,128]{3,2,1,0:T(4,128)(2,1)}), bf16[16,37,4,128]{3,2,1,0:T(4,128)(2,1)S(1)}, u32[]{:S(2)}, u32[]{:S(2)}) async-start(bf16[16,37,4,128]{3,2,1,0:T(4,128)(2,1)} %shard_map.91), calls=%async_computation | async-start | bytes 1212416 | tf_op jit(solution)/shard_map/all_to_all | solution.py:372
  12.8 13.3 %collective-permute-start = (f32[408,128]{1,0:T(8,128)S(1)}, f32[408,128]{1,0:T(8,128)S(1)}, u32[]{:S(2)}, u32[]{:S(2)}) collective-permute-start(f32[408,128]{1,0:T(8,128)S(1)} %shard_map.92), channel_id=1, source_target_pairs={{0,256},{32,288},{64,320},{96,352},{128,384},{160,416},{192,448},{... | collective-permute-start | bytes 626696 | tf_op jit(solution)/shard_map/ppermute | solution.py:380
  18.7 11.1 %copy-start.4 = (bf16[256,256]{1,0:T(8,128)(2,1)S(1)}, bf16[256,256]{1,0:T(8,128)(2,1)}, u32[]{:S(2)}) copy-start(bf16[256,256]{1,0:T(8,128)(2,1)} %constant.4.clone.along_z) | copy-start | bytes 393220
  18.7 11.1 %copy-start.5 = (bf16[128,128]{1,0:T(8,128)(2,1)S(1)}, bf16[128,128]{1,0:T(8,128)(2,1)}, u32[]{:S(2)}) copy-start(bf16[128,128]{1,0:T(8,128)(2,1)} %constant.5.clone.along_y) | copy-start | bytes 98308
  26.7 1.2 %copy-start = (f32[8,384,128]{2,1,0:T(8,128)}, f32[8,384,128]{2,1,0:T(8,128)S(1)}, u32[]{:S(2)}) copy-start(f32[8,384,128]{2,1,0:T(8,128)S(1)} %get-tuple-element.17.other_dense) | copy-start | bytes 4718596
  29.8 1.4 %copy-start.1 = (f32[8,384,128]{2,1,0:T(8,128)S(1)}, f32[8,384,128]{2,1,0:T(8,128)}, u32[]{:S(2)}) copy-start(f32[8,384,128]{2,1,0:T(8,128)} %copy-done) | copy-start | bytes 4718596
  32.5 6.4 %collective-permute-start.2 = (bf16[2,6,64,128]{3,2,1,0:T(8,128)(2,1)S(1)}, bf16[2,6,64,128]{3,2,1,0:T(8,128)(2,1)S(1)}, u32[]{:S(2)}, u32[]{:S(2)}) collective-permute-start(bf16[2,6,64,128]{3,2,1,0:T(8,128)(2,1)S(1)} %get-tuple-element.21), channel_id=1, source_target_pairs={{32,0},{64,32},{96,64},{128,96},{160,128},{192,160},{224,192},{0,2... | collective-permute-start | bytes 589832 | tf_op jit(solution)/shard_map/ppermute | solution.py:405
  35.2 7.6 %collective-permute-start.1 = (bf16[2,6,64,128]{3,2,1,0:T(8,128)(2,1)S(1)}, bf16[2,6,64,128]{3,2,1,0:T(8,128)(2,1)S(1)}, u32[]{:S(2)}, u32[]{:S(2)}) collective-permute-start(bf16[2,6,64,128]{3,2,1,0:T(8,128)(2,1)S(1)} %get-tuple-element.21), channel_id=1, source_target_pairs={{0,32},{32,64},{64,96},{96,128},{128,160},{160,192},{192,224},{224... | collective-permute-start | bytes 589832 | tf_op jit(solution)/shard_map/ppermute | solution.py:404
  37.8 10.5 %copy-start.2 = (f32[8,384,128]{2,1,0:T(8,128)S(1)}, f32[8,384,128]{2,1,0:T(8,128)}, u32[]{:S(2)}) copy-start(f32[8,384,128]{2,1,0:T(8,128)} %copy-done) | copy-start | bytes 4718596
  43.0 6.4 %collective-permute-start.4 = (bf16[2,6,64,128]{3,2,1,0:T(8,128)(2,1)S(1)}, bf16[2,6,64,128]{3,2,1,0:T(8,128)(2,1)S(1)}, u32[]{:S(2)}, u32[]{:S(2)}) collective-permute-start(bf16[2,6,64,128]{3,2,1,0:T(8,128)(2,1)S(1)} %get-tuple-element.23), channel_id=1, source_target_pairs={{32,0},{64,32},{96,64},{128,96},{160,128},{192,160},{224,192},{0,2... | collective-permute-start | bytes 589832 | tf_op jit(solution)/shard_map/ppermute | solution.py:405
  45.7 7.6 %collective-permute-start.3 = (bf16[2,6,64,128]{3,2,1,0:T(8,128)(2,1)S(1)}, bf16[2,6,64,128]{3,2,1,0:T(8,128)(2,1)S(1)}, u32[]{:S(2)}, u32[]{:S(2)}) collective-permute-start(bf16[2,6,64,128]{3,2,1,0:T(8,128)(2,1)S(1)} %get-tuple-element.23), channel_id=1, source_target_pairs={{0,32},{32,64},{64,96},{96,128},{128,160},{160,192},{192,224},{224... | collective-permute-start | bytes 589832 | tf_op jit(solution)/shard_map/ppermute | solution.py:404
  49.3 34.5 %copy-start.9 = (s32[64]{0:T(128)S(1)}, s32[64]{0:T(128)}, u32[]{:S(2)}) copy-start(s32[64]{0:T(128)} %param.15) | copy-start | bytes 772

commit v5 on v4

--- a/solution.py
+++ b/solution.py
@@ -147,10 +147,10 @@
         gains[atom : atom + 1, :] = jnp.full((1, GZ), strength[atom], F32)
 
 
-def project_other_kernel(given, dense, gains):
+def other_projectors(given, dense):
     points = given[SLAB_ROWS : SLAB_ROWS + 8, :].astype(jnp.int32)
     densify(points, given[SLAB_ROWS + 8 : SLAB_ROWS + 16, :], dense)
-    gains[...] = given[SLAB_ROWS + 16 : SLAB_ROWS + 24, :]
+    return given.at[SLAB_ROWS + 16 : SLAB_ROWS + 24]
 
 
 def apply(planes, reach, scale, potentials, denses, gains, along_z, along_y, wide_z, summed_z, emit):
@@ -217,9 +217,10 @@
 
 
 def first_kernel(
-    received, potential, other, dense, gains, other_dense, other_gains, along_z, along_y,
-    start_out, next_out, sent_out, panel_out, slabs, wide_z, summed_z,
+    received, potential, other, dense, gains, along_z, along_y,
+    start_out, next_out, sent_out, panel_out, slabs, other_dense, wide_z, summed_z,
 ):
+    other_gains = other_projectors(other, other_dense)
     panel = jnp.zeros((YPART, GZ), F32)
     for source in range(ROWS):
         for slab in range(2):
@@ -244,9 +245,11 @@
 
 
 def inside_kernel(
-    current, previous, potential, other, dense, gains, other_dense, other_gains, along_z, along_y,
-    out, wide_z, summed_z,
+    current, previous, potential, other, dense, gains, along_z, along_y,
+    out, other_dense, wide_z, summed_z,
 ):
+    other_gains = other_projectors(other, other_dense)
+
     def emit(slab, p, value):
         out[slab, p] = value - previous[slab, p]
 
@@ -353,6 +356,7 @@
     along_z, along_y = stencil_matrices()
     smem = pl.BlockSpec(memory_space=pltpu.SMEM)
     work = [
+        pltpu.VMEM((ATOM_DEV, SLAB_ROWS, GZ), F32),
         pltpu.VMEM((2 * SLAB_ROWS, 2 * GZ), BF16),
         pltpu.VMEM((2 * SLAB_ROWS, 2 * GZ), F32),
     ]
@@ -385,20 +389,12 @@
         flops=1_000_000_000,
         bytes_accessed=1_600_000,
     )(proj_points, projector, strength)
-    other_dense, other_gains = call(
-        project_other_kernel,
-        dense_gains,
-        specs=[VMEM],
-        flops=1_000_000_000,
-        bytes_accessed=1_600_000,
-    )(other)
-
-    fixed = (potential, other, dense, gains, other_dense, other_gains, along_z, along_y)
+    fixed = (potential, other, dense, gains, along_z, along_y)
     previous, current, sent, panel = call(
         first_kernel,
         (slabs_f32, slabs_f32, slabs_bf16, shape((8, GZ), F32)),
         scratch=[pltpu.VMEM((2, WIDE, GY, GZ), F32)] + work,
-        specs=[VMEM] * 9,
+        specs=[VMEM] * 7,
     )(regrouped, *fixed)
     for step in range(2):
         below = lax.ppermute(sent, "row", around)
@@ -407,7 +403,7 @@
             inside_kernel,
             slabs_f32,
             scratch=work,
-            specs=[VMEM] * 10,
+            specs=[VMEM] * 8,
             flops=2_000_000_000,
             bytes_accessed=3_000_000,
         )(current, previous, *fixed)

time: 100 us -> 97.7 us (0.977)
  local copies, waits for them, and re-layouts: 2.61 us -> 0.04 us
  blocking collectives: 45 us -> 43.7 us
    unnamed x20 -> x14, local copies, waits for them, and re-layouts: 2.61 us -> 0.04 us
    all_to_all x1, waiting for transfers between devices: 1.95 us -> 3.8 us  [per_device(): lax.all_to_all(packed, 'row', split_axis=0, concat_axis=0, tiled=True)]
    all_to_all x1, blocking collectives: 30.2 us -> 28.9 us  [per_device(): lax.all_to_all(layered, ('row', 'col'), split_axis=0, concat_axis=0, tile...]
    pallas_call x3 -> x2, Pallas kernels: 2.55 us -> 2.6 us  [per_device(): call(inside_kernel, slabs_f32, scratch=work, specs=[VMEM] * 8, flops=2000...]
  transfers between devices with their start and end apart: 6 -> 6, of which waited for: 6 -> 4; matrix products, arithmetic and copies ran while one was open for 0% -> 0% of each run, Pallas kernels for 4% -> 4%
where the time goes in v5:
time: 97.7 us; the launch traced here: 97.3 us
  blocking collectives  43.7 us (45%)
  starting transfers between devices  25.7 us (26%)
  waiting for transfers between devices  17.9 us (18%)
  Pallas kernels  9.71 us (10%)
    all_to_all x1, blocking collectives, per_device(): lax.all_to_all(layered, ('row', 'col'), split_axis=0, concat_axis=0, tile...  28.9 us
    all_to_all x1, blocking collectives, per_device(): lax.all_to_all(turned, 'col', split_axis=0, concat_axis=0, tiled=True)  14.8 us
    all_to_all x1, starting transfers between devices, per_device(): lax.all_to_all(packed, 'row', split_axis=0, concat_axis=0, tiled=True)  10.2 us
    ppermute x1, waiting for transfers between devices, per_device(): other = lax.ppermute(given, 'row', [(i, i ^ HALF) for i in range(ROWS)])  7.11 us
    ppermute x2, waiting for transfers between devices, per_device(): below = lax.ppermute(sent, 'row', around)  7 us
    ppermute x2, starting transfers between devices, per_device(): below = lax.ppermute(sent, 'row', around)  5.6 us
    ppermute x2, starting transfers between devices, per_device(): above = lax.ppermute(sent, 'row', [(d, s) for s, d in around])  4.97 us
    ppermute x1, starting transfers between devices, per_device(): other = lax.ppermute(given, 'row', [(i, i ^ HALF) for i in range(ROWS)])  4.91 us
  transfers between devices with their start and end apart: 6, of which 4 were waited for; matrix products, arithmetic and copies ran while one was open for 0% of the time, Pallas kernels for 4%

profile of v5, /device:TPU:1, one launch (start us, length us, event | category | flops | bytes accessed | tf_op | source)
XLA Modules:
  0.0 97.3 jit_solution(10465933894421142084)
XLA Ops:
  0.0 0.0 copy-start
  0.0 0.0 copy-start.5
  0.0 0.0 copy-start.4
  0.0 0.0 copy-start.3
  0.0 2.0 %shard_map.91 = bf16[16,37,4,128]{3,2,1,0:T(4,128)(2,1)} custom-call(bf16[2,96,4,128]{3,2,1,0:T(4,128)(2,1)} %orbitals.1, bf16[2,4]{1,0:T(2,128)(2,1)} %bitcast.4), custom_call_target="tpu_custom_call" | custom-call | tf_op jit(solution)/shard_map/pallas_call | solution.py:365
  2.0 10.2 %all-to-all-start = ((bf16[16,37,4,128]{3,2,1,0:T(4,128)(2,1)}), bf16[16,37,4,128]{3,2,1,0:T(4,128)(2,1)S(1)}, u32[]{:S(2)}, u32[]{:S(2)}) async-start(bf16[16,37,4,128]{3,2,1,0:T(4,128)(2,1)} %shard_map.91), calls=%async_computation | async-start | bytes 1212416 | tf_op jit(solution)/shard_map/all_to_all | solution.py:376
  12.2 0.0 copy-done
  12.2 0.0 copy-done.5
  12.2 0.0 copy-done.4
  12.2 0.0 copy-done.3
  12.3 0.6 shard_map.92
  12.8 0.0 copy-start.1
  12.8 0.0 copy-start.2
  12.8 4.9 %collective-permute-start = (f32[408,128]{1,0:T(8,128)S(1)}, f32[408,128]{1,0:T(8,128)S(1)}, u32[]{:S(2)}, u32[]{:S(2)}) collective-permute-start(f32[408,128]{1,0:T(8,128)S(1)} %shard_map.92), channel_id=1, source_target_pairs={{0,256},{32,288},{64,320},{96,352},{128,384},{160,416},{192,448},{... | collective-permute-start | bytes 626696 | tf_op jit(solution)/shard_map/ppermute | solution.py:384
  17.8 1.1 %shard_map.93 = (f32[8,384,128]{2,1,0:T(8,128)S(1)}, f32[8,128]{1,0:T(8,128)S(1)}) custom-call(s32[8,128]{1,0:T(8,128)S(1)} %copy-done.3, f32[8,128]{1,0:T(8,128)S(1)} %copy-done.4, f32[8]{0:T(128)S(1)} %copy-done.5), custom_call_target="tpu_custom_call" | custom-call | flops 1000000000 | bytes 1600000 | tf_op jit(solution)/shard_map/pallas_call | solution.py:385
  18.9 7.1 %collective-permute-done.other = f32[408,128]{1,0:T(8,128)S(1)} collective-permute-done((f32[408,128]{1,0:T(8,128)S(1)}, f32[408,128]{1,0:T(8,128)S(1)}, u32[]{:S(2)}, u32[]{:S(2)}) %collective-permute-start) | collective-permute-done | bytes 208928 | tf_op jit(solution)/shard_map/ppermute | solution.py:384
  26.0 3.8 %all-to-all-done.received = bf16[16,37,4,128]{3,2,1,0:T(4,128)(2,1)S(1)} async-done(((bf16[16,37,4,128]{3,2,1,0:T(4,128)(2,1)}), bf16[16,37,4,128]{3,2,1,0:T(4,128)(2,1)S(1)}, u32[]{:S(2)}, u32[]{:S(2)}) %all-to-all-start) | async-done | bytes 606240 | tf_op jit(solution)/shard_map/all_to_all | solution.py:376
  29.8 0.0 copy-done.1
  29.8 0.0 copy-done.2
  29.8 1.7 %shard_map.94 = (f32[2,6,64,128]{3,2,1,0:T(8,128)S(1)}, f32[2,6,64,128]{3,2,1,0:T(8,128)S(1)}, bf16[2,6,64,128]{3,2,1,0:T(8,128)(2,1)S(1)}, f32[8,128]{1,0:T(8,128)S(1)}) custom-call(bf16[16,37,4,128]{3,2,1,0:T(4,128)(2,1)S(1)} %all-to-all-done.received, f32[6,64,128]{2,1,0:T(8,128)S(1)} %copy-done, f32[408,128]{1,0:T(8,128)S(1)} %collective-permute-done.other, ...), custom_call_target="tpu_custom_call" | custom-call | tf_op jit(solution)/shard_map/pallas_call | solution.py:393
  31.5 2.6 %collective-permute-start.2 = (bf16[2,6,64,128]{3,2,1,0:T(8,128)(2,1)S(1)}, bf16[2,6,64,128]{3,2,1,0:T(8,128)(2,1)S(1)}, u32[]{:S(2)}, u32[]{:S(2)}) collective-permute-start(bf16[2,6,64,128]{3,2,1,0:T(8,128)(2,1)S(1)} %get-tuple-element.17), channel_id=1, source_target_pairs={{32,0},{64,32},{96,64},{128,96},{160,128},{192,160},{224,192},{0,2... | collective-permute-start | bytes 589832 | tf_op jit(solution)/shard_map/ppermute | solution.py:401
  34.1 2.7 %collective-permute-start.1 = (bf16[2,6,64,128]{3,2,1,0:T(8,128)(2,1)S(1)}, bf16[2,6,64,128]{3,2,1,0:T(8,128)(2,1)S(1)}, u32[]{:S(2)}, u32[]{:S(2)}) collective-permute-start(bf16[2,6,64,128]{3,2,1,0:T(8,128)(2,1)S(1)} %get-tuple-element.17), channel_id=1, source_target_pairs={{0,32},{32,64},{64,96},{96,128},{128,160},{160,192},{192,224},{224... | collective-permute-start | bytes 589832 | tf_op jit(solution)/shard_map/ppermute | solution.py:400
  36.8 1.3 %shard_map.95.partial = f32[2,6,64,128]{3,2,1,0:T(8,128)S(1)} custom-call(f32[2,6,64,128]{3,2,1,0:T(8,128)S(1)} %get-tuple-element.15.current.previous, f32[2,6,64,128]{3,2,1,0:T(8,128)S(1)} %get-tuple-element.16.previous, f32[6,64,128]{2,1,0:T(8,128)S(1)} %copy-done, f32[408,128]{1,0:T(8,128)S(1)} %collective-permute-done.other, ...), custom_call_target="tpu_custom_call" | custom-call | flops 2000000000 | bytes 3000000 | tf_op jit(solution)/shard_map/pallas_call | solution.py:402
  38.1 0.0 collective-permute-done.2.above
  38.1 3.6 %collective-permute-done.1.below = bf16[2,6,64,128]{3,2,1,0:T(8,128)(2,1)S(1)} collective-permute-done((bf16[2,6,64,128]{3,2,1,0:T(8,128)(2,1)S(1)}, bf16[2,6,64,128]{3,2,1,0:T(8,128)(2,1)S(1)}, u32[]{:S(2)}, u32[]{:S(2)}) %collective-permute-start.1) | collective-permute-done | bytes 196640 | tf_op jit(solution)/shard_map/ppermute | solution.py:400
  41.8 0.2 shard_map.96
  42.0 2.4 %collective-permute-start.4 = (bf16[2,6,64,128]{3,2,1,0:T(8,128)(2,1)S(1)}, bf16[2,6,64,128]{3,2,1,0:T(8,128)(2,1)S(1)}, u32[]{:S(2)}, u32[]{:S(2)}) collective-permute-start(bf16[2,6,64,128]{3,2,1,0:T(8,128)(2,1)S(1)} %get-tuple-element.19), channel_id=1, source_target_pairs={{32,0},{64,32},{96,64},{128,96},{160,128},{192,160},{224,192},{0,2... | collective-permute-start | bytes 589832 | tf_op jit(solution)/shard_map/ppermute | solution.py:401
  44.4 2.9 %collective-permute-start.3 = (bf16[2,6,64,128]{3,2,1,0:T(8,128)(2,1)S(1)}, bf16[2,6,64,128]{3,2,1,0:T(8,128)(2,1)S(1)}, u32[]{:S(2)}, u32[]{:S(2)}) collective-permute-start(bf16[2,6,64,128]{3,2,1,0:T(8,128)(2,1)S(1)} %get-tuple-element.19), channel_id=1, source_target_pairs={{0,32},{32,64},{64,96},{96,128},{128,160},{160,192},{192,224},{224... | collective-permute-start | bytes 589832 | tf_op jit(solution)/shard_map/ppermute | solution.py:400
  47.3 1.3 %shard_map.97.partial = f32[2,6,64,128]{3,2,1,0:T(8,128)S(1)} custom-call(f32[2,6,64,128]{3,2,1,0:T(8,128)S(1)} %get-tuple-element.18.current, f32[2,6,64,128]{3,2,1,0:T(8,128)S(1)} %get-tuple-element.15.current.previous, f32[6,64,128]{2,1,0:T(8,128)S(1)} %copy-done, f32[408,128]{1,0:T(8,128)S(1)} %collective-permute-done.other, ...), custom_call_target="tpu_custom_call" | custom-call | flops 2000000000 | bytes 3000000 | tf_op jit(solution)/shard_map/pallas_call | solution.py:402
  48.6 0.0 copy-start.6
  48.6 0.0 collective-permute-done.4.above
  48.6 3.4 %collective-permute-done.3.below = bf16[2,6,64,128]{3,2,1,0:T(8,128)(2,1)S(1)} collective-permute-done((bf16[2,6,64,128]{3,2,1,0:T(8,128)(2,1)S(1)}, bf16[2,6,64,128]{3,2,1,0:T(8,128)(2,1)S(1)}, u32[]{:S(2)}, u32[]{:S(2)}) %collective-permute-start.3) | collective-permute-done | bytes 196640 | tf_op jit(solution)/shard_map/ppermute | solution.py:400
  52.0 0.3 shard_map.98
  52.3 28.9 %all_to_all.15.received = bf16[64,4,4,128]{3,2,1,0:T(4,128)(2,1)S(1)} all-to-all(bf16[64,4,4,128]{3,2,1,0:T(4,128)(2,1)S(1)} %shard_map.98), channel_id=1, replica_groups={{0,1,2,3,4,5,6,7,8,9,10,11,12,13,14,15,16,17,18,19,20,21,22,23,24,25,26..., dimensions={0} | all-to-all | bytes 524288 | tf_op jit(solution)/shard_map/all_to_all | solution.py:425
  81.3 0.0 copy-done.6
  81.3 0.4 shard_map.99
  81.7 14.8 %all_to_all.16.received = bf16[32,6,4,128]{3,2,1,0:T(4,128)(2,1)S(1)} all-to-all(bf16[32,6,4,128]{3,2,1,0:T(4,128)(2,1)S(1)} %shard_map.99), channel_id=1, replica_groups=mesh['row'=16,'col'=32] {'col'}, dimensions={0} | all-to-all | bytes 393216 | tf_op jit(solution)/shard_map/all_to_all | solution.py:438
  96.5 0.8 shard_map.100
Async XLA Ops:
  0.0 12.2 %copy-start = (f32[6,64,128]{2,1,0:T(8,128)S(1)}, f32[6,64,128]{2,1,0:T(8,128)}, u32[]{:S(2)}) copy-start(f32[6,64,128]{2,1,0:T(8,128)} %potential.7) | copy-start | bytes 589828
  0.0 12.2 %copy-start.5 = (f32[8]{0:T(128)S(1)}, f32[8]{0:T(128)}, u32[]{:S(2)}) copy-start(f32[8]{0:T(128)} %strength.3) | copy-start | bytes 100
  0.0 12.2 %copy-start.4 = (f32[8,128]{1,0:T(8,128)S(1)}, f32[8,128]{1,0:T(8,128)}, u32[]{:S(2)}) copy-start(f32[8,128]{1,0:T(8,128)} %projector.3) | copy-start | bytes 12292
  0.0 12.2 %copy-start.3 = (s32[8,128]{1,0:T(8,128)S(1)}, s32[8,128]{1,0:T(8,128)}, u32[]{:S(2)}) copy-start(s32[8,128]{1,0:T(8,128)} %points.3) | copy-start | bytes 12292
  2.0 27.8 %all-to-all-start = ((bf16[16,37,4,128]{3,2,1,0:T(4,128)(2,1)}), bf16[16,37,4,128]{3,2,1,0:T(4,128)(2,1)S(1)}, u32[]{:S(2)}, u32[]{:S(2)}) async-start(bf16[16,37,4,128]{3,2,1,0:T(4,128)(2,1)} %shard_map.91), calls=%async_computation | async-start | bytes 1212416 | tf_op jit(solution)/shard_map/all_to_all | solution.py:376
  12.8 17.0 %copy-start.1 = (bf16[256,256]{1,0:T(8,128)(2,1)S(1)}, bf16[256,256]{1,0:T(8,128)(2,1)}, u32[]{:S(2)}) copy-start(bf16[256,256]{1,0:T(8,128)(2,1)} %constant.4.clone.along_z) | copy-start | bytes 393220
  12.8 17.0 %copy-start.2 = (bf16[128,128]{1,0:T(8,128)(2,1)S(1)}, bf16[128,128]{1,0:T(8,128)(2,1)}, u32[]{:S(2)}) copy-start(bf16[128,128]{1,0:T(8,128)(2,1)} %constant.5.clone.along_y) | copy-start | bytes 98308
  12.8 13.1 %collective-permute-start = (f32[408,128]{1,0:T(8,128)S(1)}, f32[408,128]{1,0:T(8,128)S(1)}, u32[]{:S(2)}, u32[]{:S(2)}) collective-permute-start(f32[408,128]{1,0:T(8,128)S(1)} %shard_map.92), channel_id=1, source_target_pairs={{0,256},{32,288},{64,320},{96,352},{128,384},{160,416},{192,448},{... | collective-permute-start | bytes 626696 | tf_op jit(solution)/shard_map/ppermute | solution.py:384
  31.5 6.6 %collective-permute-start.2 = (bf16[2,6,64,128]{3,2,1,0:T(8,128)(2,1)S(1)}, bf16[2,6,64,128]{3,2,1,0:T(8,128)(2,1)S(1)}, u32[]{:S(2)}, u32[]{:S(2)}) collective-permute-start(bf16[2,6,64,128]{3,2,1,0:T(8,128)(2,1)S(1)} %get-tuple-element.17), channel_id=1, source_target_pairs={{32,0},{64,32},{96,64},{128,96},{160,128},{192,160},{224,192},{0,2... | collective-permute-start | bytes 589832 | tf_op jit(solution)/shard_map/ppermute | solution.py:401
  34.1 7.6 %collective-permute-start.1 = (bf16[2,6,64,128]{3,2,1,0:T(8,128)(2,1)S(1)}, bf16[2,6,64,128]{3,2,1,0:T(8,128)(2,1)S(1)}, u32[]{:S(2)}, u32[]{:S(2)}) collective-permute-start(bf16[2,6,64,128]{3,2,1,0:T(8,128)(2,1)S(1)} %get-tuple-element.17), channel_id=1, source_target_pairs={{0,32},{32,64},{64,96},{96,128},{128,160},{160,192},{192,224},{224... | collective-permute-start | bytes 589832 | tf_op jit(solution)/shard_map/ppermute | solution.py:400
  42.0 6.6 %collective-permute-start.4 = (bf16[2,6,64,128]{3,2,1,0:T(8,128)(2,1)S(1)}, bf16[2,6,64,128]{3,2,1,0:T(8,128)(2,1)S(1)}, u32[]{:S(2)}, u32[]{:S(2)}) collective-permute-start(bf16[2,6,64,128]{3,2,1,0:T(8,128)(2,1)S(1)} %get-tuple-element.19), channel_id=1, source_target_pairs={{32,0},{64,32},{96,64},{128,96},{160,128},{192,160},{224,192},{0,2... | collective-permute-start | bytes 589832 | tf_op jit(solution)/shard_map/ppermute | solution.py:401
  44.4 7.6 %collective-permute-start.3 = (bf16[2,6,64,128]{3,2,1,0:T(8,128)(2,1)S(1)}, bf16[2,6,64,128]{3,2,1,0:T(8,128)(2,1)S(1)}, u32[]{:S(2)}, u32[]{:S(2)}) collective-permute-start(bf16[2,6,64,128]{3,2,1,0:T(8,128)(2,1)S(1)} %get-tuple-element.19), channel_id=1, source_target_pairs={{0,32},{32,64},{64,96},{96,128},{128,160},{160,192},{192,224},{224... | collective-permute-start | bytes 589832 | tf_op jit(solution)/shard_map/ppermute | solution.py:400
  48.6 32.6 %copy-start.6 = (s32[64]{0:T(128)S(1)}, s32[64]{0:T(128)}, u32[]{:S(2)}) copy-start(s32[64]{0:T(128)} %param.15) | copy-start | bytes 772

commit v6 on v5

--- a/solution.py
+++ b/solution.py
@@ -39,6 +39,7 @@
 DIAGONAL = -0.5 * 3.0 * STENCIL[0] - CENTER
 
 VMEM = pl.BlockSpec(memory_space=pltpu.VMEM)
+ANY = pl.BlockSpec(memory_space=pl.ANY)
 MIB = 1024 * 1024
 
 
@@ -61,12 +62,14 @@
     return jnp.asarray(along_z), jnp.asarray(along_y)
 
 
-def call(kernel, outs, scratch=(), flops=0, bytes_accessed=0, specs=None, vmem=12 * MIB):
+def call(
+    kernel, outs, scratch=(), flops=0, bytes_accessed=0, specs=None, vmem=12 * MIB, out_spec=VMEM
+):
     return pl.pallas_call(
         kernel,
         out_shape=outs,
         in_specs=specs,
-        out_specs=jax.tree.map(lambda _: VMEM, outs),
+        out_specs=jax.tree.map(lambda _: out_spec, outs),
         scratch_shapes=list(scratch),
         compiler_params=pltpu.CompilerParams(vmem_limit_bytes=vmem),
         cost_estimate=pl.CostEstimate(
@@ -75,14 +78,14 @@
     )
 
 
-def pack_kernel(orbitals, panel, out, states, columns, sems):
+def pack_kernel(orbitals, panel, out, states, columns, chunks, sems, out_sems):
     copies = [
         pltpu.make_async_copy(source, target, sems.at[i])
         for i, (source, target) in enumerate(
             [
-                (panel, columns),
                 (orbitals.at[0], states.at[0]),
                 (orbitals.at[1], states.at[1]),
+                (panel, columns),
             ]
         )
     ]
@@ -90,23 +93,30 @@
         copy.start()
     row = lax.axis_index("row")
     place = lax.broadcasted_iota(jnp.int32, (2, GZ), 1)
-    copies[0].wait()
+    copies[2].wait()
     values = columns[...].astype(F32)
     tile = jnp.zeros((2, GZ), F32)
     for k in range(YPART):
         tile = jnp.where(place == YPART * row + k, values[:, k : k + 1], tile)
     tile = jnp.concatenate([tile, jnp.zeros((YPART - 2, GZ), F32)], axis=0).astype(BF16)
-    for state in range(2):
-        copies[1 + state].wait()
-        for target in range(HALF * state, HALF * state + HALF):
-            for index, slab in enumerate((target, target ^ HALF)):
-                begin = (SLAB * slab - SLAB) % GX
-                base = index * WIDE
-                head = min(WIDE, GX - begin)
-                out[target, base : base + head] = states[state, begin : begin + head]
-                if head < WIDE:
-                    out[target, base + head : base + WIDE] = states[state, : WIDE - head]
-            out[target, 2 * WIDE] = tile
+    for target in range(ROWS):
+        state = target // HALF
+        if target % HALF == 0:
+            copies[state].wait()
+        for index, slab in enumerate((target, target ^ HALF)):
+            begin = (SLAB * slab - SLAB) % GX
+            base = index * WIDE
+            head = min(WIDE, GX - begin)
+            chunks[target, base : base + head] = states[state, begin : begin + head]
+            if head < WIDE:
+                chunks[target, base + head : base + WIDE] = states[state, : WIDE - head]
+        chunks[target, 2 * WIDE] = tile
+        copies.append(
+            pltpu.make_async_copy(chunks.at[target], out.at[target], out_sems.at[target])
+        )
+        copies[-1].start()
+    for copy in copies[3:]:
+        copy.wait()
 
 
 def other_kernel(potential, points, projector, strength, out):
@@ -340,12 +350,24 @@
                 ].astype(BF16)
 
 
-def place_kernel(received, out):
+def place_kernel(received, out, whole, sems):
+    copies = []
     for col in range(COLS):
         for state in range(2):
             for k in range(PIECE):
                 at = 4 * (PIECE * col + k)
-                out[state, at : at + 4, :] = received[col, state * PIECE + k].astype(F32)
+                whole[state, at : at + 4, :] = received[col, state * PIECE + k].astype(F32)
+        if col % 8 == 7:
+            rows = pl.ds(4 * PIECE * (col - 7), 32 * PIECE)
+            for state in range(2):
+                copies.append(
+                    pltpu.make_async_copy(
+                        whole.at[state, rows], out.at[state, rows], sems.at[len(copies)]
+                    )
+                )
+                copies[-1].start()
+    for copy in copies:
+        copy.wait()
 
 
 def per_device(orbitals, potential, proj_points, projector, strength, ritz_panel, panel_rows):
@@ -368,10 +390,13 @@
         scratch=[
             pltpu.VMEM((2, GX, YPART, GZ), BF16),
             pltpu.VMEM((2, YPART), BF16),
+            pltpu.VMEM((ROWS, SENT, YPART, GZ), BF16),
             pltpu.SemaphoreType.DMA((3,)),
+            pltpu.SemaphoreType.DMA((ROWS,)),
         ],
-        specs=[pl.BlockSpec(memory_space=pl.ANY)] * 2,
+        specs=[ANY] * 2,
         vmem=60 * MIB,
+        out_spec=ANY,
     )(orbitals, ritz_panel.T)
     regrouped = lax.all_to_all(packed, "row", split_axis=0, concat_axis=0, tiled=True)
     given = call(
@@ -436,7 +461,13 @@
         specs=[VMEM] * 2,
     )(columns, panel_rows.reshape(1, -1))
     result = lax.all_to_all(turned, "col", split_axis=0, concat_axis=0, tiled=True)
-    whole = call(place_kernel, shape((2, SLAB_ROWS, GZ), F32), specs=[VMEM])(result)
+    whole = call(
+        place_kernel,
+        shape((2, SLAB_ROWS, GZ), F32),
+        scratch=[pltpu.VMEM((2, SLAB_ROWS, GZ), F32), pltpu.SemaphoreType.DMA((COLS // 4,))],
+        specs=[VMEM],
+        out_spec=ANY,
+    )(result)
     return whole.reshape(2, SLAB, GY, GZ)
 
 

time: 97.7 us -> 97.7 us (level)
  no operation moved by 1% of the time
where the time goes in v6:
time: 97.7 us; the launch traced here: 97.3 us
  blocking collectives  43.7 us (45%)
  starting transfers between devices  25.7 us (26%)
  waiting for transfers between devices  17.9 us (18%)
  Pallas kernels  9.71 us (10%)
    all_to_all x1, blocking collectives, per_device(): lax.all_to_all(layered, ('row', 'col'), split_axis=0, concat_axis=0, tile...  28.9 us
    all_to_all x1, blocking collectives, per_device(): lax.all_to_all(turned, 'col', split_axis=0, concat_axis=0, tiled=True)  14.8 us
    all_to_all x1, starting transfers between devices, per_device(): lax.all_to_all(packed, 'row', split_axis=0, concat_axis=0, tiled=True)  10.2 us
    ppermute x1, waiting for transfers between devices, per_device(): other = lax.ppermute(given, 'row', [(i, i ^ HALF) for i in range(ROWS)])  7.11 us
    ppermute x2, waiting for transfers between devices, per_device(): below = lax.ppermute(sent, 'row', around)  7.01 us
    ppermute x2, starting transfers between devices, per_device(): below = lax.ppermute(sent, 'row', around)  5.59 us
    ppermute x2, starting transfers between devices, per_device(): above = lax.ppermute(sent, 'row', [(d, s) for s, d in around])  4.97 us
    ppermute x1, starting transfers between devices, per_device(): other = lax.ppermute(given, 'row', [(i, i ^ HALF) for i in range(ROWS)])  4.91 us
  transfers between devices with their start and end apart: 6, of which 4 were waited for; matrix products, arithmetic and copies ran while one was open for 0% of the time, Pallas kernels for 4%

profile of v6, /device:TPU:1, one launch (start us, length us, event | category | flops | bytes accessed | tf_op | source)
XLA Modules:
  0.0 97.3 jit_solution(722366557728957602)
XLA Ops:
  0.0 0.0 copy-start
  0.0 0.0 copy-start.5
  0.0 0.0 copy-start.4
  0.0 0.0 copy-start.3
  0.0 1.9 %shard_map.91 = bf16[16,37,4,128]{3,2,1,0:T(4,128)(2,1)} custom-call(bf16[2,96,4,128]{3,2,1,0:T(4,128)(2,1)} %orbitals.1, bf16[2,4]{1,0:T(2,128)(2,1)} %bitcast.4), custom_call_target="tpu_custom_call" | custom-call | tf_op jit(solution)/shard_map/pallas_call | solution.py:387
  2.0 10.2 %all-to-all-start = ((bf16[16,37,4,128]{3,2,1,0:T(4,128)(2,1)}), bf16[16,37,4,128]{3,2,1,0:T(4,128)(2,1)S(1)}, u32[]{:S(2)}, u32[]{:S(2)}) async-start(bf16[16,37,4,128]{3,2,1,0:T(4,128)(2,1)} %shard_map.91), calls=%async_computation | async-start | bytes 1212416 | tf_op jit(solution)/shard_map/all_to_all | solution.py:401
  12.2 0.0 copy-done
  12.2 0.0 copy-done.5
  12.2 0.0 copy-done.4
  12.2 0.0 copy-done.3
  12.2 0.6 shard_map.92
  12.8 0.0 copy-start.1
  12.8 0.0 copy-start.2
  12.8 4.9 %collective-permute-start = (f32[408,128]{1,0:T(8,128)S(1)}, f32[408,128]{1,0:T(8,128)S(1)}, u32[]{:S(2)}, u32[]{:S(2)}) collective-permute-start(f32[408,128]{1,0:T(8,128)S(1)} %shard_map.92), channel_id=1, source_target_pairs={{0,256},{32,288},{64,320},{96,352},{128,384},{160,416},{192,448},{... | collective-permute-start | bytes 626696 | tf_op jit(solution)/shard_map/ppermute | solution.py:409
  17.8 1.1 %shard_map.93 = (f32[8,384,128]{2,1,0:T(8,128)S(1)}, f32[8,128]{1,0:T(8,128)S(1)}) custom-call(s32[8,128]{1,0:T(8,128)S(1)} %copy-done.3, f32[8,128]{1,0:T(8,128)S(1)} %copy-done.4, f32[8]{0:T(128)S(1)} %copy-done.5), custom_call_target="tpu_custom_call" | custom-call | flops 1000000000 | bytes 1600000 | tf_op jit(solution)/shard_map/pallas_call | solution.py:410
  18.9 7.1 %collective-permute-done.other = f32[408,128]{1,0:T(8,128)S(1)} collective-permute-done((f32[408,128]{1,0:T(8,128)S(1)}, f32[408,128]{1,0:T(8,128)S(1)}, u32[]{:S(2)}, u32[]{:S(2)}) %collective-permute-start) | collective-permute-done | bytes 208928 | tf_op jit(solution)/shard_map/ppermute | solution.py:409
  26.0 3.8 %all-to-all-done.received = bf16[16,37,4,128]{3,2,1,0:T(4,128)(2,1)S(1)} async-done(((bf16[16,37,4,128]{3,2,1,0:T(4,128)(2,1)}), bf16[16,37,4,128]{3,2,1,0:T(4,128)(2,1)S(1)}, u32[]{:S(2)}, u32[]{:S(2)}) %all-to-all-start) | async-done | bytes 606240 | tf_op jit(solution)/shard_map/all_to_all | solution.py:401
  29.8 0.0 copy-done.1
  29.8 0.0 copy-done.2
  29.8 1.7 %shard_map.94 = (f32[2,6,64,128]{3,2,1,0:T(8,128)S(1)}, f32[2,6,64,128]{3,2,1,0:T(8,128)S(1)}, bf16[2,6,64,128]{3,2,1,0:T(8,128)(2,1)S(1)}, f32[8,128]{1,0:T(8,128)S(1)}) custom-call(bf16[16,37,4,128]{3,2,1,0:T(4,128)(2,1)S(1)} %all-to-all-done.received, f32[6,64,128]{2,1,0:T(8,128)S(1)} %copy-done, f32[408,128]{1,0:T(8,128)S(1)} %collective-permute-done.other, ...), custom_call_target="tpu_custom_call" | custom-call | tf_op jit(solution)/shard_map/pallas_call | solution.py:418
  31.5 2.6 %collective-permute-start.2 = (bf16[2,6,64,128]{3,2,1,0:T(8,128)(2,1)S(1)}, bf16[2,6,64,128]{3,2,1,0:T(8,128)(2,1)S(1)}, u32[]{:S(2)}, u32[]{:S(2)}) collective-permute-start(bf16[2,6,64,128]{3,2,1,0:T(8,128)(2,1)S(1)} %get-tuple-element.17), channel_id=1, source_target_pairs={{32,0},{64,32},{96,64},{128,96},{160,128},{192,160},{224,192},{0,2... | collective-permute-start | bytes 589832 | tf_op jit(solution)/shard_map/ppermute | solution.py:426
  34.1 2.7 %collective-permute-start.1 = (bf16[2,6,64,128]{3,2,1,0:T(8,128)(2,1)S(1)}, bf16[2,6,64,128]{3,2,1,0:T(8,128)(2,1)S(1)}, u32[]{:S(2)}, u32[]{:S(2)}) collective-permute-start(bf16[2,6,64,128]{3,2,1,0:T(8,128)(2,1)S(1)} %get-tuple-element.17), channel_id=1, source_target_pairs={{0,32},{32,64},{64,96},{96,128},{128,160},{160,192},{192,224},{224... | collective-permute-start | bytes 589832 | tf_op jit(solution)/shard_map/ppermute | solution.py:425
  36.8 1.3 %shard_map.95.partial = f32[2,6,64,128]{3,2,1,0:T(8,128)S(1)} custom-call(f32[2,6,64,128]{3,2,1,0:T(8,128)S(1)} %get-tuple-element.15.current.previous, f32[2,6,64,128]{3,2,1,0:T(8,128)S(1)} %get-tuple-element.16.previous, f32[6,64,128]{2,1,0:T(8,128)S(1)} %copy-done, f32[408,128]{1,0:T(8,128)S(1)} %collective-permute-done.other, ...), custom_call_target="tpu_custom_call" | custom-call | flops 2000000000 | bytes 3000000 | tf_op jit(solution)/shard_map/pallas_call | solution.py:427
  38.1 0.0 collective-permute-done.2.above
  38.1 3.6 %collective-permute-done.1.below = bf16[2,6,64,128]{3,2,1,0:T(8,128)(2,1)S(1)} collective-permute-done((bf16[2,6,64,128]{3,2,1,0:T(8,128)(2,1)S(1)}, bf16[2,6,64,128]{3,2,1,0:T(8,128)(2,1)S(1)}, u32[]{:S(2)}, u32[]{:S(2)}) %collective-permute-start.1) | collective-permute-done | bytes 196640 | tf_op jit(solution)/shard_map/ppermute | solution.py:425
  41.7 0.2 shard_map.96
  42.0 2.4 %collective-permute-start.4 = (bf16[2,6,64,128]{3,2,1,0:T(8,128)(2,1)S(1)}, bf16[2,6,64,128]{3,2,1,0:T(8,128)(2,1)S(1)}, u32[]{:S(2)}, u32[]{:S(2)}) collective-permute-start(bf16[2,6,64,128]{3,2,1,0:T(8,128)(2,1)S(1)} %get-tuple-element.19), channel_id=1, source_target_pairs={{32,0},{64,32},{96,64},{128,96},{160,128},{192,160},{224,192},{0,2... | collective-permute-start | bytes 589832 | tf_op jit(solution)/shard_map/ppermute | solution.py:426
  44.4 2.9 %collective-permute-start.3 = (bf16[2,6,64,128]{3,2,1,0:T(8,128)(2,1)S(1)}, bf16[2,6,64,128]{3,2,1,0:T(8,128)(2,1)S(1)}, u32[]{:S(2)}, u32[]{:S(2)}) collective-permute-start(bf16[2,6,64,128]{3,2,1,0:T(8,128)(2,1)S(1)} %get-tuple-element.19), channel_id=1, source_target_pairs={{0,32},{32,64},{64,96},{96,128},{128,160},{160,192},{192,224},{224... | collective-permute-start | bytes 589832 | tf_op jit(solution)/shard_map/ppermute | solution.py:425
  47.3 1.3 %shard_map.97.partial = f32[2,6,64,128]{3,2,1,0:T(8,128)S(1)} custom-call(f32[2,6,64,128]{3,2,1,0:T(8,128)S(1)} %get-tuple-element.18.current, f32[2,6,64,128]{3,2,1,0:T(8,128)S(1)} %get-tuple-element.15.current.previous, f32[6,64,128]{2,1,0:T(8,128)S(1)} %copy-done, f32[408,128]{1,0:T(8,128)S(1)} %collective-permute-done.other, ...), custom_call_target="tpu_custom_call" | custom-call | flops 2000000000 | bytes 3000000 | tf_op jit(solution)/shard_map/pallas_call | solution.py:427
  48.6 0.0 copy-start.6
  48.6 0.0 collective-permute-done.4.above
  48.6 3.4 %collective-permute-done.3.below = bf16[2,6,64,128]{3,2,1,0:T(8,128)(2,1)S(1)} collective-permute-done((bf16[2,6,64,128]{3,2,1,0:T(8,128)(2,1)S(1)}, bf16[2,6,64,128]{3,2,1,0:T(8,128)(2,1)S(1)}, u32[]{:S(2)}, u32[]{:S(2)}) %collective-permute-start.3) | collective-permute-done | bytes 196640 | tf_op jit(solution)/shard_map/ppermute | solution.py:425
  52.0 0.3 shard_map.98
  52.3 28.9 %all_to_all.15.received = bf16[64,4,4,128]{3,2,1,0:T(4,128)(2,1)S(1)} all-to-all(bf16[64,4,4,128]{3,2,1,0:T(4,128)(2,1)S(1)} %shard_map.98), channel_id=1, replica_groups={{0,1,2,3,4,5,6,7,8,9,10,11,12,13,14,15,16,17,18,19,20,21,22,23,24,25,26..., dimensions={0} | all-to-all | bytes 524288 | tf_op jit(solution)/shard_map/all_to_all | solution.py:450
  81.2 0.0 copy-done.6
  81.2 0.4 shard_map.99
  81.6 14.8 %all_to_all.16.received = bf16[32,6,4,128]{3,2,1,0:T(4,128)(2,1)S(1)} all-to-all(bf16[32,6,4,128]{3,2,1,0:T(4,128)(2,1)S(1)} %shard_map.99), channel_id=1, replica_groups=mesh['row'=16,'col'=32] {'col'}, dimensions={0} | all-to-all | bytes 393216 | tf_op jit(solution)/shard_map/all_to_all | solution.py:463
  96.5 0.8 shard_map.100
Async XLA Ops:
  0.0 12.2 %copy-start = (f32[6,64,128]{2,1,0:T(8,128)S(1)}, f32[6,64,128]{2,1,0:T(8,128)}, u32[]{:S(2)}) copy-start(f32[6,64,128]{2,1,0:T(8,128)} %potential.7) | copy-start | bytes 589828
  0.0 12.2 %copy-start.5 = (f32[8]{0:T(128)S(1)}, f32[8]{0:T(128)}, u32[]{:S(2)}) copy-start(f32[8]{0:T(128)} %strength.3) | copy-start | bytes 100
  0.0 12.2 %copy-start.4 = (f32[8,128]{1,0:T(8,128)S(1)}, f32[8,128]{1,0:T(8,128)}, u32[]{:S(2)}) copy-start(f32[8,128]{1,0:T(8,128)} %projector.3) | copy-start | bytes 12292
  0.0 12.2 %copy-start.3 = (s32[8,128]{1,0:T(8,128)S(1)}, s32[8,128]{1,0:T(8,128)}, u32[]{:S(2)}) copy-start(s32[8,128]{1,0:T(8,128)} %points.3) | copy-start | bytes 12292
  2.0 27.8 %all-to-all-start = ((bf16[16,37,4,128]{3,2,1,0:T(4,128)(2,1)}), bf16[16,37,4,128]{3,2,1,0:T(4,128)(2,1)S(1)}, u32[]{:S(2)}, u32[]{:S(2)}) async-start(bf16[16,37,4,128]{3,2,1,0:T(4,128)(2,1)} %shard_map.91), calls=%async_computation | async-start | bytes 1212416 | tf_op jit(solution)/shard_map/all_to_all | solution.py:401
  12.8 17.0 %copy-start.1 = (bf16[256,256]{1,0:T(8,128)(2,1)S(1)}, bf16[256,256]{1,0:T(8,128)(2,1)}, u32[]{:S(2)}) copy-start(bf16[256,256]{1,0:T(8,128)(2,1)} %constant.4.clone.along_z) | copy-start | bytes 393220
  12.8 17.0 %copy-start.2 = (bf16[128,128]{1,0:T(8,128)(2,1)S(1)}, bf16[128,128]{1,0:T(8,128)(2,1)}, u32[]{:S(2)}) copy-start(bf16[128,128]{1,0:T(8,128)(2,1)} %constant.5.clone.along_y) | copy-start | bytes 98308
  12.8 13.1 %collective-permute-start = (f32[408,128]{1,0:T(8,128)S(1)}, f32[408,128]{1,0:T(8,128)S(1)}, u32[]{:S(2)}, u32[]{:S(2)}) collective-permute-start(f32[408,128]{1,0:T(8,128)S(1)} %shard_map.92), channel_id=1, source_target_pairs={{0,256},{32,288},{64,320},{96,352},{128,384},{160,416},{192,448},{... | collective-permute-start | bytes 626696 | tf_op jit(solution)/shard_map/ppermute | solution.py:409
  31.5 6.6 %collective-permute-start.2 = (bf16[2,6,64,128]{3,2,1,0:T(8,128)(2,1)S(1)}, bf16[2,6,64,128]{3,2,1,0:T(8,128)(2,1)S(1)}, u32[]{:S(2)}, u32[]{:S(2)}) collective-permute-start(bf16[2,6,64,128]{3,2,1,0:T(8,128)(2,1)S(1)} %get-tuple-element.17), channel_id=1, source_target_pairs={{32,0},{64,32},{96,64},{128,96},{160,128},{192,160},{224,192},{0,2... | collective-permute-start | bytes 589832 | tf_op jit(solution)/shard_map/ppermute | solution.py:426
  34.1 7.6 %collective-permute-start.1 = (bf16[2,6,64,128]{3,2,1,0:T(8,128)(2,1)S(1)}, bf16[2,6,64,128]{3,2,1,0:T(8,128)(2,1)S(1)}, u32[]{:S(2)}, u32[]{:S(2)}) collective-permute-start(bf16[2,6,64,128]{3,2,1,0:T(8,128)(2,1)S(1)} %get-tuple-element.17), channel_id=1, source_target_pairs={{0,32},{32,64},{64,96},{96,128},{128,160},{160,192},{192,224},{224... | collective-permute-start | bytes 589832 | tf_op jit(solution)/shard_map/ppermute | solution.py:425
  42.0 6.6 %collective-permute-start.4 = (bf16[2,6,64,128]{3,2,1,0:T(8,128)(2,1)S(1)}, bf16[2,6,64,128]{3,2,1,0:T(8,128)(2,1)S(1)}, u32[]{:S(2)}, u32[]{:S(2)}) collective-permute-start(bf16[2,6,64,128]{3,2,1,0:T(8,128)(2,1)S(1)} %get-tuple-element.19), channel_id=1, source_target_pairs={{32,0},{64,32},{96,64},{128,96},{160,128},{192,160},{224,192},{0,2... | collective-permute-start | bytes 589832 | tf_op jit(solution)/shard_map/ppermute | solution.py:426
  44.4 7.6 %collective-permute-start.3 = (bf16[2,6,64,128]{3,2,1,0:T(8,128)(2,1)S(1)}, bf16[2,6,64,128]{3,2,1,0:T(8,128)(2,1)S(1)}, u32[]{:S(2)}, u32[]{:S(2)}) collective-permute-start(bf16[2,6,64,128]{3,2,1,0:T(8,128)(2,1)S(1)} %get-tuple-element.19), channel_id=1, source_target_pairs={{0,32},{32,64},{64,96},{96,128},{128,160},{160,192},{192,224},{224... | collective-permute-start | bytes 589832 | tf_op jit(solution)/shard_map/ppermute | solution.py:425
  48.6 32.7 %copy-start.6 = (s32[64]{0:T(128)S(1)}, s32[64]{0:T(128)}, u32[]{:S(2)}) copy-start(s32[64]{0:T(128)} %param.15) | copy-start | bytes 772

commit v7 on v5

v7 whole, which is shorter than its diff:
```python
import functools

import jax
import jax.numpy as jnp
import numpy as np
from jax import lax
from jax.experimental import pallas as pl
from jax.experimental.pallas import tpu as pltpu
from jax.sharding import PartitionSpec as P

F32 = jnp.float32
BF16 = jnp.bfloat16

STENCIL = (
    -5369.0 / 1800.0,
    12.0 / 7.0,
    -15.0 / 56.0,
    10.0 / 189.0,
    -1.0 / 112.0,
    2.0 / 1925.0,
    -1.0 / 16632.0,
)
CENTER = 7.0
HALF_WIDTH = 5.0

ROWS, COLS = 16, 32
SLAB, GY, GZ = 6, 64, 128
GX = ROWS * SLAB
YPART = GY // ROWS
PAIR = 2 * SLAB
REACH = 3 * SLAB
WIDE = PAIR + 2 * REACH
SENT = WIDE + 1
ATOM_DEV = 8
SLAB_ROWS = SLAB * GY
PIECE = SLAB_ROWS // COLS // 4
OWN_ROWS = SLAB_ROWS + 3 * ATOM_DEV
NEAR_ROWS = SLAB_ROWS + 6 * ATOM_DEV
SLABS = 6
WINDOW = ((False, 0), (False, 1), (True, 0), (True, 1), (False, 2), (False, 3))

SIDE = tuple(-0.5 * c for c in STENCIL)
DIAGONAL = -0.5 * 3.0 * STENCIL[0] - CENTER

VMEM = pl.BlockSpec(memory_space=pltpu.VMEM)
ANY = pl.BlockSpec(memory_space=pl.ANY)
MIB = 1024 * 1024


def circulant(size):
    whole = np.zeros((size, size), np.float32)
    for offset in range(1, 7):
        for i in range(size):
            whole[i, (i + offset) % size] += SIDE[offset]
            whole[i, (i - offset) % size] += SIDE[offset]
    high = whole.astype(jnp.bfloat16)
    low = (whole - high.astype(np.float32)).astype(jnp.bfloat16)
    return high, low


def stencil_matrices():
    high, low = circulant(GZ)
    along_z = np.block([[high, low], [high, low]])
    high, low = circulant(GY)
    along_y = np.block([[high, high], [low, low]])
    return jnp.asarray(along_z), jnp.asarray(along_y)


def call(kernel, outs, scratch=(), flops=0, bytes_accessed=0, specs=None, vmem=12 * MIB, out_specs=None):
    return pl.pallas_call(
        kernel,
        out_shape=outs,
        in_specs=specs,
        out_specs=out_specs or jax.tree.map(lambda _: VMEM, outs),
        scratch_shapes=list(scratch),
        compiler_params=pltpu.CompilerParams(vmem_limit_bytes=vmem),
        cost_estimate=pl.CostEstimate(
            flops=flops, bytes_accessed=bytes_accessed, transcendentals=0
        ),
    )


def pack_kernel(orbitals, panel, out, states, columns, sems):
    copies = [
        pltpu.make_async_copy(source, target, sems.at[i])
        for i, (source, target) in enumerate(
            [
                (panel, columns),
                (orbitals.at[0], states.at[0]),
                (orbitals.at[1], states.at[1]),
            ]
        )
    ]
    for copy in copies:
        copy.start()
    row = lax.axis_index("row")
    place = lax.broadcasted_iota(jnp.int32, (2, GZ), 1)
    copies[0].wait()
    values = columns[...].astype(F32)
    tile = jnp.zeros((2, GZ), F32)
    for k in range(YPART):
        tile = jnp.where(place == YPART * row + k, values[:, k : k + 1], tile)
    tile = jnp.concatenate([tile, jnp.zeros((YPART - 2, GZ), F32)], axis=0).astype(BF16)
    for state in range(2):
        copies[1 + state].wait()
        for pair in range(ROWS // 2):
            target = 2 * pair + state
            begin = (PAIR * pair - REACH) % GX
            head = min(WIDE, GX - begin)
            out[target, 0:head] = states[state, begin : begin + head]
            if head < WIDE:
                out[target, head:WIDE] = states[state, : WIDE - head]
            out[target, WIDE] = tile


def after_kernel(packed, received, out):
    pass


def three_parts(value):
    high = value.astype(BF16).astype(F32)
    rest = value - high
    middle = rest.astype(BF16).astype(F32)
    return high, middle, rest - middle


def given_kernel(potential, points, projector, strength, own, near):
    for p in range(SLAB):
        own[p * GY : (p + 1) * GY, :] = potential[p]
        near[p * GY : (p + 1) * GY, :] = potential[p].astype(BF16)
    at = points[...]
    gains = jnp.concatenate(
        [jnp.full((1, GZ), strength[atom], F32) for atom in range(ATOM_DEV)], axis=0
    )
    own[SLAB_ROWS : SLAB_ROWS + 8, :] = at.astype(F32)
    own[SLAB_ROWS + 8 : SLAB_ROWS + 16, :] = projector[...]
    own[SLAB_ROWS + 16 : SLAB_ROWS + 24, :] = gains
    lane = lax.broadcasted_iota(jnp.int32, (ATOM_DEV, GZ), 1)
    high, middle, low = three_parts(gains)
    tail = [
        lax.shift_right_logical(at, 8).astype(F32),
        (at & 255).astype(F32),
        *three_parts(projector[...]),
        jnp.where(lane == 0, high, jnp.where(lane == 1, middle, low)),
    ]
    near[SLAB_ROWS:NEAR_ROWS, :] = jnp.concatenate(tail, axis=0).astype(BF16)


def densify(points, projector, dense):
    grid_row, lane = lax.shift_right_logical(points, 7), points & (GZ - 1)
    high = projector.astype(BF16).astype(F32)
    parts = (high, projector - high)
    for atom in range(ATOM_DEV):
        rows = jnp.where(
            lax.broadcasted_iota(jnp.int32, (SLAB_ROWS, GZ), 0) == grid_row[atom : atom + 1, :],
            1.0,
            0.0,
        ).astype(BF16)
        at_lane = lax.broadcasted_iota(jnp.int32, (GZ, GZ), 0) == lane[atom : atom + 1, :]
        lanes = [
            jnp.where(at_lane, part[atom : atom + 1, :], 0.0).astype(BF16) for part in parts
        ]
        dense[atom] = lax.dot_general(
            jnp.concatenate([rows] * 2, axis=1),
            jnp.concatenate(lanes, axis=1),
            (((1,), (1,)), ((), ())),
            preferred_element_type=F32,
        )


def project_kernel(own, other, near, dense, gains, built, sems):
    parity = lax.axis_index("row") & 1
    copies = []
    for slab, (pair, index) in enumerate(WINDOW):
        if pair:
            tail = jnp.where(parity == index, own[SLAB_ROWS:OWN_ROWS, :], other[SLAB_ROWS:OWN_ROWS, :])
            points = tail[0:8].astype(jnp.int32)
            projector = tail[8:16]
            gains[slab] = tail[16:24]
        else:
            tail = near[index ^ parity, SLAB_ROWS:NEAR_ROWS, :].astype(F32)
            top, bottom, high, middle, low, gain = (
                tail[ATOM_DEV * i : ATOM_DEV * (i + 1)] for i in range(6)
            )
            points = top.astype(jnp.int32) * 256 + bottom.astype(jnp.int32)
            projector = high + middle + low
            gain = gain[:, 0:1] + gain[:, 1:2] + gain[:, 2:3]
            gains[slab] = jnp.broadcast_to(gain, (ATOM_DEV, GZ))
        densify(points, projector, built.at[slab])
        copies.append(pltpu.make_async_copy(built.at[slab], dense.at[slab], sems.at[slab]))
        copies[-1].start()
    for copy in copies:
        copy.wait()


def apply(source, window, scale, potential, dense, gains, along_z, along_y, wide_z, summed_z, emit):
    count = SLAB * len(window)
    weights = []
    for s, slab in enumerate(window):
        partial = [None] * ATOM_DEV
        for p in range(SLAB):
            value = source[SLAB * (s + 1) + p]
            high = value.astype(BF16)
            low = (value - high.astype(F32)).astype(BF16)
            start = (SLAB * s + p) * GY
            wide_z[start : start + GY, 0:GZ] = high
            wide_z[start : start + GY, GZ : 2 * GZ] = low
            for atom in range(ATOM_DEV):
                weight = dense[slab, atom, p * GY : (p + 1) * GY, :]
                term = jnp.sum((weight * value).reshape(GY // 8, 8, GZ), axis=0)
                partial[atom] = term if p == 0 else partial[atom] + term
        lines = [jnp.sum(term, axis=0, keepdims=True) for term in partial]
        total = jnp.sum(jnp.concatenate(lines, axis=0), axis=1, keepdims=True)
        weights.append(total * gains[slab])
    height = count * GY
    summed_z[0:height, :] = jnp.dot(
        wide_z[0:height, :], along_z[...], preferred_element_type=F32
    )
    for i in range(0, count, 2):
        both = jnp.concatenate(
            [
                jnp.concatenate(
                    [
                        wide_z[start : start + GY, 0:GZ],
                        wide_z[start : start + GY, GZ : 2 * GZ],
                    ],
                    axis=0,
                )
                for start in (i * GY, (i + 1) * GY)
            ],
            axis=1,
        )
        turned = jnp.dot(along_y[...], both, preferred_element_type=F32)
        turned = turned[:GY] + turned[GY:]
        for j in range(2):
            plane = i + j
            s, p = divmod(plane, SLAB)
            slab = window[s]
            at = plane + SLAB
            start = plane * GY
            total = (DIAGONAL + potential(slab, p)) * source[at] + turned[:, j * GZ : (j + 1) * GZ]
            total = total + (
                summed_z[start : start + GY, 0:GZ] + summed_z[start : start + GY, GZ : 2 * GZ]
            )
            for atom in range(ATOM_DEV):
                total = (
                    total
                    + weights[s][atom : atom + 1, :] * dense[slab, atom, p * GY : (p + 1) * GY, :]
                )
            for offset in range(1, 7):
                total = total + SIDE[offset] * (source[at - offset] + source[at + offset])
            emit(plane, scale * total)


def filter_kernel(
    received, own, other, near, projectors, gains, along_z, along_y,
    out, start, first, second, last, dense, potentials, wide_z, summed_z, sems,
):
    parity = lax.axis_index("row") & 1
    copies = [
        pltpu.make_async_copy(projectors.at[slab], dense.at[slab], sems.at[slab])
        for slab in range(SLABS)
    ]
    for copy in copies:
        copy.start()
    panel = jnp.zeros((YPART, GZ), F32)
    for source in range(ROWS):
        start[:, source * YPART : (source + 1) * YPART, :] = received[source, 0:WIDE].astype(F32)
        panel = panel + received[source, WIDE].astype(F32)
    potentials[parity] = own[0:SLAB_ROWS, :]
    potentials[1 - parity] = other[0:SLAB_ROWS, :]

    def potential(slab, p):
        pair, index = WINDOW[slab]
        rows = slice(p * GY, (p + 1) * GY)
        if pair:
            return potentials[index, rows, :]
        return near[index ^ parity, rows, :].astype(F32)

    for copy in copies:
        copy.wait()
    work = (potential, dense, gains, along_z, along_y, wide_z, summed_z)

    def emit_first(plane, value):
        first[plane] = value

    def emit_second(plane, value):
        second[plane] = value - start[plane + 2 * SLAB]

    def emit_last(plane, value):
        s, p = divmod(plane, SLAB)
        last[s, p * GY : (p + 1) * GY, :] = value - first[plane + 2 * SLAB]

    apply(start, (0, 1, 2, 3, 4, 5), 1.0 / HALF_WIDTH, *work, emit_first)
    apply(first, (1, 2, 3, 4), 2.0 / HALF_WIDTH, *work, emit_second)
    apply(second, (2, 3), 2.0 / HALF_WIDTH, *work, emit_last)

    line = lax.broadcasted_iota(jnp.int32, (4, GZ), 0)
    mine = jnp.where(parity == 0, panel[0:1], panel[1:2])
    tile = jnp.where(line == 0, mine, 0.0).astype(BF16)
    for half in range(2):
        for col in range(COLS):
            member = half * COLS + col
            for k in range(PIECE):
                at = 4 * (PIECE * col + k)
                out[member, k] = last[half, at : at + 4, :].astype(BF16)
            out[member, PIECE] = tile


def rotate_kernel(received, panel_rows, out, states, wanted, rotated):
    members = 2 * COLS
    size = 4 * members
    for member in range(members):
        at = slice(4 * member, 4 * member + 4)
        for k in range(PIECE):
            states[at, k * GZ : (k + 1) * GZ] = received[member, k].astype(F32)
        tile = received[member, PIECE].astype(F32)
        wanted[at, :] = jnp.broadcast_to(tile[0:1], (4, GZ))
    order = lax.broadcasted_iota(jnp.int32, (size, 64), 0) >> 2
    state_of = 2 * (order & (COLS - 1)) + lax.shift_right_logical(order, 5)
    stored = jnp.where(panel_rows[...] == state_of, 1.0, 0.0).astype(BF16)
    spread = lax.dot_general(
        wanted[:, 0:64].astype(BF16), stored, (((1,), (1,)), ((), ())),
        preferred_element_type=F32,
    )
    same = (
        lax.broadcasted_iota(jnp.int32, (size, size), 0) & 3
    ) == (lax.broadcasted_iota(jnp.int32, (size, size), 1) & 3)
    spread = jnp.where(same, spread, 0.0).astype(BF16)
    rotated[...] = jnp.dot(spread, states[...].astype(BF16), preferred_element_type=F32)
    for col in range(COLS):
        for state in range(2):
            at = 4 * (state * COLS + col)
            for k in range(PIECE):
                out[col, state * PIECE + k] = rotated[
                    at : at + 4, k * GZ : (k + 1) * GZ
                ].astype(BF16)


def place_kernel(received, out):
    for col in range(COLS):
        for state in range(2):
            for k in range(PIECE):
                at = 4 * (PIECE * col + k)
                out[state, at : at + 4, :] = received[col, state * PIECE + k].astype(F32)


def per_device(orbitals, potential, proj_points, projector, strength, ritz_panel, panel_rows):
    shape = jax.ShapeDtypeStruct
    along_z, along_y = stencil_matrices()
    smem = pl.BlockSpec(memory_space=pltpu.SMEM)
    axes = ("row", "col")

    own, near = call(
        given_kernel,
        (shape((OWN_ROWS, GZ), F32), shape((NEAR_ROWS, GZ), BF16)),
        specs=[VMEM] * 3 + [smem],
    )(potential, proj_points, projector, strength)
    offsets = ((-2, -1, 2, 3), (-2, -3, 2, 1))
    fetched = lax.ppermute(
        near,
        axes,
        [
            ((row + offsets[row % 2][col % 4]) % ROWS * COLS + col, row * COLS + col)
            for row in range(ROWS)
            for col in range(COLS)
        ],
    )
    packed = call(
        pack_kernel,
        shape((ROWS, SENT, YPART, GZ), BF16),
        scratch=[
            pltpu.VMEM((2, GX, YPART, GZ), BF16),
            pltpu.VMEM((2, YPART), BF16),
            pltpu.SemaphoreType.DMA((3,)),
        ],
        specs=[ANY] * 2,
        vmem=60 * MIB,
        flops=1_000_000,
        bytes_accessed=1_000_000,
    )(orbitals, ritz_panel.T)
    packed = pl.pallas_call(
        after_kernel,
        out_shape=shape(packed.shape, packed.dtype),
        in_specs=[ANY] * 2,
        out_specs=ANY,
        input_output_aliases={0: 0},
    )(packed, fetched)
    regrouped = lax.all_to_all(packed, "row", split_axis=0, concat_axis=0, tiled=True)
    other = lax.ppermute(own, "row", [(i, i ^ 1) for i in range(ROWS)])
    near = lax.all_gather(
        fetched,
        "col",
        axis=0,
        axis_index_groups=[[4 * i + k for k in range(4)] for i in range(COLS // 4)],
    )
    projectors, gains = call(
        project_kernel,
        (shape((SLABS, ATOM_DEV, SLAB_ROWS, GZ), F32), shape((SLABS, ATOM_DEV, GZ), F32)),
        scratch=[
            pltpu.VMEM((SLABS, ATOM_DEV, SLAB_ROWS, GZ), F32),
            pltpu.SemaphoreType.DMA((SLABS,)),
        ],
        specs=[VMEM] * 3,
        flops=4_000_000_000,
        bytes_accessed=10_000_000,
        vmem=24 * MIB,
        out_specs=(ANY, VMEM),
    )(own, other, near)
    layered = call(
        filter_kernel,
        shape((2 * COLS, PIECE + 1, 4, GZ), BF16),
        scratch=[
            pltpu.VMEM((WIDE, GY, GZ), F32),
            pltpu.VMEM((WIDE - PAIR, GY, GZ), F32),
            pltpu.VMEM((WIDE - 2 * PAIR, GY, GZ), F32),
            pltpu.VMEM((2, SLAB_ROWS, GZ), F32),
            pltpu.VMEM((SLABS, ATOM_DEV, SLAB_ROWS, GZ), F32),
            pltpu.VMEM((2, SLAB_ROWS, GZ), F32),
            pltpu.VMEM((SLABS * SLAB_ROWS, 2 * GZ), BF16),
            pltpu.VMEM((SLABS * SLAB_ROWS, 2 * GZ), F32),
            pltpu.SemaphoreType.DMA((SLABS,)),
        ],
        specs=[VMEM] * 4 + [ANY] + [VMEM] * 3,
        vmem=40 * MIB,
    )(regrouped, own, other, near, projectors, gains, along_z, along_y)
    columns = lax.all_to_all(
        layered,
        axes,
        split_axis=0,
        concat_axis=0,
        tiled=True,
        axis_index_groups=[
            [row * COLS + col for row in (2 * i, 2 * i + 1) for col in range(COLS)]
            for i in range(ROWS // 2)
        ],
    )
    turned = call(
        rotate_kernel,
        shape((COLS, 2 * PIECE, 4, GZ), BF16),
        scratch=[
            pltpu.VMEM((8 * COLS, PIECE * GZ), F32),
            pltpu.VMEM((8 * COLS, GZ), F32),
            pltpu.VMEM((8 * COLS, PIECE * GZ), F32),
        ],
        specs=[VMEM] * 2,
    )(columns, panel_rows.reshape(1, -1))
    result = lax.all_to_all(turned, "col", split_axis=0, concat_axis=0, tiled=True)
    whole = call(place_kernel, shape((2, SLAB_ROWS, GZ), F32), specs=[VMEM])(result)
    return whole.reshape(2, SLAB, GY, GZ)


def solution(mesh):
    placed = (
        P("col", None, "row", None),
        P("row", None, None),
        P("row", None),
        P("row", None),
        P("row"),
        P("row", "col"),
        P(),
    )
    return jax.shard_map(
        per_device,
        mesh=mesh,
        in_specs=placed,
        out_specs=P("col", "row", None, None),
        check_vma=False,
    )
```

time: 97.7 us -> 109 us (1.12)
  local copies, waits for them, and re-layouts: 0.04 us -> 10.9 us
  Pallas kernels: 9.71 us -> 16.5 us
  starting transfers between devices: 25.7 us -> 19.7 us
  waiting for transfers between devices: 17.9 us -> 12.3 us
  blocking collectives: 43.7 us -> 48.1 us
    unnamed x14 -> x20, local copies, waits for them, and re-layouts: 0.04 us -> 10.9 us
    all_gather x0 -> x1, blocking collectives: none -> 10.2 us  [per_device(): lax.all_gather(fetched, 'col', axis=0, axis_index_groups=[[4 * i + k for...]
    pallas_call x7 -> x4, Pallas kernels: 6.57 us -> 13.3 us  [the longest x1 8.41 us: per_device(): call(filter_kernel, shape((2 * COLS, PIECE + 1, 4, GZ), BF16), scratch=[p...]
    ppermute x5 -> x2, starting transfers between devices: 15.5 us -> 9.32 us  [the longest x1 6.06 us: per_device(): lax.ppermute(near, axes, [((row + offsets[row % 2][col % 4]) % ROWS * COL...]
    all_to_all x1, blocking collectives: 28.9 us -> 24.4 us  [per_device(): lax.all_to_all(layered, axes, split_axis=0, concat_axis=0, tiled=True, ax...]
    all_to_all x1, waiting for transfers between devices: 3.8 us -> 0.01 us  [per_device(): lax.all_to_all(packed, 'row', split_axis=0, concat_axis=0, tiled=True)]
    ppermute x5 -> x2, waiting for transfers between devices: 14.1 us -> 12.3 us  [the longest x1 9.93 us: per_device(): other = lax.ppermute(own, 'row', [(i, i ^ 1) for i in range(ROWS)])]
    all_to_all x1, blocking collectives: 14.8 us -> 13.5 us  [per_device(): lax.all_to_all(turned, 'col', split_axis=0, concat_axis=0, tiled=True)]
  transfers between devices with their start and end apart: 6 -> 3, of which waited for: 4 -> 2; matrix products, arithmetic and copies ran while one was open for 0% -> 0% of each run, Pallas kernels for 4% -> 6%
where the time goes in v7:
time: 109 us; the launch traced here: 108 us
  blocking collectives  48.1 us (44%)
  starting transfers between devices  19.7 us (18%)
  Pallas kernels  16.5 us (15%)
  waiting for transfers between devices  12.3 us (11%)
  local copies, waits for them, and re-layouts  10.9 us (10%)
    all_to_all x1, blocking collectives, per_device(): lax.all_to_all(layered, axes, split_axis=0, concat_axis=0, tiled=True, ax...  24.4 us
    all_to_all x1, blocking collectives, per_device(): lax.all_to_all(turned, 'col', split_axis=0, concat_axis=0, tiled=True)  13.5 us
    unnamed x20, local copies, waits for them, and re-layouts  10.9 us
    all_to_all x1, starting transfers between devices, per_device(): lax.all_to_all(packed, 'row', split_axis=0, concat_axis=0, tiled=True)  10.4 us
    all_gather x1, blocking collectives, per_device(): lax.all_gather(fetched, 'col', axis=0, axis_index_groups=[[4 * i + k for...  10.2 us
    ppermute x1, waiting for transfers between devices, per_device(): other = lax.ppermute(own, 'row', [(i, i ^ 1) for i in range(ROWS)])  9.93 us
    pallas_call x1, Pallas kernels, per_device(): call(filter_kernel, shape((2 * COLS, PIECE + 1, 4, GZ), BF16), scratch=[p...  8.41 us
    ppermute x1, starting transfers between devices, per_device(): lax.ppermute(near, axes, [((row + offsets[row % 2][col % 4]) % ROWS * COL...  6.06 us
  transfers between devices with their start and end apart: 3, of which 2 were waited for; matrix products, arithmetic and copies ran while one was open for 0% of the time, Pallas kernels for 6%

profile of v7, /device:TPU:1, one launch (start us, length us, event | category | flops | bytes accessed | tf_op | source)
XLA Modules:
  0.0 107.7 jit_solution(3772561041334441533)
XLA Ops:
  0.0 0.0 copy-start.2
  0.0 0.9 copy-done.2
  0.9 0.0 copy-start.5
  0.9 0.7 copy-done.5
  1.6 0.0 copy-start.6
  1.6 0.7 copy-done.6
  2.3 0.0 copy-start.7
  2.3 0.7 copy-done.7
  3.0 0.6 shard_map.92
  3.5 6.1 %collective-permute-start = (bf16[432,128]{1,0:T(8,128)(2,1)S(1)}, bf16[432,128]{1,0:T(8,128)(2,1)S(1)}, u32[]{:S(2)}, u32[]{:S(2)}) collective-permute-start(bf16[432,128]{1,0:T(8,128)(2,1)S(1)} %get-tuple-element.9), channel_id=1, source_target_pairs={{448,0},{481,1},{66,2},{99,3},{452,4},{485,5},{70,6},{103,7},{456,... | collective-permute-start | bytes 331784 | tf_op jit(solution)/shard_map/ppermute | solution.py:360
  9.6 2.0 %shard_map.91.packed = bf16[16,49,4,128]{3,2,1,0:T(4,128)(2,1)} custom-call(bf16[2,96,4,128]{3,2,1,0:T(4,128)(2,1)} %orbitals.1, bf16[2,4]{1,0:T(2,128)(2,1)} %bitcast.7), custom_call_target="tpu_custom_call" | custom-call | flops 1000000 | bytes 1000000 | tf_op jit(solution)/shard_map/pallas_call | solution.py:369
  11.6 0.0 copy-start.3
  11.7 0.0 copy-start.4
  11.7 2.4 %collective-permute-done.received = bf16[432,128]{1,0:T(8,128)(2,1)S(1)} collective-permute-done((bf16[432,128]{1,0:T(8,128)(2,1)S(1)}, bf16[432,128]{1,0:T(8,128)(2,1)S(1)}, u32[]{:S(2)}, u32[]{:S(2)}) %collective-permute-start) | collective-permute-done | bytes 110624 | tf_op jit(solution)/shard_map/ppermute | solution.py:360
  14.0 0.0 copy-start.9
  14.0 0.6 copy-done.9
  14.7 10.4 %all-to-all-start = ((bf16[16,49,4,128]{3,2,1,0:T(4,128)(2,1)}), bf16[16,49,4,128]{3,2,1,0:T(4,128)(2,1)S(1)}, u32[]{:S(2)}, u32[]{:S(2)}) async-start(bf16[16,49,4,128]{3,2,1,0:T(4,128)(2,1)} %shard_map.93), calls=%async_computation | async-start | bytes 1605632 | tf_op jit(solution)/shard_map/all_to_all | solution.py:389
  25.1 3.3 %collective-permute-start.1 = (f32[408,128]{1,0:T(8,128)S(1)}, f32[408,128]{1,0:T(8,128)S(1)}, u32[]{:S(2)}, u32[]{:S(2)}) collective-permute-start(f32[408,128]{1,0:T(8,128)S(1)} %get-tuple-element.10.own), channel_id=1, source_target_pairs={{0,32},{32,0},{64,96},{96,64},{128,160},{160,128},{192,224},{224,1... | collective-permute-start | bytes 626696 | tf_op jit(solution)/shard_map/ppermute | solution.py:390
  28.3 10.2 %all-gather = bf16[1728,128]{1,0:T(8,128)(2,1)S(1)} all-gather(bf16[432,128]{1,0:T(8,128)(2,1)} %copy-done.9), channel_id=2, replica_groups={{0,1,2,3},{4,5,6,7},{8,9,10,11},{12,13,14,15},{16,17,18,19},{20,21,22,2..., dimensions={0}, use_global_device_ids=true | all-gather | bytes 552960 | tf_op jit(solution)/shard_map/all_gather | solution.py:391
  38.6 9.9 %collective-permute-done.1.other = f32[408,128]{1,0:T(8,128)S(1)} collective-permute-done((f32[408,128]{1,0:T(8,128)S(1)}, f32[408,128]{1,0:T(8,128)S(1)}, u32[]{:S(2)}, u32[]{:S(2)}) %collective-permute-start.1) | collective-permute-done | bytes 208928 | tf_op jit(solution)/shard_map/ppermute | solution.py:390
  48.5 4.3 %shard_map.94 = (f32[6,8,384,128]{3,2,1,0:T(8,128)S(1)}, f32[6,8,128]{2,1,0:T(8,128)S(1)}) custom-call(f32[408,128]{1,0:T(8,128)S(1)} %get-tuple-element.10.own, f32[408,128]{1,0:T(8,128)S(1)} %collective-permute-done.1.other, bf16[4,432,128]{2,1,0:T(8,128)(2,1)S(1)} %bitcast.4), custom_call_target="tpu_custom_call" | custom-call | flops 4000000000 | bytes 10000000 | tf_op jit(solution)/shard_map/pallas_call | solution.py:397
  52.8 0.0 copy-start
  52.8 3.6 %copy-done = f32[6,8,384,128]{3,2,1,0:T(8,128)} copy-done((f32[6,8,384,128]{3,2,1,0:T(8,128)}, f32[6,8,384,128]{3,2,1,0:T(8,128)S(1)}, u32[]{:S(2)}) %copy-start) | copy-done | bytes 9437208
  56.5 0.0 copy-start.8
  56.5 0.0 all-to-all-done.received
  56.5 0.0 copy-done.3
  56.5 0.0 copy-done.4
  56.5 0.0 copy-start.1
  56.5 3.7 %copy-done.1 = f32[6,8,384,128]{3,2,1,0:T(8,128)S(1)} copy-done((f32[6,8,384,128]{3,2,1,0:T(8,128)S(1)}, f32[6,8,384,128]{3,2,1,0:T(8,128)}, u32[]{:S(2)}) %copy-start.1) | copy-done | bytes 9437208
  60.2 8.4 %shard_map.95 = bf16[64,4,4,128]{3,2,1,0:T(4,128)(2,1)S(1)} custom-call(bf16[16,49,4,128]{3,2,1,0:T(4,128)(2,1)S(1)} %all-to-all-done.received, f32[408,128]{1,0:T(8,128)S(1)} %get-tuple-element.10.own, f32[408,128]{1,0:T(8,128)S(1)} %collective-permute-done.1.other, bf16[4,432,128]{2,1,0:T(8,128)(2,1)S(1)} %bitcast.5, f32[6,8,384,128]{3,2,1,0:T(8,128)S(1)} %copy-done.1, ...), custom_call_target="tpu_custom_call" | custom-call | tf_op jit(solution)/shard_map/pallas_call | solution.py:410
  68.6 24.4 %all_to_all.15.received = bf16[64,4,4,128]{3,2,1,0:T(4,128)(2,1)S(1)} all-to-all(bf16[64,4,4,128]{3,2,1,0:T(4,128)(2,1)S(1)} %shard_map.95), channel_id=1, replica_groups={{0,1,2,3,4,5,6,7,8,9,10,11,12,13,14,15,16,17,18,19,20,21,22,23,24,25,26..., dimensions={0} | all-to-all | bytes 524288 | tf_op jit(solution)/shard_map/all_to_all | solution.py:427
  93.0 0.0 copy-done.8
  93.0 0.4 shard_map.96
  93.4 13.5 %all_to_all.16.received = bf16[32,6,4,128]{3,2,1,0:T(4,128)(2,1)S(1)} all-to-all(bf16[32,6,4,128]{3,2,1,0:T(4,128)(2,1)S(1)} %shard_map.96), channel_id=1, replica_groups=mesh['row'=16,'col'=32] {'col'}, dimensions={0} | all-to-all | bytes 393216 | tf_op jit(solution)/shard_map/all_to_all | solution.py:448
  106.9 0.8 shard_map.97
  (1 shorter events, 0.0 us)
Async XLA Ops:
  0.0 0.9 copy-start.2
  0.9 0.7 copy-start.5
  1.6 0.7 copy-start.6
  2.3 0.7 copy-start.7
  3.5 10.5 %collective-permute-start = (bf16[432,128]{1,0:T(8,128)(2,1)S(1)}, bf16[432,128]{1,0:T(8,128)(2,1)S(1)}, u32[]{:S(2)}, u32[]{:S(2)}) collective-permute-start(bf16[432,128]{1,0:T(8,128)(2,1)S(1)} %get-tuple-element.9), channel_id=1, source_target_pairs={{448,0},{481,1},{66,2},{99,3},{452,4},{485,5},{70,6},{103,7},{456,... | collective-permute-start | bytes 331784 | tf_op jit(solution)/shard_map/ppermute | solution.py:360
  11.6 44.8 %copy-start.3 = (bf16[256,256]{1,0:T(8,128)(2,1)S(1)}, bf16[256,256]{1,0:T(8,128)(2,1)}, u32[]{:S(2)}) copy-start(bf16[256,256]{1,0:T(8,128)(2,1)} %constant.4.clone.along_z) | copy-start | bytes 393220
  11.7 44.8 %copy-start.4 = (bf16[128,128]{1,0:T(8,128)(2,1)S(1)}, bf16[128,128]{1,0:T(8,128)(2,1)}, u32[]{:S(2)}) copy-start(bf16[128,128]{1,0:T(8,128)(2,1)} %constant.5.clone.along_y) | copy-start | bytes 98308
  14.0 0.6 copy-start.9
  14.7 41.8 %all-to-all-start = ((bf16[16,49,4,128]{3,2,1,0:T(4,128)(2,1)}), bf16[16,49,4,128]{3,2,1,0:T(4,128)(2,1)S(1)}, u32[]{:S(2)}, u32[]{:S(2)}) async-start(bf16[16,49,4,128]{3,2,1,0:T(4,128)(2,1)} %shard_map.93), calls=%async_computation | async-start | bytes 1605632 | tf_op jit(solution)/shard_map/all_to_all | solution.py:389
  25.1 23.4 %collective-permute-start.1 = (f32[408,128]{1,0:T(8,128)S(1)}, f32[408,128]{1,0:T(8,128)S(1)}, u32[]{:S(2)}, u32[]{:S(2)}) collective-permute-start(f32[408,128]{1,0:T(8,128)S(1)} %get-tuple-element.10.own), channel_id=1, source_target_pairs={{0,32},{32,0},{64,96},{96,64},{128,160},{160,128},{192,224},{224,1... | collective-permute-start | bytes 626696 | tf_op jit(solution)/shard_map/ppermute | solution.py:390
  52.8 3.7 %copy-start = (f32[6,8,384,128]{3,2,1,0:T(8,128)}, f32[6,8,384,128]{3,2,1,0:T(8,128)S(1)}, u32[]{:S(2)}) copy-start(f32[6,8,384,128]{3,2,1,0:T(8,128)S(1)} %get-tuple-element.11.projectors) | copy-start | bytes 28311556
  56.5 36.5 %copy-start.8 = (s32[64]{0:T(128)S(1)}, s32[64]{0:T(128)}, u32[]{:S(2)}) copy-start(s32[64]{0:T(128)} %param.15) | copy-start | bytes 772
  56.5 3.7 %copy-start.1 = (f32[6,8,384,128]{3,2,1,0:T(8,128)S(1)}, f32[6,8,384,128]{3,2,1,0:T(8,128)}, u32[]{:S(2)}) copy-start(f32[6,8,384,128]{3,2,1,0:T(8,128)} %copy-done) | copy-start | bytes 28311556

commit v8 on v5

--- a/solution.py
+++ b/solution.py
@@ -397,8 +397,8 @@
         specs=[VMEM] * 7,
     )(regrouped, *fixed)
     for step in range(2):
+        above = lax.ppermute(sent, "row", [(d, s) for s, d in around])
         below = lax.ppermute(sent, "row", around)
-        above = lax.ppermute(sent, "row", [(d, s) for s, d in around])
         partial = call(
             inside_kernel,
             slabs_f32,

time: 97.7 us -> 97.7 us (level)
  no operation moved by 1% of the time
where the time goes in v8:
time: 97.7 us; the launch traced here: 97.3 us
  blocking collectives  43.7 us (45%)
  starting transfers between devices  25.7 us (26%)
  waiting for transfers between devices  17.9 us (18%)
  Pallas kernels  9.71 us (10%)
    all_to_all x1, blocking collectives, per_device(): lax.all_to_all(layered, ('row', 'col'), split_axis=0, concat_axis=0, tile...  28.9 us
    all_to_all x1, blocking collectives, per_device(): lax.all_to_all(turned, 'col', split_axis=0, concat_axis=0, tiled=True)  14.8 us
    all_to_all x1, starting transfers between devices, per_device(): lax.all_to_all(packed, 'row', split_axis=0, concat_axis=0, tiled=True)  10.2 us
    ppermute x1, waiting for transfers between devices, per_device(): other = lax.ppermute(given, 'row', [(i, i ^ HALF) for i in range(ROWS)])  7.11 us
    ppermute x2, waiting for transfers between devices, per_device(): below = lax.ppermute(sent, 'row', around)  7 us
    ppermute x2, starting transfers between devices, per_device(): below = lax.ppermute(sent, 'row', around)  5.6 us
    ppermute x2, starting transfers between devices, per_device(): above = lax.ppermute(sent, 'row', [(d, s) for s, d in around])  4.97 us
    ppermute x1, starting transfers between devices, per_device(): other = lax.ppermute(given, 'row', [(i, i ^ HALF) for i in range(ROWS)])  4.91 us
  transfers between devices with their start and end apart: 6, of which 4 were waited for; matrix products, arithmetic and copies ran while one was open for 0% of the time, Pallas kernels for 4%

profile of v8, /device:TPU:1, one launch (start us, length us, event | category | flops | bytes accessed | tf_op | source)
XLA Modules:
  0.0 97.3 jit_solution(10465933894421142084)
XLA Ops:
  0.0 0.0 copy-start
  0.0 0.0 copy-start.5
  0.0 0.0 copy-start.4
  0.0 0.0 copy-start.3
  0.0 2.0 %shard_map.91 = bf16[16,37,4,128]{3,2,1,0:T(4,128)(2,1)} custom-call(bf16[2,96,4,128]{3,2,1,0:T(4,128)(2,1)} %orbitals.1, bf16[2,4]{1,0:T(2,128)(2,1)} %bitcast.4), custom_call_target="tpu_custom_call" | custom-call | tf_op jit(solution)/shard_map/pallas_call | solution.py:365
  2.0 10.2 %all-to-all-start = ((bf16[16,37,4,128]{3,2,1,0:T(4,128)(2,1)}), bf16[16,37,4,128]{3,2,1,0:T(4,128)(2,1)S(1)}, u32[]{:S(2)}, u32[]{:S(2)}) async-start(bf16[16,37,4,128]{3,2,1,0:T(4,128)(2,1)} %shard_map.91), calls=%async_computation | async-start | bytes 1212416 | tf_op jit(solution)/shard_map/all_to_all | solution.py:376
  12.2 0.0 copy-done
  12.2 0.0 copy-done.5
  12.2 0.0 copy-done.4
  12.2 0.0 copy-done.3
  12.3 0.6 shard_map.92
  12.8 0.0 copy-start.1
  12.8 0.0 copy-start.2
  12.8 4.9 %collective-permute-start = (f32[408,128]{1,0:T(8,128)S(1)}, f32[408,128]{1,0:T(8,128)S(1)}, u32[]{:S(2)}, u32[]{:S(2)}) collective-permute-start(f32[408,128]{1,0:T(8,128)S(1)} %shard_map.92), channel_id=1, source_target_pairs={{0,256},{32,288},{64,320},{96,352},{128,384},{160,416},{192,448},{... | collective-permute-start | bytes 626696 | tf_op jit(solution)/shard_map/ppermute | solution.py:384
  17.8 1.1 %shard_map.93 = (f32[8,384,128]{2,1,0:T(8,128)S(1)}, f32[8,128]{1,0:T(8,128)S(1)}) custom-call(s32[8,128]{1,0:T(8,128)S(1)} %copy-done.3, f32[8,128]{1,0:T(8,128)S(1)} %copy-done.4, f32[8]{0:T(128)S(1)} %copy-done.5), custom_call_target="tpu_custom_call" | custom-call | flops 1000000000 | bytes 1600000 | tf_op jit(solution)/shard_map/pallas_call | solution.py:385
  18.9 7.1 %collective-permute-done.other = f32[408,128]{1,0:T(8,128)S(1)} collective-permute-done((f32[408,128]{1,0:T(8,128)S(1)}, f32[408,128]{1,0:T(8,128)S(1)}, u32[]{:S(2)}, u32[]{:S(2)}) %collective-permute-start) | collective-permute-done | bytes 208928 | tf_op jit(solution)/shard_map/ppermute | solution.py:384
  26.0 3.8 %all-to-all-done.received = bf16[16,37,4,128]{3,2,1,0:T(4,128)(2,1)S(1)} async-done(((bf16[16,37,4,128]{3,2,1,0:T(4,128)(2,1)}), bf16[16,37,4,128]{3,2,1,0:T(4,128)(2,1)S(1)}, u32[]{:S(2)}, u32[]{:S(2)}) %all-to-all-start) | async-done | bytes 606240 | tf_op jit(solution)/shard_map/all_to_all | solution.py:376
  29.8 0.0 copy-done.1
  29.8 0.0 copy-done.2
  29.8 1.7 %shard_map.94 = (f32[2,6,64,128]{3,2,1,0:T(8,128)S(1)}, f32[2,6,64,128]{3,2,1,0:T(8,128)S(1)}, bf16[2,6,64,128]{3,2,1,0:T(8,128)(2,1)S(1)}, f32[8,128]{1,0:T(8,128)S(1)}) custom-call(bf16[16,37,4,128]{3,2,1,0:T(4,128)(2,1)S(1)} %all-to-all-done.received, f32[6,64,128]{2,1,0:T(8,128)S(1)} %copy-done, f32[408,128]{1,0:T(8,128)S(1)} %collective-permute-done.other, ...), custom_call_target="tpu_custom_call" | custom-call | tf_op jit(solution)/shard_map/pallas_call | solution.py:393
  31.5 2.6 %collective-permute-start.2 = (bf16[2,6,64,128]{3,2,1,0:T(8,128)(2,1)S(1)}, bf16[2,6,64,128]{3,2,1,0:T(8,128)(2,1)S(1)}, u32[]{:S(2)}, u32[]{:S(2)}) collective-permute-start(bf16[2,6,64,128]{3,2,1,0:T(8,128)(2,1)S(1)} %get-tuple-element.17), channel_id=1, source_target_pairs={{32,0},{64,32},{96,64},{128,96},{160,128},{192,160},{224,192},{0,2... | collective-permute-start | bytes 589832 | tf_op jit(solution)/shard_map/ppermute | solution.py:400
  34.1 2.7 %collective-permute-start.1 = (bf16[2,6,64,128]{3,2,1,0:T(8,128)(2,1)S(1)}, bf16[2,6,64,128]{3,2,1,0:T(8,128)(2,1)S(1)}, u32[]{:S(2)}, u32[]{:S(2)}) collective-permute-start(bf16[2,6,64,128]{3,2,1,0:T(8,128)(2,1)S(1)} %get-tuple-element.17), channel_id=1, source_target_pairs={{0,32},{32,64},{64,96},{96,128},{128,160},{160,192},{192,224},{224... | collective-permute-start | bytes 589832 | tf_op jit(solution)/shard_map/ppermute | solution.py:401
  36.8 1.3 %shard_map.95.partial = f32[2,6,64,128]{3,2,1,0:T(8,128)S(1)} custom-call(f32[2,6,64,128]{3,2,1,0:T(8,128)S(1)} %get-tuple-element.15.current.previous, f32[2,6,64,128]{3,2,1,0:T(8,128)S(1)} %get-tuple-element.16.previous, f32[6,64,128]{2,1,0:T(8,128)S(1)} %copy-done, f32[408,128]{1,0:T(8,128)S(1)} %collective-permute-done.other, ...), custom_call_target="tpu_custom_call" | custom-call | flops 2000000000 | bytes 3000000 | tf_op jit(solution)/shard_map/pallas_call | solution.py:402
  38.1 0.0 collective-permute-done.2.above
  38.1 3.6 %collective-permute-done.1.below = bf16[2,6,64,128]{3,2,1,0:T(8,128)(2,1)S(1)} collective-permute-done((bf16[2,6,64,128]{3,2,1,0:T(8,128)(2,1)S(1)}, bf16[2,6,64,128]{3,2,1,0:T(8,128)(2,1)S(1)}, u32[]{:S(2)}, u32[]{:S(2)}) %collective-permute-start.1) | collective-permute-done | bytes 196640 | tf_op jit(solution)/shard_map/ppermute | solution.py:401
  41.8 0.2 shard_map.96
  42.0 2.4 %collective-permute-start.4 = (bf16[2,6,64,128]{3,2,1,0:T(8,128)(2,1)S(1)}, bf16[2,6,64,128]{3,2,1,0:T(8,128)(2,1)S(1)}, u32[]{:S(2)}, u32[]{:S(2)}) collective-permute-start(bf16[2,6,64,128]{3,2,1,0:T(8,128)(2,1)S(1)} %get-tuple-element.19), channel_id=1, source_target_pairs={{32,0},{64,32},{96,64},{128,96},{160,128},{192,160},{224,192},{0,2... | collective-permute-start | bytes 589832 | tf_op jit(solution)/shard_map/ppermute | solution.py:400
  44.4 2.9 %collective-permute-start.3 = (bf16[2,6,64,128]{3,2,1,0:T(8,128)(2,1)S(1)}, bf16[2,6,64,128]{3,2,1,0:T(8,128)(2,1)S(1)}, u32[]{:S(2)}, u32[]{:S(2)}) collective-permute-start(bf16[2,6,64,128]{3,2,1,0:T(8,128)(2,1)S(1)} %get-tuple-element.19), channel_id=1, source_target_pairs={{0,32},{32,64},{64,96},{96,128},{128,160},{160,192},{192,224},{224... | collective-permute-start | bytes 589832 | tf_op jit(solution)/shard_map/ppermute | solution.py:401
  47.3 1.3 %shard_map.97.partial = f32[2,6,64,128]{3,2,1,0:T(8,128)S(1)} custom-call(f32[2,6,64,128]{3,2,1,0:T(8,128)S(1)} %get-tuple-element.18.current, f32[2,6,64,128]{3,2,1,0:T(8,128)S(1)} %get-tuple-element.15.current.previous, f32[6,64,128]{2,1,0:T(8,128)S(1)} %copy-done, f32[408,128]{1,0:T(8,128)S(1)} %collective-permute-done.other, ...), custom_call_target="tpu_custom_call" | custom-call | flops 2000000000 | bytes 3000000 | tf_op jit(solution)/shard_map/pallas_call | solution.py:402
  48.6 0.0 copy-start.6
  48.6 0.0 collective-permute-done.4.above
  48.6 3.4 %collective-permute-done.3.below = bf16[2,6,64,128]{3,2,1,0:T(8,128)(2,1)S(1)} collective-permute-done((bf16[2,6,64,128]{3,2,1,0:T(8,128)(2,1)S(1)}, bf16[2,6,64,128]{3,2,1,0:T(8,128)(2,1)S(1)}, u32[]{:S(2)}, u32[]{:S(2)}) %collective-permute-start.3) | collective-permute-done | bytes 196640 | tf_op jit(solution)/shard_map/ppermute | solution.py:401
  52.0 0.3 shard_map.98
  52.3 28.9 %all_to_all.15.received = bf16[64,4,4,128]{3,2,1,0:T(4,128)(2,1)S(1)} all-to-all(bf16[64,4,4,128]{3,2,1,0:T(4,128)(2,1)S(1)} %shard_map.98), channel_id=1, replica_groups={{0,1,2,3,4,5,6,7,8,9,10,11,12,13,14,15,16,17,18,19,20,21,22,23,24,25,26..., dimensions={0} | all-to-all | bytes 524288 | tf_op jit(solution)/shard_map/all_to_all | solution.py:425
  81.3 0.0 copy-done.6
  81.3 0.4 shard_map.99
  81.7 14.8 %all_to_all.16.received = bf16[32,6,4,128]{3,2,1,0:T(4,128)(2,1)S(1)} all-to-all(bf16[32,6,4,128]{3,2,1,0:T(4,128)(2,1)S(1)} %shard_map.99), channel_id=1, replica_groups=mesh['row'=16,'col'=32] {'col'}, dimensions={0} | all-to-all | bytes 393216 | tf_op jit(solution)/shard_map/all_to_all | solution.py:438
  96.5 0.8 shard_map.100
Async XLA Ops:
  0.0 12.2 %copy-start = (f32[6,64,128]{2,1,0:T(8,128)S(1)}, f32[6,64,128]{2,1,0:T(8,128)}, u32[]{:S(2)}) copy-start(f32[6,64,128]{2,1,0:T(8,128)} %potential.7) | copy-start | bytes 589828
  0.0 12.2 %copy-start.5 = (f32[8]{0:T(128)S(1)}, f32[8]{0:T(128)}, u32[]{:S(2)}) copy-start(f32[8]{0:T(128)} %strength.3) | copy-start | bytes 100
  0.0 12.2 %copy-start.4 = (f32[8,128]{1,0:T(8,128)S(1)}, f32[8,128]{1,0:T(8,128)}, u32[]{:S(2)}) copy-start(f32[8,128]{1,0:T(8,128)} %projector.3) | copy-start | bytes 12292
  0.0 12.2 %copy-start.3 = (s32[8,128]{1,0:T(8,128)S(1)}, s32[8,128]{1,0:T(8,128)}, u32[]{:S(2)}) copy-start(s32[8,128]{1,0:T(8,128)} %points.3) | copy-start | bytes 12292
  2.0 27.8 %all-to-all-start = ((bf16[16,37,4,128]{3,2,1,0:T(4,128)(2,1)}), bf16[16,37,4,128]{3,2,1,0:T(4,128)(2,1)S(1)}, u32[]{:S(2)}, u32[]{:S(2)}) async-start(bf16[16,37,4,128]{3,2,1,0:T(4,128)(2,1)} %shard_map.91), calls=%async_computation | async-start | bytes 1212416 | tf_op jit(solution)/shard_map/all_to_all | solution.py:376
  12.8 17.0 %copy-start.1 = (bf16[256,256]{1,0:T(8,128)(2,1)S(1)}, bf16[256,256]{1,0:T(8,128)(2,1)}, u32[]{:S(2)}) copy-start(bf16[256,256]{1,0:T(8,128)(2,1)} %constant.4.clone.along_z) | copy-start | bytes 393220
  12.8 17.0 %copy-start.2 = (bf16[128,128]{1,0:T(8,128)(2,1)S(1)}, bf16[128,128]{1,0:T(8,128)(2,1)}, u32[]{:S(2)}) copy-start(bf16[128,128]{1,0:T(8,128)(2,1)} %constant.5.clone.along_y) | copy-start | bytes 98308
  12.8 13.1 %collective-permute-start = (f32[408,128]{1,0:T(8,128)S(1)}, f32[408,128]{1,0:T(8,128)S(1)}, u32[]{:S(2)}, u32[]{:S(2)}) collective-permute-start(f32[408,128]{1,0:T(8,128)S(1)} %shard_map.92), channel_id=1, source_target_pairs={{0,256},{32,288},{64,320},{96,352},{128,384},{160,416},{192,448},{... | collective-permute-start | bytes 626696 | tf_op jit(solution)/shard_map/ppermute | solution.py:384
  31.5 6.6 %collective-permute-start.2 = (bf16[2,6,64,128]{3,2,1,0:T(8,128)(2,1)S(1)}, bf16[2,6,64,128]{3,2,1,0:T(8,128)(2,1)S(1)}, u32[]{:S(2)}, u32[]{:S(2)}) collective-permute-start(bf16[2,6,64,128]{3,2,1,0:T(8,128)(2,1)S(1)} %get-tuple-element.17), channel_id=1, source_target_pairs={{32,0},{64,32},{96,64},{128,96},{160,128},{192,160},{224,192},{0,2... | collective-permute-start | bytes 589832 | tf_op jit(solution)/shard_map/ppermute | solution.py:400
  34.1 7.6 %collective-permute-start.1 = (bf16[2,6,64,128]{3,2,1,0:T(8,128)(2,1)S(1)}, bf16[2,6,64,128]{3,2,1,0:T(8,128)(2,1)S(1)}, u32[]{:S(2)}, u32[]{:S(2)}) collective-permute-start(bf16[2,6,64,128]{3,2,1,0:T(8,128)(2,1)S(1)} %get-tuple-element.17), channel_id=1, source_target_pairs={{0,32},{32,64},{64,96},{96,128},{128,160},{160,192},{192,224},{224... | collective-permute-start | bytes 589832 | tf_op jit(solution)/shard_map/ppermute | solution.py:401
  42.0 6.6 %collective-permute-start.4 = (bf16[2,6,64,128]{3,2,1,0:T(8,128)(2,1)S(1)}, bf16[2,6,64,128]{3,2,1,0:T(8,128)(2,1)S(1)}, u32[]{:S(2)}, u32[]{:S(2)}) collective-permute-start(bf16[2,6,64,128]{3,2,1,0:T(8,128)(2,1)S(1)} %get-tuple-element.19), channel_id=1, source_target_pairs={{32,0},{64,32},{96,64},{128,96},{160,128},{192,160},{224,192},{0,2... | collective-permute-start | bytes 589832 | tf_op jit(solution)/shard_map/ppermute | solution.py:400
  44.4 7.6 %collective-permute-start.3 = (bf16[2,6,64,128]{3,2,1,0:T(8,128)(2,1)S(1)}, bf16[2,6,64,128]{3,2,1,0:T(8,128)(2,1)S(1)}, u32[]{:S(2)}, u32[]{:S(2)}) collective-permute-start(bf16[2,6,64,128]{3,2,1,0:T(8,128)(2,1)S(1)} %get-tuple-element.19), channel_id=1, source_target_pairs={{0,32},{32,64},{64,96},{96,128},{128,160},{160,192},{192,224},{224... | collective-permute-start | bytes 589832 | tf_op jit(solution)/shard_map/ppermute | solution.py:401
  48.6 32.6 %copy-start.6 = (s32[64]{0:T(128)S(1)}, s32[64]{0:T(128)}, u32[]{:S(2)}) copy-start(s32[64]{0:T(128)} %param.15) | copy-start | bytes 772

commit v9 on v8

--- a/solution.py
+++ b/solution.py
@@ -283,7 +283,7 @@
     return joined
 
 
-def join_kernel(partial, below, above, next_out, sent_out):
+def join_kernel(partial, above, below, next_out, sent_out):
     joined = joining(partial, below, above)
     for p in range(SLAB):
         for slab in range(2):
@@ -292,7 +292,7 @@
             sent_out[slab, p] = value.astype(BF16)
 
 
-def last_kernel(partial, below, above, panel, out, slabs):
+def last_kernel(partial, above, below, panel, out, slabs):
     joined = joining(partial, below, above)
     for p in range(SLAB):
         for slab in range(2):
@@ -410,14 +410,14 @@
         if step == 0:
             previous = current
             current, sent = call(join_kernel, (slabs_f32, slabs_bf16), specs=[VMEM] * 3)(
-                partial, below, above
+                partial, above, below
             )
     layered = call(
         last_kernel,
         shape((2 * COLS, PIECE + 1, 4, GZ), BF16),
         scratch=[pltpu.VMEM((2, SLAB_ROWS, GZ), F32)],
         specs=[VMEM] * 4,
-    )(partial, below, above, panel)
+    )(partial, above, below, panel)
     both = [
         [(i + HALF * half) * COLS + col for half in range(2) for col in range(COLS)]
         for i in range(HALF)

time: 97.7 us -> 96.1 us (0.984)
  waiting for transfers between devices: 17.9 us -> 13.6 us
  starting transfers between devices: 25.7 us -> 28.4 us
    ppermute x2, waiting for transfers between devices: 7 us -> 0.01 us  [per_device(): below = lax.ppermute(sent, 'row', around)]
    ppermute x2, starting transfers between devices: 4.97 us -> 8.01 us  [per_device(): above = lax.ppermute(sent, 'row', [(d, s) for s, d in around])]
    ppermute x2, waiting for transfers between devices: 0.01 us -> 2.71 us  [per_device(): above = lax.ppermute(sent, 'row', [(d, s) for s, d in around])]
where the time goes in v9:
time: 96.1 us; the launch traced here: 95.1 us
  blocking collectives  43.2 us (45%)
  starting transfers between devices  28.4 us (30%)
  waiting for transfers between devices  13.6 us (14%)
  Pallas kernels  9.7 us (10%)
    all_to_all x1, blocking collectives, per_device(): lax.all_to_all(layered, ('row', 'col'), split_axis=0, concat_axis=0, tile...  28.4 us
    all_to_all x1, blocking collectives, per_device(): lax.all_to_all(turned, 'col', split_axis=0, concat_axis=0, tiled=True)  14.8 us
    all_to_all x1, starting transfers between devices, per_device(): lax.all_to_all(packed, 'row', split_axis=0, concat_axis=0, tiled=True)  10.2 us
    ppermute x2, starting transfers between devices, per_device(): above = lax.ppermute(sent, 'row', [(d, s) for s, d in around])  8.01 us
    ppermute x1, waiting for transfers between devices, per_device(): other = lax.ppermute(given, 'row', [(i, i ^ HALF) for i in range(ROWS)])  7.11 us
    ppermute x2, starting transfers between devices, per_device(): below = lax.ppermute(sent, 'row', around)  5.27 us
    ppermute x1, starting transfers between devices, per_device(): other = lax.ppermute(given, 'row', [(i, i ^ HALF) for i in range(ROWS)])  4.91 us
    all_to_all x1, waiting for transfers between devices, per_device(): lax.all_to_all(packed, 'row', split_axis=0, concat_axis=0, tiled=True)  3.8 us
  transfers between devices with their start and end apart: 6, of which 4 were waited for; matrix products, arithmetic and copies ran while one was open for 0% of the time, Pallas kernels for 4%

profile of v9, /device:TPU:1, one launch (start us, length us, event | category | flops | bytes accessed | tf_op | source)
XLA Modules:
  0.0 95.1 jit_solution(15430808440000086490)
XLA Ops:
  0.0 0.0 copy-start
  0.0 0.0 copy-start.5
  0.0 0.0 copy-start.4
  0.0 0.0 copy-start.3
  0.0 2.0 %shard_map.91 = bf16[16,37,4,128]{3,2,1,0:T(4,128)(2,1)} custom-call(bf16[2,96,4,128]{3,2,1,0:T(4,128)(2,1)} %orbitals.1, bf16[2,4]{1,0:T(2,128)(2,1)} %bitcast.4), custom_call_target="tpu_custom_call" | custom-call | tf_op jit(solution)/shard_map/pallas_call | solution.py:365
  2.0 10.2 %all-to-all-start = ((bf16[16,37,4,128]{3,2,1,0:T(4,128)(2,1)}), bf16[16,37,4,128]{3,2,1,0:T(4,128)(2,1)S(1)}, u32[]{:S(2)}, u32[]{:S(2)}) async-start(bf16[16,37,4,128]{3,2,1,0:T(4,128)(2,1)} %shard_map.91), calls=%async_computation | async-start | bytes 1212416 | tf_op jit(solution)/shard_map/all_to_all | solution.py:376
  12.2 0.0 copy-done
  12.2 0.0 copy-done.5
  12.2 0.0 copy-done.4
  12.2 0.0 copy-done.3
  12.3 0.6 shard_map.92
  12.8 0.0 copy-start.1
  12.8 0.0 copy-start.2
  12.8 4.9 %collective-permute-start = (f32[408,128]{1,0:T(8,128)S(1)}, f32[408,128]{1,0:T(8,128)S(1)}, u32[]{:S(2)}, u32[]{:S(2)}) collective-permute-start(f32[408,128]{1,0:T(8,128)S(1)} %shard_map.92), channel_id=1, source_target_pairs={{0,256},{32,288},{64,320},{96,352},{128,384},{160,416},{192,448},{... | collective-permute-start | bytes 626696 | tf_op jit(solution)/shard_map/ppermute | solution.py:384
  17.8 1.1 %shard_map.93 = (f32[8,384,128]{2,1,0:T(8,128)S(1)}, f32[8,128]{1,0:T(8,128)S(1)}) custom-call(s32[8,128]{1,0:T(8,128)S(1)} %copy-done.3, f32[8,128]{1,0:T(8,128)S(1)} %copy-done.4, f32[8]{0:T(128)S(1)} %copy-done.5), custom_call_target="tpu_custom_call" | custom-call | flops 1000000000 | bytes 1600000 | tf_op jit(solution)/shard_map/pallas_call | solution.py:385
  18.9 7.1 %collective-permute-done.other = f32[408,128]{1,0:T(8,128)S(1)} collective-permute-done((f32[408,128]{1,0:T(8,128)S(1)}, f32[408,128]{1,0:T(8,128)S(1)}, u32[]{:S(2)}, u32[]{:S(2)}) %collective-permute-start) | collective-permute-done | bytes 208928 | tf_op jit(solution)/shard_map/ppermute | solution.py:384
  26.0 3.8 %all-to-all-done.received = bf16[16,37,4,128]{3,2,1,0:T(4,128)(2,1)S(1)} async-done(((bf16[16,37,4,128]{3,2,1,0:T(4,128)(2,1)}), bf16[16,37,4,128]{3,2,1,0:T(4,128)(2,1)S(1)}, u32[]{:S(2)}, u32[]{:S(2)}) %all-to-all-start) | async-done | bytes 606240 | tf_op jit(solution)/shard_map/all_to_all | solution.py:376
  29.8 0.0 copy-done.1
  29.8 0.0 copy-done.2
  29.8 1.7 %shard_map.94 = (f32[2,6,64,128]{3,2,1,0:T(8,128)S(1)}, f32[2,6,64,128]{3,2,1,0:T(8,128)S(1)}, bf16[2,6,64,128]{3,2,1,0:T(8,128)(2,1)S(1)}, f32[8,128]{1,0:T(8,128)S(1)}) custom-call(bf16[16,37,4,128]{3,2,1,0:T(4,128)(2,1)S(1)} %all-to-all-done.received, f32[6,64,128]{2,1,0:T(8,128)S(1)} %copy-done, f32[408,128]{1,0:T(8,128)S(1)} %collective-permute-done.other, ...), custom_call_target="tpu_custom_call" | custom-call | tf_op jit(solution)/shard_map/pallas_call | solution.py:393
  31.5 2.5 %collective-permute-start.2 = (bf16[2,6,64,128]{3,2,1,0:T(8,128)(2,1)S(1)}, bf16[2,6,64,128]{3,2,1,0:T(8,128)(2,1)S(1)}, u32[]{:S(2)}, u32[]{:S(2)}) collective-permute-start(bf16[2,6,64,128]{3,2,1,0:T(8,128)(2,1)S(1)} %get-tuple-element.17), channel_id=1, source_target_pairs={{0,32},{32,64},{64,96},{96,128},{128,160},{160,192},{192,224},{224... | collective-permute-start | bytes 589832 | tf_op jit(solution)/shard_map/ppermute | solution.py:401
  34.1 3.9 %collective-permute-start.1 = (bf16[2,6,64,128]{3,2,1,0:T(8,128)(2,1)S(1)}, bf16[2,6,64,128]{3,2,1,0:T(8,128)(2,1)S(1)}, u32[]{:S(2)}, u32[]{:S(2)}) collective-permute-start(bf16[2,6,64,128]{3,2,1,0:T(8,128)(2,1)S(1)} %get-tuple-element.17), channel_id=1, source_target_pairs={{32,0},{64,32},{96,64},{128,96},{160,128},{192,160},{224,192},{0,2... | collective-permute-start | bytes 589832 | tf_op jit(solution)/shard_map/ppermute | solution.py:400
  38.0 1.3 %shard_map.95.partial = f32[2,6,64,128]{3,2,1,0:T(8,128)S(1)} custom-call(f32[2,6,64,128]{3,2,1,0:T(8,128)S(1)} %get-tuple-element.15.current.previous, f32[2,6,64,128]{3,2,1,0:T(8,128)S(1)} %get-tuple-element.16.previous, f32[6,64,128]{2,1,0:T(8,128)S(1)} %copy-done, f32[408,128]{1,0:T(8,128)S(1)} %collective-permute-done.other, ...), custom_call_target="tpu_custom_call" | custom-call | flops 2000000000 | bytes 3000000 | tf_op jit(solution)/shard_map/pallas_call | solution.py:402
  39.3 0.0 collective-permute-done.2.below
  39.3 1.4 %collective-permute-done.1.above = bf16[2,6,64,128]{3,2,1,0:T(8,128)(2,1)S(1)} collective-permute-done((bf16[2,6,64,128]{3,2,1,0:T(8,128)(2,1)S(1)}, bf16[2,6,64,128]{3,2,1,0:T(8,128)(2,1)S(1)}, u32[]{:S(2)}, u32[]{:S(2)}) %collective-permute-start.1) | collective-permute-done | bytes 196640 | tf_op jit(solution)/shard_map/ppermute | solution.py:400
  40.8 0.2 shard_map.96
  41.0 2.7 %collective-permute-start.4 = (bf16[2,6,64,128]{3,2,1,0:T(8,128)(2,1)S(1)}, bf16[2,6,64,128]{3,2,1,0:T(8,128)(2,1)S(1)}, u32[]{:S(2)}, u32[]{:S(2)}) collective-permute-start(bf16[2,6,64,128]{3,2,1,0:T(8,128)(2,1)S(1)} %get-tuple-element.19), channel_id=1, source_target_pairs={{0,32},{32,64},{64,96},{96,128},{128,160},{160,192},{192,224},{224... | collective-permute-start | bytes 589832 | tf_op jit(solution)/shard_map/ppermute | solution.py:401
  43.8 4.1 %collective-permute-start.3 = (bf16[2,6,64,128]{3,2,1,0:T(8,128)(2,1)S(1)}, bf16[2,6,64,128]{3,2,1,0:T(8,128)(2,1)S(1)}, u32[]{:S(2)}, u32[]{:S(2)}) collective-permute-start(bf16[2,6,64,128]{3,2,1,0:T(8,128)(2,1)S(1)} %get-tuple-element.19), channel_id=1, source_target_pairs={{32,0},{64,32},{96,64},{128,96},{160,128},{192,160},{224,192},{0,2... | collective-permute-start | bytes 589832 | tf_op jit(solution)/shard_map/ppermute | solution.py:400
  47.8 1.3 %shard_map.97.partial = f32[2,6,64,128]{3,2,1,0:T(8,128)S(1)} custom-call(f32[2,6,64,128]{3,2,1,0:T(8,128)S(1)} %get-tuple-element.18.current, f32[2,6,64,128]{3,2,1,0:T(8,128)S(1)} %get-tuple-element.15.current.previous, f32[6,64,128]{2,1,0:T(8,128)S(1)} %copy-done, f32[408,128]{1,0:T(8,128)S(1)} %collective-permute-done.other, ...), custom_call_target="tpu_custom_call" | custom-call | flops 2000000000 | bytes 3000000 | tf_op jit(solution)/shard_map/pallas_call | solution.py:402
  49.1 0.0 copy-start.6
  49.2 0.0 collective-permute-done.4.below
  49.2 1.3 %collective-permute-done.3.above = bf16[2,6,64,128]{3,2,1,0:T(8,128)(2,1)S(1)} collective-permute-done((bf16[2,6,64,128]{3,2,1,0:T(8,128)(2,1)S(1)}, bf16[2,6,64,128]{3,2,1,0:T(8,128)(2,1)S(1)}, u32[]{:S(2)}, u32[]{:S(2)}) %collective-permute-start.3) | collective-permute-done | bytes 196640 | tf_op jit(solution)/shard_map/ppermute | solution.py:400
  50.4 0.3 shard_map.98
  50.8 28.4 %all_to_all.15.received = bf16[64,4,4,128]{3,2,1,0:T(4,128)(2,1)S(1)} all-to-all(bf16[64,4,4,128]{3,2,1,0:T(4,128)(2,1)S(1)} %shard_map.98), channel_id=1, replica_groups={{0,1,2,3,4,5,6,7,8,9,10,11,12,13,14,15,16,17,18,19,20,21,22,23,24,25,26..., dimensions={0} | all-to-all | bytes 524288 | tf_op jit(solution)/shard_map/all_to_all | solution.py:425
  79.1 0.0 copy-done.6
  79.1 0.4 shard_map.99
  79.5 14.8 %all_to_all.16.received = bf16[32,6,4,128]{3,2,1,0:T(4,128)(2,1)S(1)} all-to-all(bf16[32,6,4,128]{3,2,1,0:T(4,128)(2,1)S(1)} %shard_map.99), channel_id=1, replica_groups=mesh['row'=16,'col'=32] {'col'}, dimensions={0} | all-to-all | bytes 393216 | tf_op jit(solution)/shard_map/all_to_all | solution.py:438
  94.3 0.8 shard_map.100
Async XLA Ops:
  0.0 12.2 %copy-start = (f32[6,64,128]{2,1,0:T(8,128)S(1)}, f32[6,64,128]{2,1,0:T(8,128)}, u32[]{:S(2)}) copy-start(f32[6,64,128]{2,1,0:T(8,128)} %potential.7) | copy-start | bytes 589828
  0.0 12.2 %copy-start.5 = (f32[8]{0:T(128)S(1)}, f32[8]{0:T(128)}, u32[]{:S(2)}) copy-start(f32[8]{0:T(128)} %strength.3) | copy-start | bytes 100
  0.0 12.2 %copy-start.4 = (f32[8,128]{1,0:T(8,128)S(1)}, f32[8,128]{1,0:T(8,128)}, u32[]{:S(2)}) copy-start(f32[8,128]{1,0:T(8,128)} %projector.3) | copy-start | bytes 12292
  0.0 12.2 %copy-start.3 = (s32[8,128]{1,0:T(8,128)S(1)}, s32[8,128]{1,0:T(8,128)}, u32[]{:S(2)}) copy-start(s32[8,128]{1,0:T(8,128)} %points.3) | copy-start | bytes 12292
  2.0 27.8 %all-to-all-start = ((bf16[16,37,4,128]{3,2,1,0:T(4,128)(2,1)}), bf16[16,37,4,128]{3,2,1,0:T(4,128)(2,1)S(1)}, u32[]{:S(2)}, u32[]{:S(2)}) async-start(bf16[16,37,4,128]{3,2,1,0:T(4,128)(2,1)} %shard_map.91), calls=%async_computation | async-start | bytes 1212416 | tf_op jit(solution)/shard_map/all_to_all | solution.py:376
  12.8 17.0 %copy-start.1 = (bf16[256,256]{1,0:T(8,128)(2,1)S(1)}, bf16[256,256]{1,0:T(8,128)(2,1)}, u32[]{:S(2)}) copy-start(bf16[256,256]{1,0:T(8,128)(2,1)} %constant.4.clone.along_z) | copy-start | bytes 393220
  12.8 17.0 %copy-start.2 = (bf16[128,128]{1,0:T(8,128)(2,1)S(1)}, bf16[128,128]{1,0:T(8,128)(2,1)}, u32[]{:S(2)}) copy-start(bf16[128,128]{1,0:T(8,128)(2,1)} %constant.5.clone.along_y) | copy-start | bytes 98308
  12.8 13.1 %collective-permute-start = (f32[408,128]{1,0:T(8,128)S(1)}, f32[408,128]{1,0:T(8,128)S(1)}, u32[]{:S(2)}, u32[]{:S(2)}) collective-permute-start(f32[408,128]{1,0:T(8,128)S(1)} %shard_map.92), channel_id=1, source_target_pairs={{0,256},{32,288},{64,320},{96,352},{128,384},{160,416},{192,448},{... | collective-permute-start | bytes 626696 | tf_op jit(solution)/shard_map/ppermute | solution.py:384
  31.5 7.8 %collective-permute-start.2 = (bf16[2,6,64,128]{3,2,1,0:T(8,128)(2,1)S(1)}, bf16[2,6,64,128]{3,2,1,0:T(8,128)(2,1)S(1)}, u32[]{:S(2)}, u32[]{:S(2)}) collective-permute-start(bf16[2,6,64,128]{3,2,1,0:T(8,128)(2,1)S(1)} %get-tuple-element.17), channel_id=1, source_target_pairs={{0,32},{32,64},{64,96},{96,128},{128,160},{160,192},{192,224},{224... | collective-permute-start | bytes 589832 | tf_op jit(solution)/shard_map/ppermute | solution.py:401
  34.1 6.7 %collective-permute-start.1 = (bf16[2,6,64,128]{3,2,1,0:T(8,128)(2,1)S(1)}, bf16[2,6,64,128]{3,2,1,0:T(8,128)(2,1)S(1)}, u32[]{:S(2)}, u32[]{:S(2)}) collective-permute-start(bf16[2,6,64,128]{3,2,1,0:T(8,128)(2,1)S(1)} %get-tuple-element.17), channel_id=1, source_target_pairs={{32,0},{64,32},{96,64},{128,96},{160,128},{192,160},{224,192},{0,2... | collective-permute-start | bytes 589832 | tf_op jit(solution)/shard_map/ppermute | solution.py:400
  41.0 8.1 %collective-permute-start.4 = (bf16[2,6,64,128]{3,2,1,0:T(8,128)(2,1)S(1)}, bf16[2,6,64,128]{3,2,1,0:T(8,128)(2,1)S(1)}, u32[]{:S(2)}, u32[]{:S(2)}) collective-permute-start(bf16[2,6,64,128]{3,2,1,0:T(8,128)(2,1)S(1)} %get-tuple-element.19), channel_id=1, source_target_pairs={{0,32},{32,64},{64,96},{96,128},{128,160},{160,192},{192,224},{224... | collective-permute-start | bytes 589832 | tf_op jit(solution)/shard_map/ppermute | solution.py:401
  43.8 6.7 %collective-permute-start.3 = (bf16[2,6,64,128]{3,2,1,0:T(8,128)(2,1)S(1)}, bf16[2,6,64,128]{3,2,1,0:T(8,128)(2,1)S(1)}, u32[]{:S(2)}, u32[]{:S(2)}) collective-permute-start(bf16[2,6,64,128]{3,2,1,0:T(8,128)(2,1)S(1)} %get-tuple-element.19), channel_id=1, source_target_pairs={{32,0},{64,32},{96,64},{128,96},{160,128},{192,160},{224,192},{0,2... | collective-permute-start | bytes 589832 | tf_op jit(solution)/shard_map/ppermute | solution.py:400
  49.1 30.0 %copy-start.6 = (s32[64]{0:T(128)S(1)}, s32[64]{0:T(128)}, u32[]{:S(2)}) copy-start(s32[64]{0:T(128)} %param.15) | copy-start | bytes 772

commit v10 on v9

--- a/solution.py
+++ b/solution.py
@@ -283,20 +283,32 @@
     return joined
 
 
-def join_kernel(partial, above, below, next_out, sent_out):
-    joined = joining(partial, below, above)
-    for p in range(SLAB):
-        for slab in range(2):
-            value = joined(slab, p)
-            next_out[slab, p] = value
-            sent_out[slab, p] = value.astype(BF16)
-
-
-def last_kernel(partial, above, below, panel, out, slabs):
-    joined = joining(partial, below, above)
-    for p in range(SLAB):
-        for slab in range(2):
-            slabs[slab, p * GY : (p + 1) * GY, :] = joined(slab, p)
+def by_parity(body, first, second):
+    even = (lax.axis_index("row") & 1) == 0
+    pl.when(even)(lambda: body(second, first))
+    pl.when(jnp.logical_not(even))(lambda: body(first, second))
+
+
+def join_kernel(partial, first, second, next_out, sent_out):
+    def body(below, above):
+        joined = joining(partial, below, above)
+        for p in range(SLAB):
+            for slab in range(2):
+                value = joined(slab, p)
+                next_out[slab, p] = value
+                sent_out[slab, p] = value.astype(BF16)
+
+    by_parity(body, first, second)
+
+
+def last_kernel(partial, first, second, panel, out, slabs):
+    def body(below, above):
+        joined = joining(partial, below, above)
+        for p in range(SLAB):
+            for slab in range(2):
+                slabs[slab, p * GY : (p + 1) * GY, :] = joined(slab, p)
+
+    by_parity(body, first, second)
     upper = lax.axis_index("row") // HALF
     line = lax.broadcasted_iota(jnp.int32, (4, GZ), 0)
     tile = jnp.where(line == 0, panel[0:4], 0.0).astype(BF16)
@@ -397,8 +409,10 @@
         specs=[VMEM] * 7,
     )(regrouped, *fixed)
     for step in range(2):
-        above = lax.ppermute(sent, "row", [(d, s) for s, d in around])
-        below = lax.ppermute(sent, "row", around)
+        first = lax.ppermute(sent, "row", [(i, i ^ 1) for i in range(ROWS)])
+        second = lax.ppermute(
+            sent, "row", [pair for s, d in around if s % 2 for pair in ((s, d), (d, s))]
+        )
         partial = call(
             inside_kernel,
             slabs_f32,
@@ -410,14 +424,14 @@
         if step == 0:
             previous = current
             current, sent = call(join_kernel, (slabs_f32, slabs_bf16), specs=[VMEM] * 3)(
-                partial, above, below
+                partial, first, second
             )
     layered = call(
         last_kernel,
         shape((2 * COLS, PIECE + 1, 4, GZ), BF16),
         scratch=[pltpu.VMEM((2, SLAB_ROWS, GZ), F32)],
         specs=[VMEM] * 4,
-    )(partial, above, below, panel)
+    )(partial, first, second, panel)
     both = [
         [(i + HALF * half) * COLS + col for half in range(2) for col in range(COLS)]
         for i in range(HALF)

time: 96.1 us -> 95.9 us (level)
  waiting for transfers between devices: 13.6 us -> 16.9 us
  starting transfers between devices: 28.4 us -> 26.1 us
    ppermute x4, waiting for transfers between devices: 2.72 us -> 6.01 us  [the longest x2 4.38 us: per_device(): first = lax.ppermute(sent, 'row', [(i, i ^ 1) for i in range(ROWS)])]
    ppermute x4, starting transfers between devices: 13.3 us -> 11 us  [the longest x2 6.49 us: per_device(): lax.ppermute(sent, 'row', [pair for s, d in around if s % 2 for pair in (...]
  transfers between devices with their start and end apart: 6 -> 6, of which waited for: 4 -> 6; matrix products, arithmetic and copies ran while one was open for 0% -> 0% of each run, Pallas kernels for 4% -> 4%
where the time goes in v10:
time: 95.9 us; the launch traced here: 95.4 us
  blocking collectives  42.5 us (44%)
  starting transfers between devices  26.1 us (27%)
  waiting for transfers between devices  16.9 us (18%)
  Pallas kernels  9.7 us (10%)
    all_to_all x1, blocking collectives, per_device(): lax.all_to_all(layered, ('row', 'col'), split_axis=0, concat_axis=0, tile...  27.7 us
    all_to_all x1, blocking collectives, per_device(): lax.all_to_all(turned, 'col', split_axis=0, concat_axis=0, tiled=True)  14.8 us
    all_to_all x1, starting transfers between devices, per_device(): lax.all_to_all(packed, 'row', split_axis=0, concat_axis=0, tiled=True)  10.2 us
    ppermute x1, waiting for transfers between devices, per_device(): other = lax.ppermute(given, 'row', [(i, i ^ HALF) for i in range(ROWS)])  7.11 us
    ppermute x2, starting transfers between devices, per_device(): lax.ppermute(sent, 'row', [pair for s, d in around if s % 2 for pair in (...  6.49 us
    ppermute x1, starting transfers between devices, per_device(): other = lax.ppermute(given, 'row', [(i, i ^ HALF) for i in range(ROWS)])  4.91 us
    ppermute x2, starting transfers between devices, per_device(): first = lax.ppermute(sent, 'row', [(i, i ^ 1) for i in range(ROWS)])  4.48 us
    ppermute x2, waiting for transfers between devices, per_device(): first = lax.ppermute(sent, 'row', [(i, i ^ 1) for i in range(ROWS)])  4.38 us
  transfers between devices with their start and end apart: 6, of which 6 were waited for; matrix products, arithmetic and copies ran while one was open for 0% of the time, Pallas kernels for 4%

profile of v10, /device:TPU:1, one launch (start us, length us, event | category | flops | bytes accessed | tf_op | source)
XLA Modules:
  0.0 95.4 jit_solution(2607933398325829196)
XLA Ops:
  0.0 0.0 copy-start
  0.0 0.0 copy-start.5
  0.0 0.0 copy-start.4
  0.0 0.0 copy-start.3
  0.0 2.0 %shard_map.91 = bf16[16,37,4,128]{3,2,1,0:T(4,128)(2,1)} custom-call(bf16[2,96,4,128]{3,2,1,0:T(4,128)(2,1)} %orbitals.1, bf16[2,4]{1,0:T(2,128)(2,1)} %bitcast.4), custom_call_target="tpu_custom_call" | custom-call | tf_op jit(solution)/shard_map/pallas_call | solution.py:377
  2.0 10.2 %all-to-all-start = ((bf16[16,37,4,128]{3,2,1,0:T(4,128)(2,1)}), bf16[16,37,4,128]{3,2,1,0:T(4,128)(2,1)S(1)}, u32[]{:S(2)}, u32[]{:S(2)}) async-start(bf16[16,37,4,128]{3,2,1,0:T(4,128)(2,1)} %shard_map.91), calls=%async_computation | async-start | bytes 1212416 | tf_op jit(solution)/shard_map/all_to_all | solution.py:388
  12.2 0.0 copy-done
  12.2 0.0 copy-done.5
  12.2 0.0 copy-done.4
  12.2 0.0 copy-done.3
  12.3 0.6 shard_map.92
  12.8 0.0 copy-start.1
  12.8 0.0 copy-start.2
  12.8 4.9 %collective-permute-start = (f32[408,128]{1,0:T(8,128)S(1)}, f32[408,128]{1,0:T(8,128)S(1)}, u32[]{:S(2)}, u32[]{:S(2)}) collective-permute-start(f32[408,128]{1,0:T(8,128)S(1)} %shard_map.92), channel_id=1, source_target_pairs={{0,256},{32,288},{64,320},{96,352},{128,384},{160,416},{192,448},{... | collective-permute-start | bytes 626696 | tf_op jit(solution)/shard_map/ppermute | solution.py:396
  17.8 1.1 %shard_map.93 = (f32[8,384,128]{2,1,0:T(8,128)S(1)}, f32[8,128]{1,0:T(8,128)S(1)}) custom-call(s32[8,128]{1,0:T(8,128)S(1)} %copy-done.3, f32[8,128]{1,0:T(8,128)S(1)} %copy-done.4, f32[8]{0:T(128)S(1)} %copy-done.5), custom_call_target="tpu_custom_call" | custom-call | flops 1000000000 | bytes 1600000 | tf_op jit(solution)/shard_map/pallas_call | solution.py:397
  18.9 7.1 %collective-permute-done.other = f32[408,128]{1,0:T(8,128)S(1)} collective-permute-done((f32[408,128]{1,0:T(8,128)S(1)}, f32[408,128]{1,0:T(8,128)S(1)}, u32[]{:S(2)}, u32[]{:S(2)}) %collective-permute-start) | collective-permute-done | bytes 208928 | tf_op jit(solution)/shard_map/ppermute | solution.py:396
  26.0 3.8 %all-to-all-done.received = bf16[16,37,4,128]{3,2,1,0:T(4,128)(2,1)S(1)} async-done(((bf16[16,37,4,128]{3,2,1,0:T(4,128)(2,1)}), bf16[16,37,4,128]{3,2,1,0:T(4,128)(2,1)S(1)}, u32[]{:S(2)}, u32[]{:S(2)}) %all-to-all-start) | async-done | bytes 606240 | tf_op jit(solution)/shard_map/all_to_all | solution.py:388
  29.8 0.0 copy-done.1
  29.8 0.0 copy-done.2
  29.8 1.7 %shard_map.94 = (f32[2,6,64,128]{3,2,1,0:T(8,128)S(1)}, f32[2,6,64,128]{3,2,1,0:T(8,128)S(1)}, bf16[2,6,64,128]{3,2,1,0:T(8,128)(2,1)S(1)}, f32[8,128]{1,0:T(8,128)S(1)}) custom-call(bf16[16,37,4,128]{3,2,1,0:T(4,128)(2,1)S(1)} %all-to-all-done.received, f32[6,64,128]{2,1,0:T(8,128)S(1)} %copy-done, f32[408,128]{1,0:T(8,128)S(1)} %collective-permute-done.other, ...), custom_call_target="tpu_custom_call" | custom-call | tf_op jit(solution)/shard_map/pallas_call | solution.py:405
  31.5 2.6 %collective-permute-start.2 = (bf16[2,6,64,128]{3,2,1,0:T(8,128)(2,1)S(1)}, bf16[2,6,64,128]{3,2,1,0:T(8,128)(2,1)S(1)}, u32[]{:S(2)}, u32[]{:S(2)}) collective-permute-start(bf16[2,6,64,128]{3,2,1,0:T(8,128)(2,1)S(1)} %get-tuple-element.17), channel_id=1, source_target_pairs={{32,64},{64,32},{96,128},{128,96},{160,192},{192,160},{224,0},{0,2... | collective-permute-start | bytes 589832 | tf_op jit(solution)/shard_map/ppermute | solution.py:413
  34.1 2.6 %collective-permute-start.1 = (bf16[2,6,64,128]{3,2,1,0:T(8,128)(2,1)S(1)}, bf16[2,6,64,128]{3,2,1,0:T(8,128)(2,1)S(1)}, u32[]{:S(2)}, u32[]{:S(2)}) collective-permute-start(bf16[2,6,64,128]{3,2,1,0:T(8,128)(2,1)S(1)} %get-tuple-element.17), channel_id=1, source_target_pairs={{0,32},{32,0},{64,96},{96,64},{128,160},{160,128},{192,224},{224,1... | collective-permute-start | bytes 589832 | tf_op jit(solution)/shard_map/ppermute | solution.py:412
  36.7 1.3 %shard_map.95.partial = f32[2,6,64,128]{3,2,1,0:T(8,128)S(1)} custom-call(f32[2,6,64,128]{3,2,1,0:T(8,128)S(1)} %get-tuple-element.15.current.previous, f32[2,6,64,128]{3,2,1,0:T(8,128)S(1)} %get-tuple-element.16.previous, f32[6,64,128]{2,1,0:T(8,128)S(1)} %copy-done, f32[408,128]{1,0:T(8,128)S(1)} %collective-permute-done.other, ...), custom_call_target="tpu_custom_call" | custom-call | flops 2000000000 | bytes 3000000 | tf_op jit(solution)/shard_map/pallas_call | solution.py:416
  38.0 1.1 %collective-permute-done.2.second = bf16[2,6,64,128]{3,2,1,0:T(8,128)(2,1)S(1)} collective-permute-done((bf16[2,6,64,128]{3,2,1,0:T(8,128)(2,1)S(1)}, bf16[2,6,64,128]{3,2,1,0:T(8,128)(2,1)S(1)}, u32[]{:S(2)}, u32[]{:S(2)}) %collective-permute-start.2) | collective-permute-done | bytes 196640 | tf_op jit(solution)/shard_map/ppermute | solution.py:413
  39.1 1.7 %collective-permute-done.1.first = bf16[2,6,64,128]{3,2,1,0:T(8,128)(2,1)S(1)} collective-permute-done((bf16[2,6,64,128]{3,2,1,0:T(8,128)(2,1)S(1)}, bf16[2,6,64,128]{3,2,1,0:T(8,128)(2,1)S(1)}, u32[]{:S(2)}, u32[]{:S(2)}) %collective-permute-start.1) | collective-permute-done | bytes 196640 | tf_op jit(solution)/shard_map/ppermute | solution.py:412
  40.8 0.2 shard_map.96
  41.1 3.9 %collective-permute-start.4 = (bf16[2,6,64,128]{3,2,1,0:T(8,128)(2,1)S(1)}, bf16[2,6,64,128]{3,2,1,0:T(8,128)(2,1)S(1)}, u32[]{:S(2)}, u32[]{:S(2)}) collective-permute-start(bf16[2,6,64,128]{3,2,1,0:T(8,128)(2,1)S(1)} %get-tuple-element.19), channel_id=1, source_target_pairs={{32,64},{64,32},{96,128},{128,96},{160,192},{192,160},{224,0},{0,2... | collective-permute-start | bytes 589832 | tf_op jit(solution)/shard_map/ppermute | solution.py:413
  45.0 1.9 %collective-permute-start.3 = (bf16[2,6,64,128]{3,2,1,0:T(8,128)(2,1)S(1)}, bf16[2,6,64,128]{3,2,1,0:T(8,128)(2,1)S(1)}, u32[]{:S(2)}, u32[]{:S(2)}) collective-permute-start(bf16[2,6,64,128]{3,2,1,0:T(8,128)(2,1)S(1)} %get-tuple-element.19), channel_id=1, source_target_pairs={{0,32},{32,0},{64,96},{96,64},{128,160},{160,128},{192,224},{224,1... | collective-permute-start | bytes 589832 | tf_op jit(solution)/shard_map/ppermute | solution.py:412
  46.9 1.3 %shard_map.97.partial = f32[2,6,64,128]{3,2,1,0:T(8,128)S(1)} custom-call(f32[2,6,64,128]{3,2,1,0:T(8,128)S(1)} %get-tuple-element.18.current, f32[2,6,64,128]{3,2,1,0:T(8,128)S(1)} %get-tuple-element.15.current.previous, f32[6,64,128]{2,1,0:T(8,128)S(1)} %copy-done, f32[408,128]{1,0:T(8,128)S(1)} %collective-permute-done.other, ...), custom_call_target="tpu_custom_call" | custom-call | flops 2000000000 | bytes 3000000 | tf_op jit(solution)/shard_map/pallas_call | solution.py:416
  48.2 0.0 copy-start.6
  48.2 0.5 collective-permute-done.4.second
  48.7 2.7 %collective-permute-done.3.first = bf16[2,6,64,128]{3,2,1,0:T(8,128)(2,1)S(1)} collective-permute-done((bf16[2,6,64,128]{3,2,1,0:T(8,128)(2,1)S(1)}, bf16[2,6,64,128]{3,2,1,0:T(8,128)(2,1)S(1)}, u32[]{:S(2)}, u32[]{:S(2)}) %collective-permute-start.3) | collective-permute-done | bytes 196640 | tf_op jit(solution)/shard_map/ppermute | solution.py:412
  51.4 0.3 shard_map.98
  51.7 27.7 %all_to_all.15.received = bf16[64,4,4,128]{3,2,1,0:T(4,128)(2,1)S(1)} all-to-all(bf16[64,4,4,128]{3,2,1,0:T(4,128)(2,1)S(1)} %shard_map.98), channel_id=1, replica_groups={{0,1,2,3,4,5,6,7,8,9,10,11,12,13,14,15,16,17,18,19,20,21,22,23,24,25,26..., dimensions={0} | all-to-all | bytes 524288 | tf_op jit(solution)/shard_map/all_to_all | solution.py:439
  79.4 0.0 copy-done.6
  79.4 0.4 shard_map.99
  79.9 14.8 %all_to_all.16.received = bf16[32,6,4,128]{3,2,1,0:T(4,128)(2,1)S(1)} all-to-all(bf16[32,6,4,128]{3,2,1,0:T(4,128)(2,1)S(1)} %shard_map.99), channel_id=1, replica_groups=mesh['row'=16,'col'=32] {'col'}, dimensions={0} | all-to-all | bytes 393216 | tf_op jit(solution)/shard_map/all_to_all | solution.py:452
  94.7 0.8 shard_map.100
Async XLA Ops:
  0.0 12.2 %copy-start = (f32[6,64,128]{2,1,0:T(8,128)S(1)}, f32[6,64,128]{2,1,0:T(8,128)}, u32[]{:S(2)}) copy-start(f32[6,64,128]{2,1,0:T(8,128)} %potential.7) | copy-start | bytes 589828
  0.0 12.2 %copy-start.5 = (f32[8]{0:T(128)S(1)}, f32[8]{0:T(128)}, u32[]{:S(2)}) copy-start(f32[8]{0:T(128)} %strength.3) | copy-start | bytes 100
  0.0 12.2 %copy-start.4 = (f32[8,128]{1,0:T(8,128)S(1)}, f32[8,128]{1,0:T(8,128)}, u32[]{:S(2)}) copy-start(f32[8,128]{1,0:T(8,128)} %projector.3) | copy-start | bytes 12292
  0.0 12.2 %copy-start.3 = (s32[8,128]{1,0:T(8,128)S(1)}, s32[8,128]{1,0:T(8,128)}, u32[]{:S(2)}) copy-start(s32[8,128]{1,0:T(8,128)} %points.3) | copy-start | bytes 12292
  2.0 27.8 %all-to-all-start = ((bf16[16,37,4,128]{3,2,1,0:T(4,128)(2,1)}), bf16[16,37,4,128]{3,2,1,0:T(4,128)(2,1)S(1)}, u32[]{:S(2)}, u32[]{:S(2)}) async-start(bf16[16,37,4,128]{3,2,1,0:T(4,128)(2,1)} %shard_map.91), calls=%async_computation | async-start | bytes 1212416 | tf_op jit(solution)/shard_map/all_to_all | solution.py:388
  12.8 17.0 %copy-start.1 = (bf16[256,256]{1,0:T(8,128)(2,1)S(1)}, bf16[256,256]{1,0:T(8,128)(2,1)}, u32[]{:S(2)}) copy-start(bf16[256,256]{1,0:T(8,128)(2,1)} %constant.4.clone.along_z) | copy-start | bytes 393220
  12.8 17.0 %copy-start.2 = (bf16[128,128]{1,0:T(8,128)(2,1)S(1)}, bf16[128,128]{1,0:T(8,128)(2,1)}, u32[]{:S(2)}) copy-start(bf16[128,128]{1,0:T(8,128)(2,1)} %constant.5.clone.along_y) | copy-start | bytes 98308
  12.8 13.1 %collective-permute-start = (f32[408,128]{1,0:T(8,128)S(1)}, f32[408,128]{1,0:T(8,128)S(1)}, u32[]{:S(2)}, u32[]{:S(2)}) collective-permute-start(f32[408,128]{1,0:T(8,128)S(1)} %shard_map.92), channel_id=1, source_target_pairs={{0,256},{32,288},{64,320},{96,352},{128,384},{160,416},{192,448},{... | collective-permute-start | bytes 626696 | tf_op jit(solution)/shard_map/ppermute | solution.py:396
  31.5 7.6 %collective-permute-start.2 = (bf16[2,6,64,128]{3,2,1,0:T(8,128)(2,1)S(1)}, bf16[2,6,64,128]{3,2,1,0:T(8,128)(2,1)S(1)}, u32[]{:S(2)}, u32[]{:S(2)}) collective-permute-start(bf16[2,6,64,128]{3,2,1,0:T(8,128)(2,1)S(1)} %get-tuple-element.17), channel_id=1, source_target_pairs={{32,64},{64,32},{96,128},{128,96},{160,192},{192,160},{224,0},{0,2... | collective-permute-start | bytes 589832 | tf_op jit(solution)/shard_map/ppermute | solution.py:413
  34.1 6.7 %collective-permute-start.1 = (bf16[2,6,64,128]{3,2,1,0:T(8,128)(2,1)S(1)}, bf16[2,6,64,128]{3,2,1,0:T(8,128)(2,1)S(1)}, u32[]{:S(2)}, u32[]{:S(2)}) collective-permute-start(bf16[2,6,64,128]{3,2,1,0:T(8,128)(2,1)S(1)} %get-tuple-element.17), channel_id=1, source_target_pairs={{0,32},{32,0},{64,96},{96,64},{128,160},{160,128},{192,224},{224,1... | collective-permute-start | bytes 589832 | tf_op jit(solution)/shard_map/ppermute | solution.py:412
  41.1 7.6 %collective-permute-start.4 = (bf16[2,6,64,128]{3,2,1,0:T(8,128)(2,1)S(1)}, bf16[2,6,64,128]{3,2,1,0:T(8,128)(2,1)S(1)}, u32[]{:S(2)}, u32[]{:S(2)}) collective-permute-start(bf16[2,6,64,128]{3,2,1,0:T(8,128)(2,1)S(1)} %get-tuple-element.19), channel_id=1, source_target_pairs={{32,64},{64,32},{96,128},{128,96},{160,192},{192,160},{224,0},{0,2... | collective-permute-start | bytes 589832 | tf_op jit(solution)/shard_map/ppermute | solution.py:413
  45.0 6.4 %collective-permute-start.3 = (bf16[2,6,64,128]{3,2,1,0:T(8,128)(2,1)S(1)}, bf16[2,6,64,128]{3,2,1,0:T(8,128)(2,1)S(1)}, u32[]{:S(2)}, u32[]{:S(2)}) collective-permute-start(bf16[2,6,64,128]{3,2,1,0:T(8,128)(2,1)S(1)} %get-tuple-element.19), channel_id=1, source_target_pairs={{0,32},{32,0},{64,96},{96,64},{128,160},{160,128},{192,224},{224,1... | collective-permute-start | bytes 589832 | tf_op jit(solution)/shard_map/ppermute | solution.py:412
  48.2 31.2 %copy-start.6 = (s32[64]{0:T(128)S(1)}, s32[64]{0:T(128)}, u32[]{:S(2)}) copy-start(s32[64]{0:T(128)} %param.15) | copy-start | bytes 772

commit v11 on v10

--- a/solution.py
+++ b/solution.py
@@ -310,16 +310,16 @@
 
     by_parity(body, first, second)
     upper = lax.axis_index("row") // HALF
-    line = lax.broadcasted_iota(jnp.int32, (4, GZ), 0)
-    tile = jnp.where(line == 0, panel[0:4], 0.0).astype(BF16)
+    line = lax.broadcasted_iota(jnp.int32, (2, GZ), 0)
+    tile = jnp.where(line == 0, panel[0:2], 0.0).astype(BF16)
     for half in range(2):
         slab = upper ^ half
         for col in range(COLS):
             member = half * COLS + col
-            for k in range(PIECE):
-                at = 4 * (PIECE * col + k)
-                out[member, k] = slabs[slab, at : at + 4, :].astype(BF16)
-            out[member, PIECE] = tile
+            for k in range(2 * PIECE):
+                at = 2 * (2 * PIECE * col + k)
+                out[member, k] = slabs[slab, at : at + 2, :].astype(BF16)
+            out[member, 2 * PIECE] = tile
 
 
 def rotate_kernel(received, panel_rows, out, states, wanted, rotated):
@@ -327,9 +327,12 @@
     size = 4 * members
     for member in range(members):
         at = slice(4 * member, 4 * member + 4)
-        for k in range(PIECE):
-            states[at, k * GZ : (k + 1) * GZ] = received[member, k].astype(F32)
-        tile = received[member, PIECE].astype(F32)
+        for k in range(2 * PIECE):
+            half = 4 * member + 2 * (k % 2)
+            states[half : half + 2, k // 2 * GZ : (k // 2 + 1) * GZ] = received[member, k].astype(
+                F32
+            )
+        tile = received[member, 2 * PIECE].astype(F32)
         wanted[at, :] = jnp.broadcast_to(tile[0:1], (4, GZ))
     order = lax.broadcasted_iota(jnp.int32, (size, 64), 0) >> 2
     state_of = 2 * (order & (COLS - 1)) + lax.shift_right_logical(order, 5)
@@ -428,7 +431,7 @@
             )
     layered = call(
         last_kernel,
-        shape((2 * COLS, PIECE + 1, 4, GZ), BF16),
+        shape((2 * COLS, 2 * PIECE + 1, 2, GZ), BF16),
         scratch=[pltpu.VMEM((2, SLAB_ROWS, GZ), F32)],
         specs=[VMEM] * 4,
     )(partial, first, second, panel)

time: 95.9 us -> 95.4 us (level)
  transfers between devices with their start and end apart: 6 -> 6, of which waited for: 6 -> 6; matrix products, arithmetic and copies ran while one was open for 0% -> 0% of each run, Pallas kernels for 4% -> 5%
where the time goes in v11:
time: 95.4 us; the launch traced here: 95 us
  blocking collectives  41.8 us (44%)
  starting transfers between devices  26.1 us (27%)
  waiting for transfers between devices  16.9 us (18%)
  Pallas kernels  9.9 us (10%)
    all_to_all x1, blocking collectives, per_device(): lax.all_to_all(layered, ('row', 'col'), split_axis=0, concat_axis=0, tile...  26.8 us
    all_to_all x1, blocking collectives, per_device(): lax.all_to_all(turned, 'col', split_axis=0, concat_axis=0, tiled=True)  15 us
    all_to_all x1, starting transfers between devices, per_device(): lax.all_to_all(packed, 'row', split_axis=0, concat_axis=0, tiled=True)  10.2 us
    ppermute x1, waiting for transfers between devices, per_device(): other = lax.ppermute(given, 'row', [(i, i ^ HALF) for i in range(ROWS)])  7.11 us
    ppermute x2, starting transfers between devices, per_device(): lax.ppermute(sent, 'row', [pair for s, d in around if s % 2 for pair in (...  6.49 us
    ppermute x1, starting transfers between devices, per_device(): other = lax.ppermute(given, 'row', [(i, i ^ HALF) for i in range(ROWS)])  4.91 us
    ppermute x2, starting transfers between devices, per_device(): first = lax.ppermute(sent, 'row', [(i, i ^ 1) for i in range(ROWS)])  4.48 us
    ppermute x2, waiting for transfers between devices, per_device(): first = lax.ppermute(sent, 'row', [(i, i ^ 1) for i in range(ROWS)])  4.38 us
  transfers between devices with their start and end apart: 6, of which 6 were waited for; matrix products, arithmetic and copies ran while one was open for 0% of the time, Pallas kernels for 5%

profile of v11, /device:TPU:1, one launch (start us, length us, event | category | flops | bytes accessed | tf_op | source)
XLA Modules:
  0.0 95.0 jit_solution(16356550500109165507)
XLA Ops:
  0.0 0.0 copy-start
  0.0 0.0 copy-start.5
  0.0 0.0 copy-start.4
  0.0 0.0 copy-start.3
  0.0 2.0 %shard_map.91 = bf16[16,37,4,128]{3,2,1,0:T(4,128)(2,1)} custom-call(bf16[2,96,4,128]{3,2,1,0:T(4,128)(2,1)} %orbitals.1, bf16[2,4]{1,0:T(2,128)(2,1)} %bitcast.4), custom_call_target="tpu_custom_call" | custom-call | tf_op jit(solution)/shard_map/pallas_call | solution.py:380
  2.0 10.2 %all-to-all-start = ((bf16[16,37,4,128]{3,2,1,0:T(4,128)(2,1)}), bf16[16,37,4,128]{3,2,1,0:T(4,128)(2,1)S(1)}, u32[]{:S(2)}, u32[]{:S(2)}) async-start(bf16[16,37,4,128]{3,2,1,0:T(4,128)(2,1)} %shard_map.91), calls=%async_computation | async-start | bytes 1212416 | tf_op jit(solution)/shard_map/all_to_all | solution.py:391
  12.2 0.0 copy-done
  12.2 0.0 copy-done.5
  12.2 0.0 copy-done.4
  12.2 0.0 copy-done.3
  12.3 0.6 shard_map.92
  12.8 0.0 copy-start.1
  12.8 0.0 copy-start.2
  12.8 4.9 %collective-permute-start = (f32[408,128]{1,0:T(8,128)S(1)}, f32[408,128]{1,0:T(8,128)S(1)}, u32[]{:S(2)}, u32[]{:S(2)}) collective-permute-start(f32[408,128]{1,0:T(8,128)S(1)} %shard_map.92), channel_id=1, source_target_pairs={{0,256},{32,288},{64,320},{96,352},{128,384},{160,416},{192,448},{... | collective-permute-start | bytes 626696 | tf_op jit(solution)/shard_map/ppermute | solution.py:399
  17.8 1.1 %shard_map.93 = (f32[8,384,128]{2,1,0:T(8,128)S(1)}, f32[8,128]{1,0:T(8,128)S(1)}) custom-call(s32[8,128]{1,0:T(8,128)S(1)} %copy-done.3, f32[8,128]{1,0:T(8,128)S(1)} %copy-done.4, f32[8]{0:T(128)S(1)} %copy-done.5), custom_call_target="tpu_custom_call" | custom-call | flops 1000000000 | bytes 1600000 | tf_op jit(solution)/shard_map/pallas_call | solution.py:400
  18.9 7.1 %collective-permute-done.other = f32[408,128]{1,0:T(8,128)S(1)} collective-permute-done((f32[408,128]{1,0:T(8,128)S(1)}, f32[408,128]{1,0:T(8,128)S(1)}, u32[]{:S(2)}, u32[]{:S(2)}) %collective-permute-start) | collective-permute-done | bytes 208928 | tf_op jit(solution)/shard_map/ppermute | solution.py:399
  26.0 3.8 %all-to-all-done.received = bf16[16,37,4,128]{3,2,1,0:T(4,128)(2,1)S(1)} async-done(((bf16[16,37,4,128]{3,2,1,0:T(4,128)(2,1)}), bf16[16,37,4,128]{3,2,1,0:T(4,128)(2,1)S(1)}, u32[]{:S(2)}, u32[]{:S(2)}) %all-to-all-start) | async-done | bytes 606240 | tf_op jit(solution)/shard_map/all_to_all | solution.py:391
  29.8 0.0 copy-done.1
  29.8 0.0 copy-done.2
  29.8 1.7 %shard_map.94 = (f32[2,6,64,128]{3,2,1,0:T(8,128)S(1)}, f32[2,6,64,128]{3,2,1,0:T(8,128)S(1)}, bf16[2,6,64,128]{3,2,1,0:T(8,128)(2,1)S(1)}, f32[8,128]{1,0:T(8,128)S(1)}) custom-call(bf16[16,37,4,128]{3,2,1,0:T(4,128)(2,1)S(1)} %all-to-all-done.received, f32[6,64,128]{2,1,0:T(8,128)S(1)} %copy-done, f32[408,128]{1,0:T(8,128)S(1)} %collective-permute-done.other, ...), custom_call_target="tpu_custom_call" | custom-call | tf_op jit(solution)/shard_map/pallas_call | solution.py:408
  31.5 2.6 %collective-permute-start.2 = (bf16[2,6,64,128]{3,2,1,0:T(8,128)(2,1)S(1)}, bf16[2,6,64,128]{3,2,1,0:T(8,128)(2,1)S(1)}, u32[]{:S(2)}, u32[]{:S(2)}) collective-permute-start(bf16[2,6,64,128]{3,2,1,0:T(8,128)(2,1)S(1)} %get-tuple-element.17), channel_id=1, source_target_pairs={{32,64},{64,32},{96,128},{128,96},{160,192},{192,160},{224,0},{0,2... | collective-permute-start | bytes 589832 | tf_op jit(solution)/shard_map/ppermute | solution.py:416
  34.1 2.6 %collective-permute-start.1 = (bf16[2,6,64,128]{3,2,1,0:T(8,128)(2,1)S(1)}, bf16[2,6,64,128]{3,2,1,0:T(8,128)(2,1)S(1)}, u32[]{:S(2)}, u32[]{:S(2)}) collective-permute-start(bf16[2,6,64,128]{3,2,1,0:T(8,128)(2,1)S(1)} %get-tuple-element.17), channel_id=1, source_target_pairs={{0,32},{32,0},{64,96},{96,64},{128,160},{160,128},{192,224},{224,1... | collective-permute-start | bytes 589832 | tf_op jit(solution)/shard_map/ppermute | solution.py:415
  36.7 1.3 %shard_map.95.partial = f32[2,6,64,128]{3,2,1,0:T(8,128)S(1)} custom-call(f32[2,6,64,128]{3,2,1,0:T(8,128)S(1)} %get-tuple-element.15.current.previous, f32[2,6,64,128]{3,2,1,0:T(8,128)S(1)} %get-tuple-element.16.previous, f32[6,64,128]{2,1,0:T(8,128)S(1)} %copy-done, f32[408,128]{1,0:T(8,128)S(1)} %collective-permute-done.other, ...), custom_call_target="tpu_custom_call" | custom-call | flops 2000000000 | bytes 3000000 | tf_op jit(solution)/shard_map/pallas_call | solution.py:419
  38.0 1.1 %collective-permute-done.2.second = bf16[2,6,64,128]{3,2,1,0:T(8,128)(2,1)S(1)} collective-permute-done((bf16[2,6,64,128]{3,2,1,0:T(8,128)(2,1)S(1)}, bf16[2,6,64,128]{3,2,1,0:T(8,128)(2,1)S(1)}, u32[]{:S(2)}, u32[]{:S(2)}) %collective-permute-start.2) | collective-permute-done | bytes 196640 | tf_op jit(solution)/shard_map/ppermute | solution.py:416
  39.1 1.7 %collective-permute-done.1.first = bf16[2,6,64,128]{3,2,1,0:T(8,128)(2,1)S(1)} collective-permute-done((bf16[2,6,64,128]{3,2,1,0:T(8,128)(2,1)S(1)}, bf16[2,6,64,128]{3,2,1,0:T(8,128)(2,1)S(1)}, u32[]{:S(2)}, u32[]{:S(2)}) %collective-permute-start.1) | collective-permute-done | bytes 196640 | tf_op jit(solution)/shard_map/ppermute | solution.py:415
  40.8 0.2 shard_map.96
  41.1 3.9 %collective-permute-start.4 = (bf16[2,6,64,128]{3,2,1,0:T(8,128)(2,1)S(1)}, bf16[2,6,64,128]{3,2,1,0:T(8,128)(2,1)S(1)}, u32[]{:S(2)}, u32[]{:S(2)}) collective-permute-start(bf16[2,6,64,128]{3,2,1,0:T(8,128)(2,1)S(1)} %get-tuple-element.19), channel_id=1, source_target_pairs={{32,64},{64,32},{96,128},{128,96},{160,192},{192,160},{224,0},{0,2... | collective-permute-start | bytes 589832 | tf_op jit(solution)/shard_map/ppermute | solution.py:416
  45.0 1.9 %collective-permute-start.3 = (bf16[2,6,64,128]{3,2,1,0:T(8,128)(2,1)S(1)}, bf16[2,6,64,128]{3,2,1,0:T(8,128)(2,1)S(1)}, u32[]{:S(2)}, u32[]{:S(2)}) collective-permute-start(bf16[2,6,64,128]{3,2,1,0:T(8,128)(2,1)S(1)} %get-tuple-element.19), channel_id=1, source_target_pairs={{0,32},{32,0},{64,96},{96,64},{128,160},{160,128},{192,224},{224,1... | collective-permute-start | bytes 589832 | tf_op jit(solution)/shard_map/ppermute | solution.py:415
  46.9 0.0 copy-start.6
  46.9 1.3 %shard_map.97.partial = f32[2,6,64,128]{3,2,1,0:T(8,128)S(1)} custom-call(f32[2,6,64,128]{3,2,1,0:T(8,128)S(1)} %get-tuple-element.18.current, f32[2,6,64,128]{3,2,1,0:T(8,128)S(1)} %get-tuple-element.15.current.previous, f32[6,64,128]{2,1,0:T(8,128)S(1)} %copy-done, f32[408,128]{1,0:T(8,128)S(1)} %collective-permute-done.other, ...), custom_call_target="tpu_custom_call" | custom-call | flops 2000000000 | bytes 3000000 | tf_op jit(solution)/shard_map/pallas_call | solution.py:419
  48.2 0.5 collective-permute-done.4.second
  48.7 2.7 %collective-permute-done.3.first = bf16[2,6,64,128]{3,2,1,0:T(8,128)(2,1)S(1)} collective-permute-done((bf16[2,6,64,128]{3,2,1,0:T(8,128)(2,1)S(1)}, bf16[2,6,64,128]{3,2,1,0:T(8,128)(2,1)S(1)}, u32[]{:S(2)}, u32[]{:S(2)}) %collective-permute-start.3) | collective-permute-done | bytes 196640 | tf_op jit(solution)/shard_map/ppermute | solution.py:415
  51.4 0.4 shard_map.98
  51.8 26.8 %all_to_all.15.received = bf16[64,7,2,128]{3,2,1,0:T(2,128)(2,1)S(1)} all-to-all(bf16[64,7,2,128]{3,2,1,0:T(2,128)(2,1)S(1)} %shard_map.98), channel_id=1, replica_groups={{0,1,2,3,4,5,6,7,8,9,10,11,12,13,14,15,16,17,18,19,20,21,22,23,24,25,26..., dimensions={0} | all-to-all | bytes 458752 | tf_op jit(solution)/shard_map/all_to_all | solution.py:442
  78.6 0.0 copy-done.6
  78.6 0.5 shard_map.99
  79.2 15.0 %all_to_all.16.received = bf16[32,6,4,128]{3,2,1,0:T(4,128)(2,1)S(1)} all-to-all(bf16[32,6,4,128]{3,2,1,0:T(4,128)(2,1)S(1)} %shard_map.99), channel_id=1, replica_groups=mesh['row'=16,'col'=32] {'col'}, dimensions={0} | all-to-all | bytes 393216 | tf_op jit(solution)/shard_map/all_to_all | solution.py:455
  94.2 0.8 shard_map.100
Async XLA Ops:
  0.0 12.2 %copy-start = (f32[6,64,128]{2,1,0:T(8,128)S(1)}, f32[6,64,128]{2,1,0:T(8,128)}, u32[]{:S(2)}) copy-start(f32[6,64,128]{2,1,0:T(8,128)} %potential.7) | copy-start | bytes 589828
  0.0 12.2 %copy-start.5 = (f32[8]{0:T(128)S(1)}, f32[8]{0:T(128)}, u32[]{:S(2)}) copy-start(f32[8]{0:T(128)} %strength.3) | copy-start | bytes 100
  0.0 12.2 %copy-start.4 = (f32[8,128]{1,0:T(8,128)S(1)}, f32[8,128]{1,0:T(8,128)}, u32[]{:S(2)}) copy-start(f32[8,128]{1,0:T(8,128)} %projector.3) | copy-start | bytes 12292
  0.0 12.2 %copy-start.3 = (s32[8,128]{1,0:T(8,128)S(1)}, s32[8,128]{1,0:T(8,128)}, u32[]{:S(2)}) copy-start(s32[8,128]{1,0:T(8,128)} %points.3) | copy-start | bytes 12292
  2.0 27.8 %all-to-all-start = ((bf16[16,37,4,128]{3,2,1,0:T(4,128)(2,1)}), bf16[16,37,4,128]{3,2,1,0:T(4,128)(2,1)S(1)}, u32[]{:S(2)}, u32[]{:S(2)}) async-start(bf16[16,37,4,128]{3,2,1,0:T(4,128)(2,1)} %shard_map.91), calls=%async_computation | async-start | bytes 1212416 | tf_op jit(solution)/shard_map/all_to_all | solution.py:391
  12.8 17.0 %copy-start.1 = (bf16[256,256]{1,0:T(8,128)(2,1)S(1)}, bf16[256,256]{1,0:T(8,128)(2,1)}, u32[]{:S(2)}) copy-start(bf16[256,256]{1,0:T(8,128)(2,1)} %constant.4.clone.along_z) | copy-start | bytes 393220
  12.8 17.0 %copy-start.2 = (bf16[128,128]{1,0:T(8,128)(2,1)S(1)}, bf16[128,128]{1,0:T(8,128)(2,1)}, u32[]{:S(2)}) copy-start(bf16[128,128]{1,0:T(8,128)(2,1)} %constant.5.clone.along_y) | copy-start | bytes 98308
  12.8 13.1 %collective-permute-start = (f32[408,128]{1,0:T(8,128)S(1)}, f32[408,128]{1,0:T(8,128)S(1)}, u32[]{:S(2)}, u32[]{:S(2)}) collective-permute-start(f32[408,128]{1,0:T(8,128)S(1)} %shard_map.92), channel_id=1, source_target_pairs={{0,256},{32,288},{64,320},{96,352},{128,384},{160,416},{192,448},{... | collective-permute-start | bytes 626696 | tf_op jit(solution)/shard_map/ppermute | solution.py:399
  31.5 7.6 %collective-permute-start.2 = (bf16[2,6,64,128]{3,2,1,0:T(8,128)(2,1)S(1)}, bf16[2,6,64,128]{3,2,1,0:T(8,128)(2,1)S(1)}, u32[]{:S(2)}, u32[]{:S(2)}) collective-permute-start(bf16[2,6,64,128]{3,2,1,0:T(8,128)(2,1)S(1)} %get-tuple-element.17), channel_id=1, source_target_pairs={{32,64},{64,32},{96,128},{128,96},{160,192},{192,160},{224,0},{0,2... | collective-permute-start | bytes 589832 | tf_op jit(solution)/shard_map/ppermute | solution.py:416
  34.1 6.7 %collective-permute-start.1 = (bf16[2,6,64,128]{3,2,1,0:T(8,128)(2,1)S(1)}, bf16[2,6,64,128]{3,2,1,0:T(8,128)(2,1)S(1)}, u32[]{:S(2)}, u32[]{:S(2)}) collective-permute-start(bf16[2,6,64,128]{3,2,1,0:T(8,128)(2,1)S(1)} %get-tuple-element.17), channel_id=1, source_target_pairs={{0,32},{32,0},{64,96},{96,64},{128,160},{160,128},{192,224},{224,1... | collective-permute-start | bytes 589832 | tf_op jit(solution)/shard_map/ppermute | solution.py:415
  41.1 7.6 %collective-permute-start.4 = (bf16[2,6,64,128]{3,2,1,0:T(8,128)(2,1)S(1)}, bf16[2,6,64,128]{3,2,1,0:T(8,128)(2,1)S(1)}, u32[]{:S(2)}, u32[]{:S(2)}) collective-permute-start(bf16[2,6,64,128]{3,2,1,0:T(8,128)(2,1)S(1)} %get-tuple-element.19), channel_id=1, source_target_pairs={{32,64},{64,32},{96,128},{128,96},{160,192},{192,160},{224,0},{0,2... | collective-permute-start | bytes 589832 | tf_op jit(solution)/shard_map/ppermute | solution.py:416
  45.0 6.4 %collective-permute-start.3 = (bf16[2,6,64,128]{3,2,1,0:T(8,128)(2,1)S(1)}, bf16[2,6,64,128]{3,2,1,0:T(8,128)(2,1)S(1)}, u32[]{:S(2)}, u32[]{:S(2)}) collective-permute-start(bf16[2,6,64,128]{3,2,1,0:T(8,128)(2,1)S(1)} %get-tuple-element.19), channel_id=1, source_target_pairs={{0,32},{32,0},{64,96},{96,64},{128,160},{160,128},{192,224},{224,1... | collective-permute-start | bytes 589832 | tf_op jit(solution)/shard_map/ppermute | solution.py:415
  46.9 31.7 %copy-start.6 = (s32[64]{0:T(128)S(1)}, s32[64]{0:T(128)}, u32[]{:S(2)}) copy-start(s32[64]{0:T(128)} %param.15) | copy-start | bytes 772

commit v12 on v11

--- a/solution.py
+++ b/solution.py
@@ -32,6 +32,7 @@
 SLAB_ROWS = SLAB * GY
 SENT = 2 * WIDE + 1
 HALF = ROWS // 2
+EARLY = 4
 PIECE = SLAB_ROWS // COLS // 4
 OTHER_ROWS = SLAB_ROWS + 3 * ATOM_DEV
 
@@ -119,11 +120,11 @@
         out[at : at + 1, :] = jnp.full((1, GZ), strength[atom], F32)
 
 
-def densify(points, projector, dense):
+def densify(points, projector, dense, atoms=range(ATOM_DEV)):
     grid_row, lane = lax.shift_right_logical(points, 7), points & (GZ - 1)
     high = projector.astype(BF16).astype(F32)
     parts = (high, projector - high)
-    for atom in range(ATOM_DEV):
+    for atom in atoms:
         rows = jnp.where(
             lax.broadcasted_iota(jnp.int32, (SLAB_ROWS, GZ), 0) == grid_row[atom : atom + 1, :],
             1.0,
@@ -133,7 +134,7 @@
         lanes = [
             jnp.where(at_lane, part[atom : atom + 1, :], 0.0).astype(BF16) for part in parts
         ]
-        dense[atom] = lax.dot_general(
+        dense[atom - atoms[0]] = lax.dot_general(
             jnp.concatenate([rows] * 2, axis=1),
             jnp.concatenate(lanes, axis=1),
             (((1,), (1,)), ((), ())),
@@ -147,38 +148,56 @@
         gains[atom : atom + 1, :] = jnp.full((1, GZ), strength[atom], F32)
 
 
-def other_projectors(given, dense):
+def project_other_kernel(given, dense):
     points = given[SLAB_ROWS : SLAB_ROWS + 8, :].astype(jnp.int32)
-    densify(points, given[SLAB_ROWS + 8 : SLAB_ROWS + 16, :], dense)
-    return given.at[SLAB_ROWS + 16 : SLAB_ROWS + 24]
-
-
-def apply(planes, reach, scale, potentials, denses, gains, along_z, along_y, wide_z, summed_z, emit):
+    densify(points, given[SLAB_ROWS + 8 : SLAB_ROWS + 16, :], dense, range(EARLY))
+
+
+def projectors_of(dense, gains, given, early, late):
+    points = given[SLAB_ROWS : SLAB_ROWS + 8, :].astype(jnp.int32)
+    densify(points, given[SLAB_ROWS + 8 : SLAB_ROWS + 16, :], late, range(EARLY, ATOM_DEV))
+
+    def own(atom, rows):
+        return dense[atom, rows, :]
+
+    def other(atom, rows):
+        return early[atom, rows, :] if atom < EARLY else late[atom - EARLY, rows, :]
+
+    return (own, other), (gains, given.at[SLAB_ROWS + 16 : SLAB_ROWS + 24])
+
+
+def apply(
+    planes, reach, scale, exact, potentials, denses, gains, along_z, along_y, wide_z, summed_z, emit
+):
+    deep = GZ if exact else 2 * GZ
     weights = []
     for slab in range(2):
         partial = [None] * ATOM_DEV
         for p in range(SLAB):
             value = planes(slab, p)
             high = value.astype(BF16)
-            low = (value - high.astype(F32)).astype(BF16)
             start = (slab * SLAB + p) * GY
             wide_z[start : start + GY, 0:GZ] = high
-            wide_z[start : start + GY, GZ : 2 * GZ] = low
+            if not exact:
+                low = (value - high.astype(F32)).astype(BF16)
+                wide_z[start : start + GY, GZ : 2 * GZ] = low
             for atom in range(ATOM_DEV):
-                weight = denses[slab][atom, p * GY : (p + 1) * GY, :]
+                weight = denses[slab](atom, slice(p * GY, (p + 1) * GY))
                 term = jnp.sum((weight * value).reshape(GY // 8, 8, GZ), axis=0)
                 partial[atom] = term if p == 0 else partial[atom] + term
         lines = [jnp.sum(term, axis=0, keepdims=True) for term in partial]
         total = jnp.sum(jnp.concatenate(lines, axis=0), axis=1, keepdims=True)
         weights.append(total * gains[slab][...])
-    summed_z[...] = jnp.dot(wide_z[...], along_z[...], preferred_element_type=F32)
+    summed_z[...] = jnp.dot(
+        wide_z[:, 0:deep], along_z[0:deep, :], preferred_element_type=F32
+    )
     for p in range(SLAB):
         both = jnp.concatenate(
             [
                 jnp.concatenate(
                     [
-                        wide_z[start : start + GY, 0:GZ],
-                        wide_z[start : start + GY, GZ : 2 * GZ],
+                        wide_z[start : start + GY, at : at + GZ]
+                        for at in range(0, deep, GZ)
                     ],
                     axis=0,
                 )
@@ -186,7 +205,7 @@
             ],
             axis=1,
         )
-        turned = jnp.dot(along_y[...], both, preferred_element_type=F32)
+        turned = jnp.dot(along_y[:, 0 : deep // 2], both, preferred_element_type=F32)
         turned = turned[:GY] + turned[GY:]
         for slab in range(2):
             start = (slab * SLAB + p) * GY
@@ -199,7 +218,7 @@
                 total = (
                     total
                     + weights[slab][atom : atom + 1, :]
-                    * denses[slab][atom, p * GY : (p + 1) * GY, :]
+                    * denses[slab](atom, slice(p * GY, (p + 1) * GY))
                 )
             for offset in range(1, 7):
                 terms = [
@@ -217,10 +236,10 @@
 
 
 def first_kernel(
-    received, potential, other, dense, gains, along_z, along_y,
-    start_out, next_out, sent_out, panel_out, slabs, other_dense, wide_z, summed_z,
+    received, potential, other, dense, gains, early, along_z, along_y,
+    start_out, next_out, sent_out, panel_out, slabs, late, wide_z, summed_z,
 ):
-    other_gains = other_projectors(other, other_dense)
+    denses, all_gains = projectors_of(dense, gains, other, early, late)
     panel = jnp.zeros((YPART, GZ), F32)
     for source in range(ROWS):
         for slab in range(2):
@@ -238,24 +257,24 @@
         sent_out[slab, p] = value.astype(BF16)
 
     apply(
-        lambda slab, p: slabs[slab, SLAB + p], SLAB, 1.0 / HALF_WIDTH,
-        potentials_of(potential, other), (dense, other_dense), (gains, other_gains),
+        lambda slab, p: slabs[slab, SLAB + p], SLAB, 1.0 / HALF_WIDTH, True,
+        potentials_of(potential, other), denses, all_gains,
         along_z, along_y, wide_z, summed_z, emit,
     )
 
 
 def inside_kernel(
-    current, previous, potential, other, dense, gains, along_z, along_y,
-    out, other_dense, wide_z, summed_z,
+    current, previous, potential, other, dense, gains, early, along_z, along_y,
+    out, late, wide_z, summed_z,
 ):
-    other_gains = other_projectors(other, other_dense)
+    denses, all_gains = projectors_of(dense, gains, other, early, late)
 
     def emit(slab, p, value):
         out[slab, p] = value - previous[slab, p]
 
     apply(
-        lambda slab, p: current[slab, p], 0, 2.0 / HALF_WIDTH,
-        potentials_of(potential, other), (dense, other_dense), (gains, other_gains),
+        lambda slab, p: current[slab, p], 0, 2.0 / HALF_WIDTH, False,
+        potentials_of(potential, other), denses, all_gains,
         along_z, along_y, wide_z, summed_z, emit,
     )
 
@@ -371,7 +390,7 @@
     along_z, along_y = stencil_matrices()
     smem = pl.BlockSpec(memory_space=pltpu.SMEM)
     work = [
-        pltpu.VMEM((ATOM_DEV, SLAB_ROWS, GZ), F32),
+        pltpu.VMEM((ATOM_DEV - EARLY, SLAB_ROWS, GZ), F32),
         pltpu.VMEM((2 * SLAB_ROWS, 2 * GZ), BF16),
         pltpu.VMEM((2 * SLAB_ROWS, 2 * GZ), F32),
     ]
@@ -404,12 +423,19 @@
         flops=1_000_000_000,
         bytes_accessed=1_600_000,
     )(proj_points, projector, strength)
-    fixed = (potential, other, dense, gains, along_z, along_y)
+    early = call(
+        project_other_kernel,
+        shape((EARLY, SLAB_ROWS, GZ), F32),
+        specs=[VMEM],
+        flops=500_000_000,
+        bytes_accessed=800_000,
+    )(other)
+    fixed = (potential, other, dense, gains, early, along_z, along_y)
     previous, current, sent, panel = call(
         first_kernel,
         (slabs_f32, slabs_f32, slabs_bf16, shape((8, GZ), F32)),
         scratch=[pltpu.VMEM((2, WIDE, GY, GZ), F32)] + work,
-        specs=[VMEM] * 7,
+        specs=[VMEM] * 8,
     )(regrouped, *fixed)
     for step in range(2):
         first = lax.ppermute(sent, "row", [(i, i ^ 1) for i in range(ROWS)])
@@ -420,7 +446,7 @@
             inside_kernel,
             slabs_f32,
             scratch=work,
-            specs=[VMEM] * 8,
+            specs=[VMEM] * 9,
             flops=2_000_000_000,
             bytes_accessed=3_000_000,
         )(current, previous, *fixed)

time: 95.4 us -> 95.2 us (level)
    pallas_call x2 -> x3, Pallas kernels: 2.6 us -> 2.69 us  [the longest x2 2.31 us: per_device(): call(inside_kernel, slabs_f32, scratch=work, specs=[VMEM] * 9, flops=2000...]
where the time goes in v12:
time: 95.2 us; the launch traced here: 94.8 us
  blocking collectives  41.8 us (44%)
  starting transfers between devices  26.1 us (27%)
  waiting for transfers between devices  16.9 us (18%)
  Pallas kernels  9.81 us (10%)
    all_to_all x1, blocking collectives, per_device(): lax.all_to_all(layered, ('row', 'col'), split_axis=0, concat_axis=0, tile...  26.8 us
    all_to_all x1, blocking collectives, per_device(): lax.all_to_all(turned, 'col', split_axis=0, concat_axis=0, tiled=True)  15 us
    all_to_all x1, starting transfers between devices, per_device(): lax.all_to_all(packed, 'row', split_axis=0, concat_axis=0, tiled=True)  10.2 us
    ppermute x1, waiting for transfers between devices, per_device(): other = lax.ppermute(given, 'row', [(i, i ^ HALF) for i in range(ROWS)])  7.33 us
    ppermute x2, starting transfers between devices, per_device(): lax.ppermute(sent, 'row', [pair for s, d in around if s % 2 for pair in (...  6.49 us
    ppermute x1, starting transfers between devices, per_device(): other = lax.ppermute(given, 'row', [(i, i ^ HALF) for i in range(ROWS)])  4.78 us
    ppermute x2, starting transfers between devices, per_device(): first = lax.ppermute(sent, 'row', [(i, i ^ 1) for i in range(ROWS)])  4.58 us
    ppermute x2, waiting for transfers between devices, per_device(): first = lax.ppermute(sent, 'row', [(i, i ^ 1) for i in range(ROWS)])  4.38 us
  transfers between devices with their start and end apart: 6, of which 6 were waited for; matrix products, arithmetic and copies ran while one was open for 0% of the time, Pallas kernels for 5%

profile of v12, /device:TPU:1, one launch (start us, length us, event | category | flops | bytes accessed | tf_op | source)
XLA Modules:
  0.0 94.8 jit_solution(4566595028223282008)
XLA Ops:
  0.0 0.0 copy-start
  0.0 0.0 copy-start.5
  0.0 0.0 copy-start.4
  0.0 0.0 copy-start.3
  0.0 2.0 %shard_map.91 = bf16[16,37,4,128]{3,2,1,0:T(4,128)(2,1)} custom-call(bf16[2,96,4,128]{3,2,1,0:T(4,128)(2,1)} %orbitals.1, bf16[2,4]{1,0:T(2,128)(2,1)} %bitcast.4), custom_call_target="tpu_custom_call" | custom-call | tf_op jit(solution)/shard_map/pallas_call | solution.py:399
  2.0 10.2 %all-to-all-start = ((bf16[16,37,4,128]{3,2,1,0:T(4,128)(2,1)}), bf16[16,37,4,128]{3,2,1,0:T(4,128)(2,1)S(1)}, u32[]{:S(2)}, u32[]{:S(2)}) async-start(bf16[16,37,4,128]{3,2,1,0:T(4,128)(2,1)} %shard_map.91), calls=%async_computation | async-start | bytes 1212416 | tf_op jit(solution)/shard_map/all_to_all | solution.py:410
  12.2 0.0 copy-done
  12.2 0.0 copy-done.5
  12.2 0.0 copy-done.4
  12.2 0.0 copy-done.3
  12.3 0.6 shard_map.92
  12.8 4.8 %collective-permute-start = (f32[408,128]{1,0:T(8,128)S(1)}, f32[408,128]{1,0:T(8,128)S(1)}, u32[]{:S(2)}, u32[]{:S(2)}) collective-permute-start(f32[408,128]{1,0:T(8,128)S(1)} %shard_map.92), channel_id=1, source_target_pairs={{0,256},{32,288},{64,320},{96,352},{128,384},{160,416},{192,448},{... | collective-permute-start | bytes 626696 | tf_op jit(solution)/shard_map/ppermute | solution.py:418
  17.6 1.1 %shard_map.93 = (f32[8,384,128]{2,1,0:T(8,128)S(1)}, f32[8,128]{1,0:T(8,128)S(1)}) custom-call(s32[8,128]{1,0:T(8,128)S(1)} %copy-done.3, f32[8,128]{1,0:T(8,128)S(1)} %copy-done.4, f32[8]{0:T(128)S(1)} %copy-done.5), custom_call_target="tpu_custom_call" | custom-call | flops 1000000000 | bytes 1600000 | tf_op jit(solution)/shard_map/pallas_call | solution.py:419
  18.7 0.0 copy-start.1
  18.7 0.0 copy-start.2
  18.8 7.3 %collective-permute-done.given.other = f32[408,128]{1,0:T(8,128)S(1)} collective-permute-done((f32[408,128]{1,0:T(8,128)S(1)}, f32[408,128]{1,0:T(8,128)S(1)}, u32[]{:S(2)}, u32[]{:S(2)}) %collective-permute-start) | collective-permute-done | bytes 208928 | tf_op jit(solution)/shard_map/ppermute | solution.py:418
  26.1 0.4 shard_map.94.early
  26.5 3.3 %all-to-all-done.received = bf16[16,37,4,128]{3,2,1,0:T(4,128)(2,1)S(1)} async-done(((bf16[16,37,4,128]{3,2,1,0:T(4,128)(2,1)}), bf16[16,37,4,128]{3,2,1,0:T(4,128)(2,1)S(1)}, u32[]{:S(2)}, u32[]{:S(2)}) %all-to-all-start) | async-done | bytes 606240 | tf_op jit(solution)/shard_map/all_to_all | solution.py:410
  29.8 0.0 copy-done.1
  29.8 0.0 copy-done.2
  29.8 1.5 %shard_map.95 = (f32[2,6,64,128]{3,2,1,0:T(8,128)S(1)}, f32[2,6,64,128]{3,2,1,0:T(8,128)S(1)}, bf16[2,6,64,128]{3,2,1,0:T(8,128)(2,1)S(1)}, f32[8,128]{1,0:T(8,128)S(1)}) custom-call(bf16[16,37,4,128]{3,2,1,0:T(4,128)(2,1)S(1)} %all-to-all-done.received, f32[6,64,128]{2,1,0:T(8,128)S(1)} %copy-done, f32[408,128]{1,0:T(8,128)S(1)} %collective-permute-done.given.other, ...), custom_call_target="tpu_custom_call" | custom-call | tf_op jit(solution)/shard_map/pallas_call | solution.py:434
  31.3 2.6 %collective-permute-start.2 = (bf16[2,6,64,128]{3,2,1,0:T(8,128)(2,1)S(1)}, bf16[2,6,64,128]{3,2,1,0:T(8,128)(2,1)S(1)}, u32[]{:S(2)}, u32[]{:S(2)}) collective-permute-start(bf16[2,6,64,128]{3,2,1,0:T(8,128)(2,1)S(1)} %get-tuple-element.17), channel_id=1, source_target_pairs={{32,64},{64,32},{96,128},{128,96},{160,192},{192,160},{224,0},{0,2... | collective-permute-start | bytes 589832 | tf_op jit(solution)/shard_map/ppermute | solution.py:442
  33.9 2.7 %collective-permute-start.1 = (bf16[2,6,64,128]{3,2,1,0:T(8,128)(2,1)S(1)}, bf16[2,6,64,128]{3,2,1,0:T(8,128)(2,1)S(1)}, u32[]{:S(2)}, u32[]{:S(2)}) collective-permute-start(bf16[2,6,64,128]{3,2,1,0:T(8,128)(2,1)S(1)} %get-tuple-element.17), channel_id=1, source_target_pairs={{0,32},{32,0},{64,96},{96,64},{128,160},{160,128},{192,224},{224,1... | collective-permute-start | bytes 589832 | tf_op jit(solution)/shard_map/ppermute | solution.py:441
  36.6 1.2 %shard_map.96.partial = f32[2,6,64,128]{3,2,1,0:T(8,128)S(1)} custom-call(f32[2,6,64,128]{3,2,1,0:T(8,128)S(1)} %get-tuple-element.15.current.previous, f32[2,6,64,128]{3,2,1,0:T(8,128)S(1)} %get-tuple-element.16.previous, f32[6,64,128]{2,1,0:T(8,128)S(1)} %copy-done, f32[408,128]{1,0:T(8,128)S(1)} %collective-permute-done.given.other, ...), custom_call_target="tpu_custom_call" | custom-call | flops 2000000000 | bytes 3000000 | tf_op jit(solution)/shard_map/pallas_call | solution.py:445
  37.8 1.2 %collective-permute-done.2.second = bf16[2,6,64,128]{3,2,1,0:T(8,128)(2,1)S(1)} collective-permute-done((bf16[2,6,64,128]{3,2,1,0:T(8,128)(2,1)S(1)}, bf16[2,6,64,128]{3,2,1,0:T(8,128)(2,1)S(1)}, u32[]{:S(2)}, u32[]{:S(2)}) %collective-permute-start.2) | collective-permute-done | bytes 196640 | tf_op jit(solution)/shard_map/ppermute | solution.py:442
  39.0 1.7 %collective-permute-done.1.first = bf16[2,6,64,128]{3,2,1,0:T(8,128)(2,1)S(1)} collective-permute-done((bf16[2,6,64,128]{3,2,1,0:T(8,128)(2,1)S(1)}, bf16[2,6,64,128]{3,2,1,0:T(8,128)(2,1)S(1)}, u32[]{:S(2)}, u32[]{:S(2)}) %collective-permute-start.1) | collective-permute-done | bytes 196640 | tf_op jit(solution)/shard_map/ppermute | solution.py:441
  40.7 0.2 shard_map.97
  40.9 3.9 %collective-permute-start.4 = (bf16[2,6,64,128]{3,2,1,0:T(8,128)(2,1)S(1)}, bf16[2,6,64,128]{3,2,1,0:T(8,128)(2,1)S(1)}, u32[]{:S(2)}, u32[]{:S(2)}) collective-permute-start(bf16[2,6,64,128]{3,2,1,0:T(8,128)(2,1)S(1)} %get-tuple-element.19), channel_id=1, source_target_pairs={{32,64},{64,32},{96,128},{128,96},{160,192},{192,160},{224,0},{0,2... | collective-permute-start | bytes 589832 | tf_op jit(solution)/shard_map/ppermute | solution.py:442
  44.8 1.9 %collective-permute-start.3 = (bf16[2,6,64,128]{3,2,1,0:T(8,128)(2,1)S(1)}, bf16[2,6,64,128]{3,2,1,0:T(8,128)(2,1)S(1)}, u32[]{:S(2)}, u32[]{:S(2)}) collective-permute-start(bf16[2,6,64,128]{3,2,1,0:T(8,128)(2,1)S(1)} %get-tuple-element.19), channel_id=1, source_target_pairs={{0,32},{32,0},{64,96},{96,64},{128,160},{160,128},{192,224},{224,1... | collective-permute-start | bytes 589832 | tf_op jit(solution)/shard_map/ppermute | solution.py:441
  46.7 0.0 copy-start.6
  46.7 1.2 %shard_map.98.partial = f32[2,6,64,128]{3,2,1,0:T(8,128)S(1)} custom-call(f32[2,6,64,128]{3,2,1,0:T(8,128)S(1)} %get-tuple-element.18.current, f32[2,6,64,128]{3,2,1,0:T(8,128)S(1)} %get-tuple-element.15.current.previous, f32[6,64,128]{2,1,0:T(8,128)S(1)} %copy-done, f32[408,128]{1,0:T(8,128)S(1)} %collective-permute-done.given.other, ...), custom_call_target="tpu_custom_call" | custom-call | flops 2000000000 | bytes 3000000 | tf_op jit(solution)/shard_map/pallas_call | solution.py:445
  47.9 0.6 collective-permute-done.4.second
  48.5 2.7 %collective-permute-done.3.first = bf16[2,6,64,128]{3,2,1,0:T(8,128)(2,1)S(1)} collective-permute-done((bf16[2,6,64,128]{3,2,1,0:T(8,128)(2,1)S(1)}, bf16[2,6,64,128]{3,2,1,0:T(8,128)(2,1)S(1)}, u32[]{:S(2)}, u32[]{:S(2)}) %collective-permute-start.3) | collective-permute-done | bytes 196640 | tf_op jit(solution)/shard_map/ppermute | solution.py:441
  51.2 0.4 shard_map.99
  51.6 26.8 %all_to_all.15.received = bf16[64,7,2,128]{3,2,1,0:T(2,128)(2,1)S(1)} all-to-all(bf16[64,7,2,128]{3,2,1,0:T(2,128)(2,1)S(1)} %shard_map.99), channel_id=1, replica_groups={{0,1,2,3,4,5,6,7,8,9,10,11,12,13,14,15,16,17,18,19,20,21,22,23,24,25,26..., dimensions={0} | all-to-all | bytes 458752 | tf_op jit(solution)/shard_map/all_to_all | solution.py:468
  78.5 0.0 copy-done.6
  78.5 0.5 shard_map.100
  79.0 15.0 %all_to_all.16.received = bf16[32,6,4,128]{3,2,1,0:T(4,128)(2,1)S(1)} all-to-all(bf16[32,6,4,128]{3,2,1,0:T(4,128)(2,1)S(1)} %shard_map.100), channel_id=1, replica_groups=mesh['row'=16,'col'=32] {'col'}, dimensions={0} | all-to-all | bytes 393216 | tf_op jit(solution)/shard_map/all_to_all | solution.py:481
  94.0 0.8 shard_map.101
Async XLA Ops:
  0.0 12.2 %copy-start = (f32[6,64,128]{2,1,0:T(8,128)S(1)}, f32[6,64,128]{2,1,0:T(8,128)}, u32[]{:S(2)}) copy-start(f32[6,64,128]{2,1,0:T(8,128)} %potential.7) | copy-start | bytes 589828
  0.0 12.2 %copy-start.5 = (f32[8]{0:T(128)S(1)}, f32[8]{0:T(128)}, u32[]{:S(2)}) copy-start(f32[8]{0:T(128)} %strength.3) | copy-start | bytes 100
  0.0 12.2 %copy-start.4 = (f32[8,128]{1,0:T(8,128)S(1)}, f32[8,128]{1,0:T(8,128)}, u32[]{:S(2)}) copy-start(f32[8,128]{1,0:T(8,128)} %projector.3) | copy-start | bytes 12292
  0.0 12.2 %copy-start.3 = (s32[8,128]{1,0:T(8,128)S(1)}, s32[8,128]{1,0:T(8,128)}, u32[]{:S(2)}) copy-start(s32[8,128]{1,0:T(8,128)} %points.3) | copy-start | bytes 12292
  2.0 27.8 %all-to-all-start = ((bf16[16,37,4,128]{3,2,1,0:T(4,128)(2,1)}), bf16[16,37,4,128]{3,2,1,0:T(4,128)(2,1)S(1)}, u32[]{:S(2)}, u32[]{:S(2)}) async-start(bf16[16,37,4,128]{3,2,1,0:T(4,128)(2,1)} %shard_map.91), calls=%async_computation | async-start | bytes 1212416 | tf_op jit(solution)/shard_map/all_to_all | solution.py:410
  12.8 13.3 %collective-permute-start = (f32[408,128]{1,0:T(8,128)S(1)}, f32[408,128]{1,0:T(8,128)S(1)}, u32[]{:S(2)}, u32[]{:S(2)}) collective-permute-start(f32[408,128]{1,0:T(8,128)S(1)} %shard_map.92), channel_id=1, source_target_pairs={{0,256},{32,288},{64,320},{96,352},{128,384},{160,416},{192,448},{... | collective-permute-start | bytes 626696 | tf_op jit(solution)/shard_map/ppermute | solution.py:418
  18.7 11.1 %copy-start.1 = (bf16[256,256]{1,0:T(8,128)(2,1)S(1)}, bf16[256,256]{1,0:T(8,128)(2,1)}, u32[]{:S(2)}) copy-start(bf16[256,256]{1,0:T(8,128)(2,1)} %constant.4.clone.along_z) | copy-start | bytes 393220
  18.7 11.1 %copy-start.2 = (bf16[128,128]{1,0:T(8,128)(2,1)S(1)}, bf16[128,128]{1,0:T(8,128)(2,1)}, u32[]{:S(2)}) copy-start(bf16[128,128]{1,0:T(8,128)(2,1)} %constant.5.clone.along_y) | copy-start | bytes 98308
  31.3 7.6 %collective-permute-start.2 = (bf16[2,6,64,128]{3,2,1,0:T(8,128)(2,1)S(1)}, bf16[2,6,64,128]{3,2,1,0:T(8,128)(2,1)S(1)}, u32[]{:S(2)}, u32[]{:S(2)}) collective-permute-start(bf16[2,6,64,128]{3,2,1,0:T(8,128)(2,1)S(1)} %get-tuple-element.17), channel_id=1, source_target_pairs={{32,64},{64,32},{96,128},{128,96},{160,192},{192,160},{224,0},{0,2... | collective-permute-start | bytes 589832 | tf_op jit(solution)/shard_map/ppermute | solution.py:442
  33.9 6.7 %collective-permute-start.1 = (bf16[2,6,64,128]{3,2,1,0:T(8,128)(2,1)S(1)}, bf16[2,6,64,128]{3,2,1,0:T(8,128)(2,1)S(1)}, u32[]{:S(2)}, u32[]{:S(2)}) collective-permute-start(bf16[2,6,64,128]{3,2,1,0:T(8,128)(2,1)S(1)} %get-tuple-element.17), channel_id=1, source_target_pairs={{0,32},{32,0},{64,96},{96,64},{128,160},{160,128},{192,224},{224,1... | collective-permute-start | bytes 589832 | tf_op jit(solution)/shard_map/ppermute | solution.py:441
  40.9 7.6 %collective-permute-start.4 = (bf16[2,6,64,128]{3,2,1,0:T(8,128)(2,1)S(1)}, bf16[2,6,64,128]{3,2,1,0:T(8,128)(2,1)S(1)}, u32[]{:S(2)}, u32[]{:S(2)}) collective-permute-start(bf16[2,6,64,128]{3,2,1,0:T(8,128)(2,1)S(1)} %get-tuple-element.19), channel_id=1, source_target_pairs={{32,64},{64,32},{96,128},{128,96},{160,192},{192,160},{224,0},{0,2... | collective-permute-start | bytes 589832 | tf_op jit(solution)/shard_map/ppermute | solution.py:442
  44.8 6.4 %collective-permute-start.3 = (bf16[2,6,64,128]{3,2,1,0:T(8,128)(2,1)S(1)}, bf16[2,6,64,128]{3,2,1,0:T(8,128)(2,1)S(1)}, u32[]{:S(2)}, u32[]{:S(2)}) collective-permute-start(bf16[2,6,64,128]{3,2,1,0:T(8,128)(2,1)S(1)} %get-tuple-element.19), channel_id=1, source_target_pairs={{0,32},{32,0},{64,96},{96,64},{128,160},{160,128},{192,224},{224,1... | collective-permute-start | bytes 589832 | tf_op jit(solution)/shard_map/ppermute | solution.py:441
  46.7 31.7 %copy-start.6 = (s32[64]{0:T(128)S(1)}, s32[64]{0:T(128)}, u32[]{:S(2)}) copy-start(s32[64]{0:T(128)} %param.15) | copy-start | bytes 772
